TPU v7x, 32 devices: a whole 2x2x4 slice. The times are simulated.
32 devices in a mesh: tm: 4 (over z), gx: 2 (over y), gy: 4 (over x, core).
Axes of the slice: x: 2, y: 2, z: 4, core: 2. Of those that a mesh axis runs over, the one named last changes fastest.
Arguments:
- fine_nodes: float32 [4, 3, 64, 256, 128], P('tm', None, 'gx', 'gy'), may hold values from -1 to 1
- section_steps: int32 [4], replicated, may hold values from 1 to 4
- diffusivities: float32 [16], replicated, may hold values from 0.5 to 4
- tile_kinds: int32 [16, 64], P('gx', 'gy'), may hold values from 0 to 15
Outputs:
- next_nodes: float32 [4, 3, 64, 256, 128], P('tm', None, 'gx', 'gy')
All inputs are finite; a program needn't handle non-finite values.
Results may differ from a plain program's by a relative error of at most 0.0001.
Values sent between devices are 32-bit elements; how exact they have to be, the bound alone decides.
No kernel may reach another device: no remote copies, remote signals or barrier semaphores. Data moves between devices by JAX's collectives and lax.ppermute only.
A program may use at most 128 MiB of HBM per device.

v0:
```python
import jax
import jax.numpy as jnp
from jax import lax
from jax.sharding import PartitionSpec as P

JACOBI = 4
TILE = 4


step_unit = 0.05
node_weights = ((5.0 / 24.0, 1.0 / 3.0, -1.0 / 24.0), (-1.0 / 24.0, 1.0 / 3.0, 5.0 / 24.0))


def extended(array, sides, width):
    for axis, dim in sides:
        size, length = (lax.axis_size(axis), array.shape[dim])
        up = [(i, (i + 1) % size) for i in range(size - 1)]
        down = [(j, i) for i, j in up]
        last = lax.slice_in_dim(array, length - width, length, axis=dim)
        leading = lax.slice_in_dim(array, 0, width, axis=dim)
        before = lax.ppermute(last, axis, up)
        after = lax.ppermute(leading, axis, down)
        array = jnp.concatenate([before, array, after], axis=dim)
    return array


def from_behind(block, axis, distance):
    devices = range(lax.axis_size(axis))
    route = [(i - distance, i) for i in devices if i - distance in devices]
    return lax.ppermute(block, axis, route)


def shifted_sums(padded):
    center = padded[..., 1:-1, 1:-1, :]
    planar = padded[..., 2:, 1:-1, :] + padded[..., :-2, 1:-1, :]
    planar = planar + padded[..., 1:-1, 2:, :] + padded[..., 1:-1, :-2, :]
    zero_plane = jnp.zeros(center.shape[:-1] + (1,), center.dtype)
    z_above = jnp.concatenate([center[..., 1:], zero_plane], axis=-1)
    z_below = jnp.concatenate([zero_plane, center[..., :-1]], axis=-1)
    return (center, planar, z_above + z_below)


def reaction(field):
    return field - field * field * field


def forces_of(padded, diffusivity, planar_weight):
    center, planar, vertical = shifted_sums(padded)
    laplace = planar_weight * planar + vertical - (4.0 * planar_weight + 2.0) * center
    return (reaction(center), diffusivity * laplace)


def jacobi_update(padded, right_side, diffusivity, half_step, planar_weight):
    sums = shifted_sums(padded)
    coupling = half_step * diffusivity
    return (right_side + coupling * (planar_weight * sums[1] + sums[2])) / (
        1.0 + coupling * (4.0 * planar_weight + 2.0)
    )


def restrict(field):
    shape = field.shape
    blocks = field.reshape(shape[:-3] + (shape[-3] // 2, 2, shape[-2] // 2, 2, shape[-1]))
    return (
        blocks[..., :, 0, :, 0, :]
        + blocks[..., :, 0, :, 1, :]
        + blocks[..., :, 1, :, 0, :]
        + blocks[..., :, 1, :, 1, :]
    ) * 0.25


def prolong(field):
    return jnp.repeat(jnp.repeat(field, 2, axis=-3), 2, axis=-2)


def sweep(
    start_value,
    node_vals,
    reactions,
    diffusion,
    forces,
    tau_terms,
    half_step,
    step_size,
    diffusivity,
    planar_weight,
    solver,
):
    updated = [start_value]
    for node_num in range(len(node_weights)):
        weights = node_weights[node_num]
        integral = weights[0] * forces[0] + weights[1] * forces[1] + weights[2] * forces[2]
        right_side = (
            updated[node_num]
            + half_step * (reaction(updated[node_num]) - reactions[node_num])
            - half_step * diffusion[node_num + 1]
            + step_size * integral
        )
        if tau_terms is not None:
            right_side = right_side + tau_terms[node_num]
        updated.append(
            solver(right_side, node_vals[node_num + 1], diffusivity, half_step, planar_weight)
        )
    return jnp.stack(updated)


def make_solver(coarse):

    def solver(right_side, initial, diffusivity, half_step, planar_weight):
        current = initial
        for iter_num in range(JACOBI):
            if coarse:
                padded = extended(current, (("gx", 0), ("gy", 1)), 1)
            else:
                padded = extended(current, (("gx", 0), ("gy", 1)), 1)
            current = jacobi_update(padded, right_side, diffusivity, half_step, planar_weight)
        return current

    return solver


def per_device(fine_nodes, section_steps, diffusivities, tile_kinds):
    node_vals = fine_nodes[0]
    sect_num = lax.axis_index("tm")
    sections = lax.axis_size("tm")
    kinds = diffusivities.shape[0]
    picks = tile_kinds[:, :, None] == jnp.arange(kinds, dtype=jnp.int32)[None, None, :]
    tile_values = jnp.sum(jnp.where(picks, diffusivities[None, None, :], 0.0), axis=-1)
    diffusivity = jnp.repeat(jnp.repeat(tile_values, TILE, axis=0), TILE, axis=1)[:, :, None]
    coarse_diffusivity = restrict(diffusivity)
    steps_float = section_steps.astype(jnp.float32)
    own_steps = jnp.sum(jnp.where(jnp.arange(sections) == sect_num, steps_float, 0.0))
    step_size = own_steps * step_unit
    half_step = step_size * 0.5
    fine_solver = make_solver(False)
    coarse_solver = make_solver(True)
    padded = extended(node_vals, (("gx", 1), ("gy", 2)), 1)
    reactions, diffusion = forces_of(padded, diffusivity, 1.0)
    forces = reactions + diffusion
    updated = sweep(
        node_vals[0],
        node_vals,
        reactions,
        diffusion,
        forces,
        None,
        half_step,
        step_size,
        diffusivity,
        1.0,
        fine_solver,
    )
    later = extended(updated[1:], (("gx", 1), ("gy", 2)), 1)
    late_react, late_diff = forces_of(later, diffusivity, 1.0)
    fine_forces = jnp.concatenate([forces[:1], late_react + late_diff])
    coarse_nodes = restrict(updated)
    restricted = restrict(fine_forces)
    coarse_padded = extended(coarse_nodes, (("gx", 1), ("gy", 2)), 1)
    coarse_react, coarse_diff = forces_of(coarse_padded, coarse_diffusivity, 0.25)
    coarse_forces = coarse_react + coarse_diff
    defect = restricted - coarse_forces
    tau_terms = jnp.stack(
        [
            step_size * (weights[0] * defect[0] + weights[1] * defect[1] + weights[2] * defect[2])
            for weights in node_weights
        ]
    )
    start_value = coarse_nodes[0]
    chained = coarse_nodes
    for chain_num in range(sections):
        chained = sweep(
            start_value,
            coarse_nodes,
            coarse_react,
            coarse_diff,
            coarse_forces,
            tau_terms,
            half_step,
            step_size,
            coarse_diffusivity,
            0.25,
            coarse_solver,
        )
        if chain_num + 1 < sections:
            incoming = from_behind(chained[2], "tm", 1)
            start_value = jnp.where(sect_num == 0, coarse_nodes[0], incoming)
    corrected = updated + prolong(chained - coarse_nodes)
    arriving = from_behind(corrected[2], "tm", 1)
    first = jnp.where(sect_num == 0, corrected[0], arriving)
    return jnp.concatenate([first[None], corrected[1:]])[None]


def solution(mesh):
    return jax.shard_map(
        per_device,
        mesh=mesh,
        in_specs=(P("tm", None, "gx", "gy", None), P(), P(), P("gx", "gy")),
        out_specs=P("tm", None, "gx", "gy", None),
        check_vma=False,
    )
```

profile of v0, /device:TPU:26, one launch (start us, length us, event | category | flops | bytes accessed | tf_op | source)
XLA Modules:
  0.0 626.6 jit_solution(8260780207597803075)
XLA Ops:
  2.9 4.6 collective-permute-start.1
  10.2 4.5 collective-permute-start.5
  16.4 6.5 %fusion.375 = (f32[3,32,64,127]{3,2,1,0:T(8,128)}, f32[3,32,64,127]{3,2,1,0:T(8,128)}) fusion(f32[3,32,64,128]{3,2,1,0:T(8,128)} %bitcast.218), kind=kLoop, calls=%fused_computation.854 | loop fusion | bytes 12484608 | tf_op jit(solution)/shard_map/slice | solution.py:38
  30.9 4.8 collective-permute-start.21
  45.4 6.7 %fusion.355 = (f32[3,32,64,128]{3,2,1,0:T(8,128)S(1)}, f32[3,32,64,128]{3,2,1,0:T(8,128)S(1)}, f32[3,32,64,128]{3,2,1,0:T(8,128)S(1)}) fusion(f32[1,3,32,64,128]{4,3,2,1,0:T(8,128)S(1)} %copy-done, f32[3,32,64,128]{3,2,1,0:T(8,128)S(1)} %bitcast.220, f32[3,32,64,127]{3,2,1,0:T(8,128)} %get-tuple-element.58, f32[3,32,64,127]{3,2,1,0:T(8,128)S(1)} %copy-done.9, ...), kind=kLoop, calls=%fused_computation.851 | loop fusion | flops 15728640 | bytes 22280192 | tf_op jit(solution)/shard_map/add | solution.py:139
  58.3 4.5 collective-permute-start.9
  75.9 4.5 collective-permute-start.13
  92.2 4.8 collective-permute-start.17
  109.8 5.2 fusion.52
  116.3 4.5 collective-permute-start.25
  132.5 4.5 collective-permute-start.29
  148.8 4.5 collective-permute-start.33
  166.0 4.5 collective-permute-start.45
  171.9 4.5 collective-permute-start.37
  178.7 4.5 collective-permute-start.41
  207.7 4.5 collective-permute-start.49
  213.6 4.5 collective-permute-start.61
  227.3 4.5 collective-permute-start.53
  241.8 4.5 collective-permute-start.57
  261.9 4.5 collective-permute-start.65
  276.4 4.5 collective-permute-start.69
  306.1 7.6 %collective-permute-done.76 = f32[16,32,128]{2,1,0:T(8,128)S(1)} collective-permute-done((f32[16,32,128]{2,1,0:T(8,128)}, f32[16,32,128]{2,1,0:T(8,128)S(1)}, u32[]{:S(2)}, u32[]{:S(2)}) %collective-permute-start.76) | collective-permute-done | bytes 262176 | tf_op jit(solution)/shard_map/ppermute | solution.py:30
  317.3 4.5 collective-permute-start.78
  332.0 4.5 collective-permute-start.82
  346.5 4.5 collective-permute-start.86
  361.1 4.5 collective-permute-start.90
  375.8 4.5 collective-permute-start.94
  390.3 4.5 collective-permute-start.98
  404.8 7.0 %collective-permute-done.101 = f32[16,32,128]{2,1,0:T(8,128)S(1)} collective-permute-done((f32[16,32,128]{2,1,0:T(8,128)S(1)}, f32[16,32,128]{2,1,0:T(8,128)S(1)}, u32[]{:S(2)}, u32[]{:S(2)}) %collective-permute-start.101) | collective-permute-done | bytes 262176 | tf_op jit(solution)/shard_map/ppermute | solution.py:30
  428.6 4.5 collective-permute-start.107
  501.3 7.4 %collective-permute-done.126 = f32[16,32,128]{2,1,0:T(8,128)S(1)} collective-permute-done((f32[16,32,128]{2,1,0:T(8,128)S(1)}, f32[16,32,128]{2,1,0:T(8,128)S(1)}, u32[]{:S(2)}, u32[]{:S(2)}) %collective-permute-start.126) | collective-permute-done | bytes 262176 | tf_op jit(solution)/shard_map/ppermute | solution.py:30
  600.0 24.0 %collective-permute-done.151 = f32[32,64,128]{2,1,0:T(8,128)S(1)} collective-permute-done((f32[32,64,128]{2,1,0:T(8,128)S(1)}, f32[32,64,128]{2,1,0:T(8,128)S(1)}, u32[]{:S(2)}, u32[]{:S(2)}) %collective-permute-start.151) | collective-permute-done | bytes 1048608 | tf_op jit(solution)/shard_map/ppermute | solution.py:30
  (519 shorter events, 442.3 us)
Async XLA Ops:
  1.6 29.3 %collective-permute-start = (f32[3,1,64,128]{3,2,1,0:T(8,128)}, f32[3,1,64,128]{3,2,1,0:T(8,128)S(1)}, u32[]{:S(2)}, u32[]{:S(2)}) collective-permute-start(f32[3,1,64,128]{3,2,1,0:T(8,128)} %get-tuple-element.56), channel_id=1, source_target_pairs={{4,0},{5,1},{6,2},{7,3},{12,8},{13,9},{14,10},{15,11},{20,16},{21,... | collective-permute-start | bytes 294920 | tf_op jit(solution)/shard_map/ppermute | solution.py:22
  2.9 32.8 %collective-permute-start.1 = (f32[3,1,64,128]{3,2,1,0:T(8,128)}, f32[3,1,64,128]{3,2,1,0:T(8,128)S(1)}, u32[]{:S(2)}, u32[]{:S(2)}) collective-permute-start(f32[3,1,64,128]{3,2,1,0:T(8,128)} %get-tuple-element.55), channel_id=1, source_target_pairs={{0,4},{1,5},{2,6},{3,7},{8,12},{9,13},{10,14},{11,15},{16,20},{17,... | collective-permute-start | bytes 294920 | tf_op jit(solution)/shard_map/ppermute | solution.py:21
  8.9 28.8 %collective-permute-start.4 = (f32[1,64,128]{2,1,0:T(8,128)}, f32[1,64,128]{2,1,0:T(8,128)S(1)}, u32[]{:S(2)}, u32[]{:S(2)}) collective-permute-start(f32[1,64,128]{2,1,0:T(8,128)} %get-tuple-element.51), channel_id=1, source_target_pairs={{4,0},{5,1},{6,2},{7,3},{12,8},{13,9},{14,10},{15,11},{20,16},{21,... | collective-permute-start | bytes 98312 | tf_op jit(solution)/shard_map/ppermute | solution.py:22
  10.2 30.0 %collective-permute-start.5 = (f32[1,64,128]{2,1,0:T(8,128)}, f32[1,64,128]{2,1,0:T(8,128)S(1)}, u32[]{:S(2)}, u32[]{:S(2)}) collective-permute-start(f32[1,64,128]{2,1,0:T(8,128)} %get-tuple-element.50), channel_id=1, source_target_pairs={{0,4},{1,5},{2,6},{3,7},{8,12},{9,13},{10,14},{11,15},{16,20},{17,... | collective-permute-start | bytes 98312 | tf_op jit(solution)/shard_map/ppermute | solution.py:21
  14.8 82.3 %collective-permute-start.20 = (f32[1,64,128]{2,1,0:T(8,128)}, f32[1,64,128]{2,1,0:T(8,128)S(1)}, u32[]{:S(2)}, u32[]{:S(2)}) collective-permute-start(f32[1,64,128]{2,1,0:T(8,128)} %get-tuple-element.53), channel_id=1, source_target_pairs={{4,0},{5,1},{6,2},{7,3},{12,8},{13,9},{14,10},{15,11},{20,16},{21,... | collective-permute-start | bytes 98312 | tf_op jit(solution)/shard_map/ppermute | solution.py:22
  30.9 66.2 %collective-permute-start.21 = (f32[1,64,128]{2,1,0:T(8,128)}, f32[1,64,128]{2,1,0:T(8,128)S(1)}, u32[]{:S(2)}, u32[]{:S(2)}) collective-permute-start(f32[1,64,128]{2,1,0:T(8,128)} %get-tuple-element.52), channel_id=1, source_target_pairs={{0,4},{1,5},{2,6},{3,7},{8,12},{9,13},{10,14},{11,15},{16,20},{17,... | collective-permute-start | bytes 98312 | tf_op jit(solution)/shard_map/ppermute | solution.py:21
  40.2 11.9 %collective-permute-start.6 = (f32[34,1,128]{2,1,0:T(1,128)S(1)}, f32[34,1,128]{2,1,0:T(1,128)S(1)}, u32[]{:S(2)}, u32[]{:S(2)}) collective-permute-start(f32[34,1,128]{2,1,0:T(1,128)S(1)} %get-tuple-element.77), channel_id=1, source_target_pairs={{1,0},{2,1},{3,2},{5,4},{6,5},{7,6},{9,8},{10,9},{11,10},{13,12},{... | collective-permute-start | bytes 52232 | tf_op jit(solution)/shard_map/ppermute | solution.py:22
  43.4 8.8 %collective-permute-start.7 = (f32[34,1,128]{2,1,0:T(1,128)S(1)}, f32[34,1,128]{2,1,0:T(1,128)S(1)}, u32[]{:S(2)}, u32[]{:S(2)}) collective-permute-start(f32[34,1,128]{2,1,0:T(1,128)S(1)} %get-tuple-element.78), channel_id=1, source_target_pairs={{0,1},{1,2},{2,3},{4,5},{5,6},{6,7},{8,9},{9,10},{10,11},{12,13},{... | collective-permute-start | bytes 52232 | tf_op jit(solution)/shard_map/ppermute | solution.py:21
  90.9 10.6 %collective-permute-start.16 = (f32[1,64,128]{2,1,0:T(8,128)S(1)}, f32[1,64,128]{2,1,0:T(8,128)S(1)}, u32[]{:S(2)}, u32[]{:S(2)}) collective-permute-start(f32[1,64,128]{2,1,0:T(8,128)S(1)} %get-tuple-element.95), channel_id=1, source_target_pairs={{4,0},{5,1},{6,2},{7,3},{12,8},{13,9},{14,10},{15,11},{20,16},{21,... | collective-permute-start | bytes 98312 | tf_op jit(solution)/shard_map/ppermute | solution.py:22
  92.2 9.2 %collective-permute-start.17 = (f32[1,64,128]{2,1,0:T(8,128)S(1)}, f32[1,64,128]{2,1,0:T(8,128)S(1)}, u32[]{:S(2)}, u32[]{:S(2)}) collective-permute-start(f32[1,64,128]{2,1,0:T(8,128)S(1)} %get-tuple-element.94), channel_id=1, source_target_pairs={{0,4},{1,5},{2,6},{3,7},{8,12},{9,13},{10,14},{11,15},{16,20},{17,... | collective-permute-start | bytes 98312 | tf_op jit(solution)/shard_map/ppermute | solution.py:21
  97.1 9.9 %collective-permute-start.22 = (f32[34,1,128]{2,1,0:T(1,128)S(1)}, f32[34,1,128]{2,1,0:T(1,128)S(1)}, u32[]{:S(2)}, u32[]{:S(2)}) collective-permute-start(f32[34,1,128]{2,1,0:T(1,128)S(1)} %get-tuple-element.79), channel_id=1, source_target_pairs={{1,0},{2,1},{3,2},{5,4},{6,5},{7,6},{9,8},{10,9},{11,10},{13,12},{... | collective-permute-start | bytes 52232 | tf_op jit(solution)/shard_map/ppermute | solution.py:22
  164.7 14.0 %collective-permute-start.44 = (f32[1,32,128]{2,1,0:T(8,128)S(1)}, f32[1,32,128]{2,1,0:T(8,128)S(1)}, u32[]{:S(2)}, u32[]{:S(2)}) collective-permute-start(f32[1,32,128]{2,1,0:T(8,128)S(1)} %get-tuple-element.113), channel_id=1, source_target_pairs={{4,0},{5,1},{6,2},{7,3},{12,8},{13,9},{14,10},{15,11},{20,16},{21,... | collective-permute-start | bytes 49160 | tf_op jit(solution)/shard_map/ppermute | solution.py:22
  166.0 17.2 %collective-permute-start.45 = (f32[1,32,128]{2,1,0:T(8,128)S(1)}, f32[1,32,128]{2,1,0:T(8,128)S(1)}, u32[]{:S(2)}, u32[]{:S(2)}) collective-permute-start(f32[1,32,128]{2,1,0:T(8,128)S(1)} %get-tuple-element.112), channel_id=1, source_target_pairs={{0,4},{1,5},{2,6},{3,7},{8,12},{9,13},{10,14},{11,15},{16,20},{17,... | collective-permute-start | bytes 49160 | tf_op jit(solution)/shard_map/ppermute | solution.py:21
  170.6 20.3 %collective-permute-start.36 = (f32[3,1,32,128]{3,2,1,0:T(8,128)S(1)}, f32[3,1,32,128]{3,2,1,0:T(8,128)S(1)}, u32[]{:S(2)}, u32[]{:S(2)}) collective-permute-start(f32[3,1,32,128]{3,2,1,0:T(8,128)S(1)} %get-tuple-element.120), channel_id=1, source_target_pairs={{4,0},{5,1},{6,2},{7,3},{12,8},{13,9},{14,10},{15,11},{20,16},{21,... | collective-permute-start | bytes 147464 | tf_op jit(solution)/shard_map/ppermute | solution.py:22
  171.9 20.9 %collective-permute-start.37 = (f32[3,1,32,128]{3,2,1,0:T(8,128)S(1)}, f32[3,1,32,128]{3,2,1,0:T(8,128)S(1)}, u32[]{:S(2)}, u32[]{:S(2)}) collective-permute-start(f32[3,1,32,128]{3,2,1,0:T(8,128)S(1)} %get-tuple-element.119), channel_id=1, source_target_pairs={{0,4},{1,5},{2,6},{3,7},{8,12},{9,13},{10,14},{11,15},{16,20},{17,... | collective-permute-start | bytes 147464 | tf_op jit(solution)/shard_map/ppermute | solution.py:21
  176.5 8.7 %collective-permute-start.40 = (f32[2,1,64,128]{3,2,1,0:T(8,128)S(1)}, f32[2,1,64,128]{3,2,1,0:T(8,128)S(1)}, u32[]{:S(2)}, u32[]{:S(2)}) collective-permute-start(f32[2,1,64,128]{3,2,1,0:T(8,128)S(1)} %get-tuple-element.64), channel_id=1, source_target_pairs={{4,0},{5,1},{6,2},{7,3},{12,8},{13,9},{14,10},{15,11},{20,16},{21,... | collective-permute-start | bytes 196616 | tf_op jit(solution)/shard_map/ppermute | solution.py:22
  178.7 8.9 %collective-permute-start.41 = (f32[2,1,64,128]{3,2,1,0:T(8,128)S(1)}, f32[2,1,64,128]{3,2,1,0:T(8,128)S(1)}, u32[]{:S(2)}, u32[]{:S(2)}) collective-permute-start(f32[2,1,64,128]{3,2,1,0:T(8,128)S(1)} %get-tuple-element.63), channel_id=1, source_target_pairs={{0,4},{1,5},{2,6},{3,7},{8,12},{9,13},{10,14},{11,15},{16,20},{17,... | collective-permute-start | bytes 196616 | tf_op jit(solution)/shard_map/ppermute | solution.py:21
  183.3 21.8 %collective-permute-start.46 = (f32[18,1,128]{2,1,0:T(1,128)S(1)}, f32[18,1,128]{2,1,0:T(1,128)S(1)}, u32[]{:S(2)}, u32[]{:S(2)}) collective-permute-start(f32[18,1,128]{2,1,0:T(1,128)S(1)} %get-tuple-element.171), channel_id=1, source_target_pairs={{1,0},{2,1},{3,2},{5,4},{6,5},{7,6},{9,8},{10,9},{11,10},{13,12},{... | collective-permute-start | bytes 27656 | tf_op jit(solution)/shard_map/ppermute | solution.py:22
  185.3 19.9 %collective-permute-start.47 = (f32[18,1,128]{2,1,0:T(1,128)S(1)}, f32[18,1,128]{2,1,0:T(1,128)S(1)}, u32[]{:S(2)}, u32[]{:S(2)}) collective-permute-start(f32[18,1,128]{2,1,0:T(1,128)S(1)} %get-tuple-element.172), channel_id=1, source_target_pairs={{0,1},{1,2},{2,3},{4,5},{5,6},{6,7},{8,9},{9,10},{10,11},{12,13},{... | collective-permute-start | bytes 27656 | tf_op jit(solution)/shard_map/ppermute | solution.py:21
  187.7 8.8 %collective-permute-start.42 = (f32[2,34,1,128]{3,2,1,0:T(1,128)S(1)}, f32[2,34,1,128]{3,2,1,0:T(1,128)S(1)}, u32[]{:S(2)}, u32[]{:S(2)}) collective-permute-start(f32[2,34,1,128]{3,2,1,0:T(1,128)S(1)} %get-tuple-element.59), channel_id=1, source_target_pairs={{1,0},{2,1},{3,2},{5,4},{6,5},{7,6},{9,8},{10,9},{11,10},{13,12},{... | collective-permute-start | bytes 104456 | tf_op jit(solution)/shard_map/ppermute | solution.py:22
  192.9 11.3 %collective-permute-start.38 = (f32[3,18,1,128]{3,2,1,0:T(1,128)S(1)}, f32[3,18,1,128]{3,2,1,0:T(1,128)S(1)}, u32[]{:S(2)}, u32[]{:S(2)}) collective-permute-start(f32[3,18,1,128]{3,2,1,0:T(1,128)S(1)} %get-tuple-element.110), channel_id=1, source_target_pairs={{1,0},{2,1},{3,2},{5,4},{6,5},{7,6},{9,8},{10,9},{11,10},{13,12},{... | collective-permute-start | bytes 82952 | tf_op jit(solution)/shard_map/ppermute | solution.py:22
  206.4 11.7 %collective-permute-start.48 = (f32[1,32,128]{2,1,0:T(8,128)S(1)}, f32[1,32,128]{2,1,0:T(8,128)S(1)}, u32[]{:S(2)}, u32[]{:S(2)}) collective-permute-start(f32[1,32,128]{2,1,0:T(8,128)S(1)} %get-tuple-element.270), channel_id=1, source_target_pairs={{4,0},{5,1},{6,2},{7,3},{12,8},{13,9},{14,10},{15,11},{20,16},{21,... | collective-permute-start | bytes 49160 | tf_op jit(solution)/shard_map/ppermute | solution.py:22
  207.7 10.4 %collective-permute-start.49 = (f32[1,32,128]{2,1,0:T(8,128)S(1)}, f32[1,32,128]{2,1,0:T(8,128)S(1)}, u32[]{:S(2)}, u32[]{:S(2)}) collective-permute-start(f32[1,32,128]{2,1,0:T(8,128)S(1)} %get-tuple-element.269), channel_id=1, source_target_pairs={{0,4},{1,5},{2,6},{3,7},{8,12},{9,13},{10,14},{11,15},{16,20},{17,... | collective-permute-start | bytes 49160 | tf_op jit(solution)/shard_map/ppermute | solution.py:21
  212.3 34.1 %collective-permute-start.60 = (f32[1,32,128]{2,1,0:T(8,128)S(1)}, f32[1,32,128]{2,1,0:T(8,128)S(1)}, u32[]{:S(2)}, u32[]{:S(2)}) collective-permute-start(f32[1,32,128]{2,1,0:T(8,128)S(1)} %get-tuple-element.114), channel_id=1, source_target_pairs={{4,0},{5,1},{6,2},{7,3},{12,8},{13,9},{14,10},{15,11},{20,16},{21,... | collective-permute-start | bytes 49160 | tf_op jit(solution)/shard_map/ppermute | solution.py:22
  213.6 32.8 %collective-permute-start.61 = (f32[1,32,128]{2,1,0:T(8,128)S(1)}, f32[1,32,128]{2,1,0:T(8,128)S(1)}, u32[]{:S(2)}, u32[]{:S(2)}) collective-permute-start(f32[1,32,128]{2,1,0:T(8,128)S(1)} %get-tuple-element.115), channel_id=1, source_target_pairs={{0,4},{1,5},{2,6},{3,7},{8,12},{9,13},{10,14},{11,15},{16,20},{17,... | collective-permute-start | bytes 49160 | tf_op jit(solution)/shard_map/ppermute | solution.py:21
  240.5 10.2 %collective-permute-start.56 = (f32[1,32,128]{2,1,0:T(8,128)S(1)}, f32[1,32,128]{2,1,0:T(8,128)S(1)}, u32[]{:S(2)}, u32[]{:S(2)}) collective-permute-start(f32[1,32,128]{2,1,0:T(8,128)S(1)} %get-tuple-element.260), channel_id=1, source_target_pairs={{4,0},{5,1},{6,2},{7,3},{12,8},{13,9},{14,10},{15,11},{20,16},{21,... | collective-permute-start | bytes 49160 | tf_op jit(solution)/shard_map/ppermute | solution.py:22
  241.8 8.9 %collective-permute-start.57 = (f32[1,32,128]{2,1,0:T(8,128)S(1)}, f32[1,32,128]{2,1,0:T(8,128)S(1)}, u32[]{:S(2)}, u32[]{:S(2)}) collective-permute-start(f32[1,32,128]{2,1,0:T(8,128)S(1)} %get-tuple-element.259), channel_id=1, source_target_pairs={{0,4},{1,5},{2,6},{3,7},{8,12},{9,13},{10,14},{11,15},{16,20},{17,... | collective-permute-start | bytes 49160 | tf_op jit(solution)/shard_map/ppermute | solution.py:21
  246.4 9.8 %collective-permute-start.62 = (f32[18,1,128]{2,1,0:T(1,128)S(1)}, f32[18,1,128]{2,1,0:T(1,128)S(1)}, u32[]{:S(2)}, u32[]{:S(2)}) collective-permute-start(f32[18,1,128]{2,1,0:T(1,128)S(1)} %get-tuple-element.173), channel_id=1, source_target_pairs={{1,0},{2,1},{3,2},{5,4},{6,5},{7,6},{9,8},{10,9},{11,10},{13,12},{... | collective-permute-start | bytes 27656 | tf_op jit(solution)/shard_map/ppermute | solution.py:22
  304.8 8.9 %collective-permute-start.76 = (f32[16,32,128]{2,1,0:T(8,128)}, f32[16,32,128]{2,1,0:T(8,128)S(1)}, u32[]{:S(2)}, u32[]{:S(2)}) collective-permute-start(f32[16,32,128]{2,1,0:T(8,128)} %fusion.290), channel_id=1, source_target_pairs={{0,8},{8,16},{16,24},{1,9},{9,17},{17,25},{2,10},{10,18},{18,26},{... | collective-permute-start | bytes 786440 | tf_op jit(solution)/shard_map/ppermute | solution.py:30
  403.5 8.3 %collective-permute-start.101 = (f32[16,32,128]{2,1,0:T(8,128)S(1)}, f32[16,32,128]{2,1,0:T(8,128)S(1)}, u32[]{:S(2)}, u32[]{:S(2)}) collective-permute-start(f32[16,32,128]{2,1,0:T(8,128)S(1)} %fusion.242), channel_id=1, source_target_pairs={{0,8},{8,16},{16,24},{1,9},{9,17},{17,25},{2,10},{10,18},{18,26},{... | collective-permute-start | bytes 786440 | tf_op jit(solution)/shard_map/ppermute | solution.py:30
  500.0 8.7 %collective-permute-start.126 = (f32[16,32,128]{2,1,0:T(8,128)S(1)}, f32[16,32,128]{2,1,0:T(8,128)S(1)}, u32[]{:S(2)}, u32[]{:S(2)}) collective-permute-start(f32[16,32,128]{2,1,0:T(8,128)S(1)} %fusion.194), channel_id=1, source_target_pairs={{0,8},{8,16},{16,24},{1,9},{9,17},{17,25},{2,10},{10,18},{18,26},{... | collective-permute-start | bytes 786440 | tf_op jit(solution)/shard_map/ppermute | solution.py:30
  598.4 25.5 %collective-permute-start.151 = (f32[32,64,128]{2,1,0:T(8,128)S(1)}, f32[32,64,128]{2,1,0:T(8,128)S(1)}, u32[]{:S(2)}, u32[]{:S(2)}) collective-permute-start(f32[32,64,128]{2,1,0:T(8,128)S(1)} %slice_bitcast_fusion), channel_id=1, source_target_pairs={{0,8},{8,16},{16,24},{1,9},{9,17},{17,25},{2,10},{10,18},{18,26},{... | collective-permute-start | bytes 3145736 | tf_op jit(solution)/shard_map/ppermute | solution.py:30
  (155 other events, 1321.6 us)
where the time goes:
time: 639 us; the launch traced here: 627 us
  starting transfers between devices  389 us (61%)
  waiting for transfers between devices  152 us (24%)
  other arithmetic  49.8 us (8%)
  local copies, waits for them, and re-layouts  29.6 us (5%)
    ppermute x74, starting transfers between devices, extended(): before = lax.ppermute(last, axis, up)  254 us
    ppermute x74, starting transfers between devices, extended(): after = lax.ppermute(leading, axis, down)  130 us
    ppermute x74, waiting for transfers between devices, extended(): before = lax.ppermute(last, axis, up)  105 us
    ppermute x4, waiting for transfers between devices, from_behind(): return lax.ppermute(block, axis, route)  46 us
    div x34, other arithmetic, jacobi_update(): (right_side + coupling * (planar_weight * sums[1] + sums[2])) / (1.0 + co...  30.4 us
    slice x36, local copies, waits for them, and re-layouts, shifted_sums(): z_above = jnp.concatenate([center[..., 1:], zero_plane], axis=-1)  17.5 us
  transfers between devices with their start and end apart: 152, of which 60 were waited for; matrix products, arithmetic and copies ran while one was open for 8% of the time, Pallas kernels for 0%

commit v1 on v0

v1 whole, which is shorter than its diff:
```python
import functools
import jax
import jax.numpy as jnp
from jax import lax
from jax.experimental import pallas as pl
from jax.experimental.pallas import tpu as pltpu
from jax.sharding import PartitionSpec as P

TILE = 4
FW = 8
CW = 6
CN = 3
YW = 8
STEP_UNIT = 0.05
WEIGHTS = ((5.0 / 24.0, 1.0 / 3.0, -1.0 / 24.0), (-1.0 / 24.0, 1.0 / 3.0, 5.0 / 24.0))
VMEM_LIMIT = 50 * 1024 * 1024
AXES = ("tm", "gx", "gy")
ANY = pl.BlockSpec(memory_space=pl.ANY)
VM = pl.BlockSpec(memory_space=pltpu.VMEM)
SM = pl.BlockSpec(memory_space=pltpu.SMEM)
f32 = jnp.float32


def params(**kw):
    return pltpu.CompilerParams(vmem_limit_bytes=VMEM_LIMIT, **kw)


def shape(*dims):
    return jax.ShapeDtypeStruct(dims, f32)


def partner(i, color, size):
    j = i + 1 if (i + color) % 2 == 0 else i - 1
    return j if 0 <= j < size else None


def colors(size):
    return [k for k in (0, 1) if any(partner(i, k, size) is not None for i in range(size))]


def routes(sizes, cx, cy, hop):
    nt, nx, ny = sizes
    out = []
    for t in range(nt):
        if hop is not None and t != hop:
            continue
        for x in range(nx):
            px = x if cx is None else partner(x, cx, nx)
            for y in range(ny):
                py = y if cy is None else partner(y, cy, ny)
                if px is None or py is None:
                    continue
                target = t if hop is None else t + 1
                out.append(((t * nx + px) * ny + py, (target * nx + x) * ny + y))
    return out


def message_keys(nx, ny):
    keys = [(k, None) for k in colors(nx)]
    keys += [(k, l) for k in colors(nx) for l in colors(ny)]
    keys += [(None, l) for l in colors(ny)]
    return keys


def upper(axis, color):
    return lax.rem(lax.axis_index(axis) + color, 2) == 0


def pick(cond, a, b):
    return jnp.where(cond, jnp.int32(a), jnp.int32(b))


def times(steps, sect):
    h = steps[sect].astype(f32) * STEP_UNIT
    return h, 0.5 * h


def reaction(v):
    return v - v * v * v


def run_copies(pairs, sems):
    copies = [pltpu.make_async_copy(a, b, sems.at[i]) for i, (a, b) in enumerate(pairs)]
    for c in copies:
        c.start()
    for c in copies:
        c.wait()


def pack_kernel(keys, u, *rest):
    outs, sems = rest[:-1], rest[-1]
    nx, ny = u.shape[1], u.shape[2]
    pairs = []
    for (k, l), o in zip(keys, outs):
        xs = pl.ds(0, nx) if k is None else pl.ds(pick(upper("gx", k), nx - FW, 0), FW)
        ys = pl.ds(0, ny) if l is None else pl.ds(pl.multiple_of(pick(upper("gy", l), ny - YW, 0), 8), YW)
        pairs.append((u.at[:, xs, ys, :], o))
    run_copies(pairs, sems)


def coefficient_kernel(local, whole_tiles, kinds, diffs, steps, fine, coarse):
    tx, ty = local
    wx, wy = whole_tiles
    _, a = times(steps, lax.axis_index("tm"))
    x0 = lax.axis_index("gx") * tx
    y0 = lax.axis_index("gy") * ty
    sub = lax.broadcasted_iota(jnp.int32, (8, 128), 0)

    def value(i, j):
        ok = (i >= 0) & (i < wx) & (j >= 0) & (j < wy)
        kind = kinds[jnp.clip(i, 0, wx - 1), jnp.clip(j, 0, wy - 1)]
        return jnp.where(ok, diffs[kind], 0.0)

    ft = FW // TILE

    def fine_row(i, _):
        for jt in range(fine.shape[2] // 8):
            base = y0 - YW // TILE + jt * 2
            k = jnp.where(sub < 4, value(x0 - ft + i, base), value(x0 - ft + i, base + 1))
            inv = 1.0 / (1.0 + a * k * 6.0)
            at = pl.ds(jt * 8, 8)
            fine[0, i, at, :] = k
            fine[1, i, at, :] = a * k * inv
            fine[2, i, at, :] = inv
        return 0

    lax.fori_loop(0, fine.shape[1], fine_row, 0)
    ct = CW // 2

    def coarse_row(i, _):
        for jt in range(coarse.shape[2] // 8):
            base = y0 - YW // 2 + jt * 4
            v = [value(x0 - ct + i, base + q) for q in range(4)]
            k = jnp.where(sub < 4, jnp.where(sub < 2, v[0], v[1]), jnp.where(sub < 6, v[2], v[3]))
            inv = 1.0 / (1.0 + a * k * 3.0)
            at = pl.ds(jt * 8, 8)
            coarse[0, i, at, :] = a * k * inv
            coarse[1, i, at, :] = inv
        return 0

    lax.fori_loop(0, coarse.shape[1], coarse_row, 0)


def neighbours(ref, x, masks):
    c = ref[x]
    rows = c.shape[0]
    px = ref[x + 1] + ref[x - 1]
    py = pltpu.roll(c, 1, 0) + pltpu.roll(c, rows - 1, 0)
    z = pltpu.roll(c, 1, 1) * masks[0] + pltpu.roll(c, 127, 1) * masks[1]
    return c, px + py, z


def z_masks(rows):
    lane = lax.broadcasted_iota(jnp.int32, (rows, 128), 1)
    return (jnp.where(lane == 0, 0.0, 1.0), jnp.where(lane == 127, 0.0, 1.0))


def fine_kernel(keys, ckeys, steps, u, fine, *rest):
    nmsg = len(keys)
    msgs, rest = rest[:nmsg], rest[nmsg:]
    w1o, w2o, co = rest[:3]
    nc = len(ckeys)
    couts, rest = rest[3 : 3 + nc], rest[3 + nc :]
    ue, f0, q0, qa, qb, p2, w1, w2, tmp, sems = rest
    nx, ny = u.shape[1], u.shape[2]
    ye = ny + 2 * YW
    h, a = times(steps, lax.axis_index("tm"))
    gx, ngx = lax.axis_index("gx"), lax.axis_size("gx")
    low, high = gx > 0, gx < ngx - 1
    zero = jnp.zeros((ye, 128), f32)
    bufs = [q0, qa, qb, w1, w2]

    @pl.when(jnp.logical_not(low))
    def _():
        for j in range(3):
            ue[j, FW - 1] = zero
        for b in bufs:
            b[FW - 1] = zero

    @pl.when(jnp.logical_not(high))
    def _():
        for j in range(3):
            ue[j, FW + nx] = zero
        for b in bufs:
            b[FW + nx] = zero

    if len(colors(lax.axis_size("gy"))) < 2:
        def clear(i, _):
            for j in range(3):
                ue[j, i] = zero
            return 0
        lax.fori_loop(0, ue.shape[1], clear, 0)

    pairs = [(u, ue.at[:, pl.ds(FW, nx), pl.ds(YW, ny), :])]
    for (k, l), m in zip(keys, msgs):
        xs = pl.ds(FW, nx) if k is None else pl.ds(pick(upper("gx", k), FW + nx, 0), FW)
        ys = pl.ds(YW, ny) if l is None else pl.ds(pl.multiple_of(pick(upper("gy", l), YW + ny, 0), 8), YW)
        pairs.append((m, ue.at[:, xs, ys, :]))
    run_copies(pairs, sems)
    masks = z_masks(ye)

    def rows(r, body):
        first = FW - jnp.where(low, r, 0)
        last = FW + nx + jnp.where(high, r, 0)
        lax.fori_loop(first, last, lambda x, _: (body(x), 0)[1], 0)

    def kap(n, x):
        return fine[n, lax.div(x, TILE)]

    def stage1(x):
        k = kap(0, x)
        c, f = [], []
        for j in range(3):
            cj, pj, zj = neighbours(ue.at[j], x, masks)
            c.append(cj)
            f.append(reaction(cj) + k * (pj + zj - 6.0 * cj))
        f0[x] = f[0]
        h0 = WEIGHTS[0][0] * f[0] + WEIGHTS[0][1] * f[1] + WEIGHTS[0][2] * f[2]
        h1 = WEIGHTS[1][0] * f[0] + WEIGHTS[1][1] * f[1] + WEIGHTS[1][2] * f[2]
        q0[x] = (c[0] + h * h0 - c[1]) * kap(2, x)
        p2[x] = h * h1 - c[2] - a * reaction(c[1])

    rows(7, stage1)

    def jacobi(src, start, x):
        _, p, z = neighbours(src, x, masks)
        return start[x] + kap(1, x) * (p + z)

    def into(dst, src, start):
        def body(x):
            dst[x] = jacobi(src, start, x)
        return body

    rows(6, into(qa, q0, q0))
    rows(5, into(qb, qa, q0))

    def end1(x):
        w = ue[1, x] + jacobi(qb, q0, x)
        w1[x] = w
        p2[x] = (w + a * reaction(w) + p2[x]) * kap(2, x)

    rows(4, end1)

    @pl.when(jnp.logical_not(low))
    def _():
        p2[FW - 1] = zero

    @pl.when(jnp.logical_not(high))
    def _():
        p2[FW + nx] = zero

    rows(3, into(qa, p2, p2))
    rows(2, into(qb, qa, p2))

    def end2(x):
        w2[x] = ue[2, x] + jacobi(qb, p2, x)

    rows(1, end2)

    def halve(slot, v):
        tmp[slot] = v
        n = ny // 2
        return tmp[slot, pl.ds(YW, n, stride=2), :] + tmp[slot, pl.ds(YW + 1, n, stride=2), :]

    def coarse_row(i, _):
        sums = [0.0] * 5
        for d in range(2):
            x = FW + 2 * i + d
            k = kap(0, x)
            u0 = ue[0, x]
            g = [f0[x]]
            w = [u0]
            for ref in (w1, w2):
                c, p, z = neighbours(ref, x, masks)
                w.append(c)
                g.append(reaction(c) + k * (p + z - 6.0 * c))
            for m, ref in ((1, w1o), (2, w2o)):
                ref[2 * i + d] = w[m][YW : YW + ny]
            for m in range(2):
                sums[m] = sums[m] + (WEIGHTS[m][0] * g[0] + WEIGHTS[m][1] * g[1] + WEIGHTS[m][2] * g[2])
            for m in range(3):
                sums[2 + m] = sums[2 + m] + w[m]
        c0, c1, u0, u1, u2 = [halve(s, v) * 0.25 for s, v in enumerate(sums)]
        co[0, i] = h * c0 - a * reaction(u0) - u1
        co[1, i] = u1
        co[2, i] = h * c1 - a * reaction(u1) - u2
        co[3, i] = u0
        co[4, i] = u2
        return 0

    lax.fori_loop(0, nx // 2, coarse_row, 0)
    cx, cy = nx // 2, ny // 2
    fields = ((0, CW), (1, CN), (2, CN), (3, CW))
    for (k, l), o in zip(ckeys, couts):
        ys = pl.ds(0, cy) if l is None else pl.ds(pl.multiple_of(pick(upper("gy", l), cy - YW, 0), 8), YW)
        at = 0
        for fld, width in fields:
            if k is None:
                width, first = cx, 0
            else:
                first = pick(upper("gx", k), cx - width, 0)
            o[pl.ds(at, width)] = co[fld, pl.ds(first, width), ys, :]
            at += width


def assemble_kernel(keys, co, *rest):
    nm = len(keys)
    msgs, (ge, ce), sems = rest[:nm], rest[nm : nm + 2], rest[nm + 2]
    cx, cy = co.shape[1], co.shape[2]
    zero = jnp.zeros(ge.shape[1:], f32)
    for f in range(3):
        ge[f] = zero
    ce[...] = zero
    fields = ((0, CW), (1, CN), (2, CN), (3, CW))
    pairs = []

    def target(f):
        return ce if f == 3 else ge.at[f]

    for f, _ in fields:
        pairs.append((co.at[f], target(f).at[pl.ds(CW, cx), pl.ds(YW, cy), :]))
    for (k, l), m in zip(keys, msgs):
        ys = pl.ds(YW, cy) if l is None else pl.ds(pl.multiple_of(pick(upper("gy", l), YW + cy, 0), 8), YW)
        at = 0
        for f, width in fields:
            if k is None:
                width, first = cx, CW
            else:
                first = pick(upper("gx", k), CW + cx, CW - width)
            pairs.append((m.at[pl.ds(at, width)], target(f).at[pl.ds(first, width), ys, :]))
            at += width
    run_copies(pairs, sems)


def chain_kernel(turn, keys, steps, ge, coef, co, *rest):
    first = turn == 0
    if first:
        ce, rest = rest[0], rest[1:]
        nm = 0
    else:
        old, own, rest = rest[0], rest[1], rest[2:]
        nm = len(keys)
        msgs, rest = rest[:nm], rest[nm:]
    state = rest[0]
    rest = rest[1:]
    no = len(keys)
    couts, rest = rest[:no], rest[no:]
    cin, q0, qa, qb, sems = rest
    cx, cy = co.shape[1], co.shape[2]
    ye = cy + 2 * YW
    sect = lax.axis_index("tm")
    h, a = times(steps, sect)
    gx, ngx = lax.axis_index("gx"), lax.axis_size("gx")
    low, high = gx > 0, gx < ngx - 1

    @pl.when(sect == turn)
    def _():
        zero = jnp.zeros((ye, 128), f32)
        for b in (q0, qa, qb):
            b[CW - 1] = zero
            b[CW + cx] = zero
        if first:
            c = ce
        else:
            c = cin
            if len(colors(ngx)) < 2 or len(colors(lax.axis_size("gy"))) < 2:
                cin[...] = jnp.zeros(cin.shape, f32)
            pairs = [(own, cin.at[pl.ds(CW, cx), pl.ds(YW, cy), :])]
            for (k, l), m in zip(keys, msgs):
                xs = pl.ds(CW, cx) if k is None else pl.ds(pick(upper("gx", k), CW + cx, 0), CW)
                ys = pl.ds(YW, cy) if l is None else pl.ds(pl.multiple_of(pick(upper("gy", l), YW + cy, 0), 8), YW)
                pairs.append((m, cin.at[xs, ys, :]))
            run_copies(pairs, sems)
        masks = z_masks(ye)

        def rows(r, body):
            begin = CW - jnp.where(low, r, 0)
            end = CW + cx + jnp.where(high, r, 0)
            lax.fori_loop(begin, end, lambda x, _: (body(x), 0)[1], 0)

        def jacobi(src, x):
            _, p, z = neighbours(src, x, masks)
            return q0[x] + coef[0, lax.div(x, 2)] * (0.25 * p + z)

        def into(dst, src):
            def body(x):
                dst[x] = jacobi(src, x)
            return body

        def start(x):
            v = c[x]
            q0[x] = (v + a * reaction(v) + ge[0, x]) * coef[1, lax.div(x, 2)]

        rows(6, start)
        rows(5, into(qa, q0))
        rows(4, into(qb, qa))

        def middle(x):
            w = ge[1, x] + jacobi(qb, x)
            qa[x] = w

        rows(3, middle)

        def keep(i, _):
            state[0, i] = c[CW + i, YW : YW + cy]
            state[1, i] = qa[CW + i, YW : YW + cy]
            return 0

        lax.fori_loop(0, cx, keep, 0)

        def second(x):
            w = qa[x]
            q0[x] = (w + a * reaction(w) + ge[2, x]) * coef[1, lax.div(x, 2)]

        rows(3, second)

        @pl.when(jnp.logical_not(low))
        def _():
            qa[CW - 1] = zero

        @pl.when(jnp.logical_not(high))
        def _():
            qa[CW + cx] = zero

        rows(2, into(qa, q0))
        rows(1, into(qb, qa))

        def end(x):
            i = x - CW
            state[2, i] = co[4, i] + jacobi(qb, x)[YW : YW + cy]

        rows(0, end)
        for (k, l), o in zip(keys, couts):
            xs = pl.ds(0, cx) if k is None else pl.ds(pick(upper("gx", k), cx - CW, 0), CW)
            ys = pl.ds(0, cy) if l is None else pl.ds(pl.multiple_of(pick(upper("gy", l), cy - YW, 0), 8), YW)
            o[...] = state[2, xs, ys, :]


def finish_kernel(u0, arrived, w1, w2, state, co, out, tmp):
    sect = lax.axis_index("tm")
    ny = u0.shape[1]
    half = ny // 2

    def spread(slot, v):
        tmp[slot, pl.ds(0, half, stride=2), :] = v
        tmp[slot, pl.ds(1, half, stride=2), :] = v
        return tmp[slot]

    def row(i, _):
        base = [jnp.where(sect == 0, u0[2 * i + d], arrived[2 * i + d]) for d in range(2)]
        tmp[3] = base[0] + base[1]
        low = (tmp[3, pl.ds(0, half, stride=2), :] + tmp[3, pl.ds(1, half, stride=2), :]) * 0.25
        d0 = spread(0, state[0, i] - low)
        d1 = spread(1, state[1, i] - co[1, i])
        d2 = spread(2, state[2, i] - co[4, i])
        for d in range(2):
            out[0, 2 * i + d] = base[d] + d0
            out[1, 2 * i + d] = w1[2 * i + d] + d1
            out[2, 2 * i + d] = w2[2 * i + d] + d2
        return 0

    lax.fori_loop(0, u0.shape[0] // 2, row, 0)


def per_device(sizes, fine_nodes, section_steps, diffusivities, tile_kinds):
    nt, ngx, ngy = sizes
    u = fine_nodes[0]
    nodes, nx, ny, cz = u.shape
    cx, cy = nx // 2, ny // 2
    keys = message_keys(ngx, ngy)
    nk = len(keys)

    def dims(k, l, wx, lx, ly):
        return (lx if k is None else wx, ly if l is None else YW, cz)

    def send(arrays, hop):
        return [lax.ppermute(v, AXES, routes(sizes, k, l, hop)) for (k, l), v in zip(keys, arrays)]

    packed = pl.pallas_call(
        functools.partial(pack_kernel, keys),
        out_shape=[shape(nodes, *dims(k, l, FW, nx, ny)) for k, l in keys],
        in_specs=[ANY],
        out_specs=[ANY] * nk,
        scratch_shapes=[pltpu.SemaphoreType.DMA((nk,))],
        compiler_params=params(),
        name="pack",
    )(u)
    halos = send(packed, None)

    kinds = lax.all_gather(tile_kinds, "gy", axis=1, tiled=True)
    kinds = lax.all_gather(kinds, "gx", axis=0, tiled=True)
    fye, cye = ny + 2 * YW, cy + 2 * YW
    fine, coef = pl.pallas_call(
        functools.partial(coefficient_kernel, tile_kinds.shape, kinds.shape),
        out_shape=[shape(3, (nx + 2 * FW) // TILE, fye, cz), shape(2, (cx + 2 * CW) // 2, cye, cz)],
        in_specs=[SM, SM, SM],
        out_specs=[VM, VM],
        compiler_params=params(),
        name="coefficients",
    )(kinds, diffusivities, section_steps)

    xe = nx + 2 * FW
    buf = pltpu.VMEM((xe, fye, cz), f32)
    depth = 2 * CW + 2 * CN
    out = pl.pallas_call(
        functools.partial(fine_kernel, keys, keys),
        out_shape=[shape(nx, ny, cz), shape(nx, ny, cz), shape(5, cx, cy, cz)]
        + [shape(*dims(k, l, depth, 4 * cx, cy)) for k, l in keys],
        in_specs=[SM, ANY, VM] + [ANY] * nk,
        out_specs=[VM] * (3 + nk),
        scratch_shapes=[pltpu.VMEM((3, xe, fye, cz), f32)] + [buf] * 7
        + [pltpu.VMEM((5, fye, cz), f32), pltpu.SemaphoreType.DMA((nk + 1,))],
        compiler_params=params(),
        name="fine_sweep",
    )(section_steps, u, fine, *halos)
    w1, w2, co = out[:3]
    strips = send(out[3:], None)
    arrived = lax.ppermute(w2, "tm", [(i, i + 1) for i in range(nt - 1)])

    ncopy = 4 + 4 * nk
    ge, ce = pl.pallas_call(
        functools.partial(assemble_kernel, keys),
        out_shape=[shape(3, cx + 2 * CW, cye, cz), shape(cx + 2 * CW, cye, cz)],
        in_specs=[ANY] + [ANY] * nk,
        out_specs=[VM, VM],
        scratch_shapes=[pltpu.SemaphoreType.DMA((ncopy,))],
        compiler_params=params(),
        name="assemble",
    )(co, *strips)

    state, handed = None, None
    cbuf = pltpu.VMEM((cx + 2 * CW, cye, cz), f32)
    for n in range(nt):
        last = n == nt - 1
        args = [section_steps, ge, coef, co]
        specs = [SM, VM, VM, VM]
        alias = {}
        if n == 0:
            args.append(ce)
            specs.append(VM)
        else:
            alias = {len(args): 0}
            args += [state] + handed
            specs += [VM] + [ANY] * len(handed)
        res = pl.pallas_call(
            functools.partial(chain_kernel, n, keys),
            out_shape=[shape(3, cx, cy, cz)] + [shape(*dims(k, l, CW, cx, cy)) for k, l in keys],
            in_specs=specs,
            out_specs=[VM] * (1 + nk),
            scratch_shapes=[cbuf] * 4 + [pltpu.SemaphoreType.DMA((nk + 1,))],
            input_output_aliases=alias,
            compiler_params=params(),
            name=f"chain_{n}",
        )(*args)
        state = res[0]
        if not last:
            own = lax.ppermute(state[2], AXES, routes(sizes, None, None, n))
            handed = [own] + send(res[1:], n)

    blk = 8
    fspec = pl.BlockSpec((blk, ny, cz), lambda i: (i, 0, 0))
    result = pl.pallas_call(
        finish_kernel,
        grid=(nx // blk,),
        out_shape=shape(3, nx, ny, cz),
        in_specs=[fspec] * 4
        + [pl.BlockSpec((3, blk // 2, cy, cz), lambda i: (0, i, 0, 0)), pl.BlockSpec((5, blk // 2, cy, cz), lambda i: (0, i, 0, 0))],
        out_specs=pl.BlockSpec((3, blk, ny, cz), lambda i: (0, i, 0, 0)),
        scratch_shapes=[pltpu.VMEM((4, ny, cz), f32)],
        compiler_params=params(),
        name="finish",
    )(u[0], arrived, w1, w2, state, co)
    return result[None]


def solution(mesh):
    sizes = tuple(mesh.shape[a] for a in AXES)
    return jax.shard_map(
        functools.partial(per_device, sizes),
        mesh=mesh,
        in_specs=(P("tm", None, "gx", "gy", None), P(), P(), P("gx", "gy")),
        out_specs=P("tm", None, "gx", "gy", None),
        check_vma=False,
    )
```

time: 639 us -> 188 us (0.29); the launches traced: 627 us -> 187 us
  starting transfers between devices: 389 us -> 32.9 us
  waiting for transfers between devices: 152 us -> 70.1 us
  Pallas kernels: 0 us -> 63.9 us
  other arithmetic: 49.8 us -> 0 us
  local copies, waits for them, and re-layouts: 29.6 us -> 5.22 us
  blocking collectives: 0 us -> 14.1 us
    ppermute x152 -> x29, starting transfers between devices: 389 us -> 32.9 us  [the longest x25 28.9 us: send(): lax.ppermute(v, AXES, routes(sizes, k, l, hop))]
    ppermute x152 -> x29, waiting for transfers between devices: 152 us -> 70.1 us  [the longest x25 70.1 us: send(): lax.ppermute(v, AXES, routes(sizes, k, l, hop))]
    pallas_call x0 -> x9, Pallas kernels: none -> 63.9 us  [the longest x1 35.1 us: per_device(): pl.pallas_call(functools.partial(fine_kernel, keys, keys), out_shape=[sha...]
    div x34 -> x0, other arithmetic: 30.4 us -> none  [jacobi_update(): (right_side + coupling * (planar_weight * sums[1] + sums[2])) / (1.0 + co...]
    slice x74 -> x0, local copies, waits for them, and re-layouts: 24.7 us -> none  [the longest x36 17.5 us: shifted_sums(): z_above = jnp.concatenate([center[..., 1:], zero_plane], axis=-1)]
    all_gather x0 -> x2, blocking collectives: none -> 14.1 us  [the longest x1 8.78 us: per_device(): kinds = lax.all_gather(kinds, 'gx', axis=0, tiled=True)]
    add x5 -> x0, other arithmetic: 11 us -> none  [the longest x1 6.75 us: per_device(): forces = reactions + diffusion]
  transfers between devices with their start and end apart: 152 -> 29, of which waited for: 60 -> 5; matrix products, arithmetic and copies ran while one was open for 8% -> 1% of each run, Pallas kernels for 0% -> 10%
where the time goes in v1:
time: 188 us; the launch traced here: 187 us
  waiting for transfers between devices  70.1 us (37%)
  Pallas kernels  63.9 us (34%)
  starting transfers between devices  32.9 us (18%)
  blocking collectives  14.1 us (8%)
  local copies, waits for them, and re-layouts  5.22 us (3%)
    ppermute x25, waiting for transfers between devices, send(): lax.ppermute(v, AXES, routes(sizes, k, l, hop))  70.1 us
    pallas_call x1, Pallas kernels, per_device(): pl.pallas_call(functools.partial(fine_kernel, keys, keys), out_shape=[sha...  35.1 us
    ppermute x25, starting transfers between devices, send(): lax.ppermute(v, AXES, routes(sizes, k, l, hop))  28.9 us
    pallas_call x4, Pallas kernels, per_device(): pl.pallas_call(functools.partial(chain_kernel, n, keys), out_shape=[shape...  17.7 us
    all_gather x1, blocking collectives, per_device(): kinds = lax.all_gather(kinds, 'gx', axis=0, tiled=True)  8.78 us
    all_gather x1, blocking collectives, per_device(): kinds = lax.all_gather(tile_kinds, 'gy', axis=1, tiled=True)  5.28 us
    pallas_call x1, Pallas kernels, per_device(): pl.pallas_call(finish_kernel, grid=(nx // blk,), out_shape=shape(3, nx, n...  4.21 us
  transfers between devices with their start and end apart: 29, of which 5 were waited for; matrix products, arithmetic and copies ran while one was open for 1% of the time, Pallas kernels for 10%

profile of v1, /device:TPU:26, one launch (start us, length us, event | category | flops | bytes accessed | tf_op | source)
XLA Modules:
  0.0 186.6 jit_solution(13162054395784926381)
XLA Ops:
  0.0 1.6 pack.1
  1.6 1.5 collective-permute-start
  3.1 2.5 %collective-permute-start.4 = (f32[3,32,8,128]{3,2,1,0:T(8,128)S(1)}, f32[3,32,8,128]{3,2,1,0:T(8,128)S(1)}, u32[]{:S(2)}, u32[]{:S(2)}) collective-permute-start(f32[3,32,8,128]{3,2,1,0:T(8,128)S(1)} %get-tuple-element.46), channel_id=1, source_target_pairs={{2,1},{1,2},{6,5},{5,6},{10,9},{9,10},{14,13},{13,14},{18,17},{17,... | collective-permute-start | bytes 1179656 | tf_op jit(solution)/shard_map/ppermute | solution.py:477
  5.8 3.0 %collective-permute-start.2 = (f32[3,8,8,128]{3,2,1,0:T(8,128)S(1)}, f32[3,8,8,128]{3,2,1,0:T(8,128)S(1)}, u32[]{:S(2)}, u32[]{:S(2)}) collective-permute-start(f32[3,8,8,128]{3,2,1,0:T(8,128)S(1)} %get-tuple-element.44), channel_id=1, source_target_pairs={{6,1},{5,2},{2,5},{1,6},{14,9},{13,10},{10,13},{9,14},{22,17},{21,... | collective-permute-start | bytes 294920 | tf_op jit(solution)/shard_map/ppermute | solution.py:477
  8.8 5.3 %all-gather = s32[4,16,8]{1,2,0:T(8,128)S(1)} all-gather(s32[1,16,8]{1,2,0:T(8,128)S(1)} %bitcast.19), channel_id=1, replica_groups=mesh['tm'=4,'gx'=2,'gy'=4] {'gy'}, dimensions={0}, use_global_device_ids=true | all-gather | bytes 2560 | tf_op jit(solution)/shard_map/all_gather | solution.py:490
  14.7 0.8 reshape.3
  15.5 8.8 %all_gather.7.kinds = s32[16,64]{1,0:T(8,128)S(1)} all-gather(s32[8,64]{1,0:T(8,128)S(1)} %bitcast.18), channel_id=1, replica_groups=mesh['tm'=4,'gx'=2,'gy'=4] {'gx'}, dimensions={0}, use_global_device_ids=true | all-gather | bytes 6144 | tf_op jit(solution)/shard_map/all_gather | solution.py:491
  24.3 3.2 %coefficients.1 = (f32[3,12,80,128]{3,2,1,0:T(8,128)S(1)}, f32[2,14,48,128]{3,2,1,0:T(8,128)S(1)}) custom-call(s32[16,64]{1,0:T(8,128)S(1)} %all_gather.7.kinds, f32[16]{0:T(128)S(1)} %copy-done.4, s32[4]{0:T(128)S(1)} %copy-done.3), custom_call_target="tpu_custom_call" | custom-call | tf_op jit(solution)/shard_map/coefficients/pallas_call | solution.py:493
  27.5 1.1 copy-done.2
  28.7 35.1 %fine_sweep.1 = (f32[32,64,128]{2,1,0:T(8,128)S(1)}, f32[32,64,128]{2,1,0:T(8,128)}, f32[5,16,32,128]{3,2,1,0:T(8,128)}, f32[18,32,128]{2,1,0:T(8,128)S(1)}, f32...) custom-call(s32[4]{0:T(128)S(1)} %copy-done.3, ...), custom_call_target="tpu_custom_call" | custom-call | tf_op jit(solution)/shard_map/fine_sweep/pallas_call | solution.py:505
  63.8 1.5 collective-permute-start.6
  65.3 1.9 %collective-permute-start.10 = (f32[64,8,128]{2,1,0:T(8,128)S(1)}, f32[64,8,128]{2,1,0:T(8,128)S(1)}, u32[]{:S(2)}, u32[]{:S(2)}) collective-permute-start(f32[64,8,128]{2,1,0:T(8,128)S(1)} %get-tuple-element.54), channel_id=1, source_target_pairs={{2,1},{1,2},{6,5},{5,6},{10,9},{9,10},{14,13},{13,14},{18,17},{17,... | collective-permute-start | bytes 786440 | tf_op jit(solution)/shard_map/ppermute | solution.py:477
  68.0 4.5 %collective-permute-start.8 = (f32[18,8,128]{2,1,0:T(8,128)S(1)}, f32[18,8,128]{2,1,0:T(8,128)S(1)}, u32[]{:S(2)}, u32[]{:S(2)}) collective-permute-start(f32[18,8,128]{2,1,0:T(8,128)S(1)} %get-tuple-element.52), channel_id=1, source_target_pairs={{6,1},{5,2},{2,5},{1,6},{14,9},{13,10},{10,13},{9,14},{22,17},{21,... | collective-permute-start | bytes 221192 | tf_op jit(solution)/shard_map/ppermute | solution.py:477
  72.5 2.0 %collective-permute-done.8.rest_2_ = f32[18,8,128]{2,1,0:T(8,128)S(1)} collective-permute-done((f32[18,8,128]{2,1,0:T(8,128)S(1)}, f32[18,8,128]{2,1,0:T(8,128)S(1)}, u32[]{:S(2)}, u32[]{:S(2)}) %collective-permute-start.8) | collective-permute-done | bytes 73760 | tf_op jit(solution)/shard_map/ppermute | solution.py:477
  74.6 1.3 copy-done
  75.9 2.0 %assemble.1 = (f32[3,28,48,128]{3,2,1,0:T(8,128)}, f32[28,48,128]{2,1,0:T(8,128)S(1)}) custom-call(f32[5,16,32,128]{3,2,1,0:T(8,128)S(1)} %copy-done, f32[18,32,128]{2,1,0:T(8,128)S(1)} %collective-permute-done.6.rest_0_, f32[18,8,128]{2,1,0:T(8,128)S(1)} %collective-permute-done.7.rest_1_, f32[18,8,128]{2,1,0:T(8,128)S(1)} %collective-permute-done.8.rest_2_, ...), custom_call_target="tpu_custom_call" | custom-call | tf_op jit(solution)/shard_map/assemble/pallas_call | solution.py:521
  77.9 1.7 chain_0.1
  83.7 1.3 collective-permute-start.5
  85.1 1.7 chain_1.1
  90.9 1.7 chain_2.1
  92.6 1.3 collective-permute-start.25
  93.9 1.3 collective-permute-start.26
  95.2 1.3 collective-permute-start.23
  96.5 1.3 collective-permute-start.24
  97.8 58.5 %collective-permute-done.25.rest_3_ = f32[6,8,128]{2,1,0:T(8,128)S(1)} collective-permute-done((f32[6,8,128]{2,1,0:T(8,128)S(1)}, f32[6,8,128]{2,1,0:T(8,128)S(1)}, u32[]{:S(2)}, u32[]{:S(2)}) %collective-permute-start.25) | collective-permute-done | bytes 24608 | tf_op jit(solution)/shard_map/ppermute | solution.py:477
  156.3 1.3 collective-permute-start.27
  157.6 2.3 %collective-permute-done.26.rest_4_ = f32[6,8,128]{2,1,0:T(8,128)S(1)} collective-permute-done((f32[6,8,128]{2,1,0:T(8,128)S(1)}, f32[6,8,128]{2,1,0:T(8,128)S(1)}, u32[]{:S(2)}, u32[]{:S(2)}) %collective-permute-start.26) | collective-permute-done | bytes 24608 | tf_op jit(solution)/shard_map/ppermute | solution.py:477
  160.0 1.3 collective-permute-start.28
  161.3 1.3 slice_bitcast_fusion.u0
  162.7 7.0 %collective-permute-done.28.rest_6_ = f32[16,8,128]{2,1,0:T(8,128)S(1)} collective-permute-done((f32[16,8,128]{2,1,0:T(8,128)S(1)}, f32[16,8,128]{2,1,0:T(8,128)S(1)}, u32[]{:S(2)}, u32[]{:S(2)}) %collective-permute-start.28) | collective-permute-done | bytes 65568 | tf_op jit(solution)/shard_map/ppermute | solution.py:477
  169.7 12.6 %chain_3.1 = (f32[3,16,32,128]{3,2,1,0:T(8,128)S(1)}, f32[6,32,128]{2,1,0:T(8,128)}, f32[6,8,128]{2,1,0:T(8,128)}, f32[6,8,128]{2,1,0:T(8,128)}, f32[16,8,128]{2,1,0:T(8,128)}, /*index=5*/f32[16,8,128]{2,1,0:T(8,128)}) custom-call(s32[4]{0:T(128)S(1)} %copy-done.3, f32[3,28,48,128]{3,2,1,0:T(8,128)} %get-tuple-element.55.ge, ...), custom_call_target="tpu_custom_call", output_to_operand_aliasing={{0}: (4, {})} | custom-call | tf_op jit(solution)/shard_map/chain_3/pallas_call | solution.py:545
  182.4 4.2 %finish.1 = f32[3,32,64,128]{3,2,1,0:T(8,128)} custom-call(f32[32,64,128]{2,1,0:T(8,128)S(1)} %slice_bitcast_fusion.u0, f32[32,64,128]{2,1,0:T(8,128)S(1)} %collective-permute-done.5.arrived, f32[32,64,128]{2,1,0:T(8,128)S(1)} %get-tuple-element.48.w1, f32[32,64,128]{2,1,0:T(8,128)} %get-tuple-element.47.w2, f32[3,16,32,128]{3,2,1,0:T(8,128)S(1)} %get-tuple-element.76.state, ...), custom_call_target="tpu_custom_call" | custom-call | tf_op jit(solution)/shard_map/finish/pallas_call | solution.py:562
  (57 shorter events, 9.7 us)
Async XLA Ops:
  0.0 8.8 %copy-start.6 = (s32[8,16]{1,0:T(8,128)S(1)}, s32[8,16]{1,0:T(8,128)}, u32[]{:S(2)}) copy-start(s32[8,16]{1,0:T(8,128)} %param.7) | copy-start | bytes 1540
  0.0 24.3 %copy-start.3 = (s32[4]{0:T(128)S(1)}, s32[4]{0:T(128)}, u32[]{:S(2)}) copy-start(s32[4]{0:T(128)} %steps.11) | copy-start | bytes 52
  0.0 24.3 %copy-start.4 = (f32[16]{0:T(128)S(1)}, f32[16]{0:T(128)}, u32[]{:S(2)}) copy-start(f32[16]{0:T(128)} %diffs.1) | copy-start | bytes 196
  1.6 27.0 %collective-permute-start = (f32[3,8,64,128]{3,2,1,0:T(8,128)S(1)}, f32[3,8,64,128]{3,2,1,0:T(8,128)S(1)}, u32[]{:S(2)}, u32[]{:S(2)}) collective-permute-start(f32[3,8,64,128]{3,2,1,0:T(8,128)S(1)} %get-tuple-element.42), channel_id=1, source_target_pairs={{4,0},{5,1},{6,2},{7,3},{0,4},{1,5},{2,6},{3,7},{12,8},{13,9},{14,... | collective-permute-start | bytes 2359304 | tf_op jit(solution)/shard_map/ppermute | solution.py:477
  3.1 25.5 %collective-permute-start.3 = (f32[3,32,8,128]{3,2,1,0:T(8,128)S(1)}, f32[3,32,8,128]{3,2,1,0:T(8,128)S(1)}, u32[]{:S(2)}, u32[]{:S(2)}) collective-permute-start(f32[3,32,8,128]{3,2,1,0:T(8,128)S(1)} %get-tuple-element.45), channel_id=1, source_target_pairs={{1,0},{0,1},{3,2},{2,3},{5,4},{4,5},{7,6},{6,7},{9,8},{8,9},{11,10... | collective-permute-start | bytes 1179656 | tf_op jit(solution)/shard_map/ppermute | solution.py:477
  3.1 25.5 %collective-permute-start.4 = (f32[3,32,8,128]{3,2,1,0:T(8,128)S(1)}, f32[3,32,8,128]{3,2,1,0:T(8,128)S(1)}, u32[]{:S(2)}, u32[]{:S(2)}) collective-permute-start(f32[3,32,8,128]{3,2,1,0:T(8,128)S(1)} %get-tuple-element.46), channel_id=1, source_target_pairs={{2,1},{1,2},{6,5},{5,6},{10,9},{9,10},{14,13},{13,14},{18,17},{17,... | collective-permute-start | bytes 1179656 | tf_op jit(solution)/shard_map/ppermute | solution.py:477
  5.7 23.0 %collective-permute-start.1 = (f32[3,8,8,128]{3,2,1,0:T(8,128)S(1)}, f32[3,8,8,128]{3,2,1,0:T(8,128)S(1)}, u32[]{:S(2)}, u32[]{:S(2)}) collective-permute-start(f32[3,8,8,128]{3,2,1,0:T(8,128)S(1)} %get-tuple-element.43), channel_id=1, source_target_pairs={{5,0},{4,1},{7,2},{6,3},{1,4},{0,5},{3,6},{2,7},{13,8},{12,9},{15,... | collective-permute-start | bytes 294920 | tf_op jit(solution)/shard_map/ppermute | solution.py:477
  5.8 22.9 %collective-permute-start.2 = (f32[3,8,8,128]{3,2,1,0:T(8,128)S(1)}, f32[3,8,8,128]{3,2,1,0:T(8,128)S(1)}, u32[]{:S(2)}, u32[]{:S(2)}) collective-permute-start(f32[3,8,8,128]{3,2,1,0:T(8,128)S(1)} %get-tuple-element.44), channel_id=1, source_target_pairs={{6,1},{5,2},{2,5},{1,6},{14,9},{13,10},{10,13},{9,14},{22,17},{21,... | collective-permute-start | bytes 294920 | tf_op jit(solution)/shard_map/ppermute | solution.py:477
  63.8 10.8 %collective-permute-start.6 = (f32[18,32,128]{2,1,0:T(8,128)S(1)}, f32[18,32,128]{2,1,0:T(8,128)S(1)}, u32[]{:S(2)}, u32[]{:S(2)}) collective-permute-start(f32[18,32,128]{2,1,0:T(8,128)S(1)} %get-tuple-element.50), channel_id=1, source_target_pairs={{4,0},{5,1},{6,2},{7,3},{0,4},{1,5},{2,6},{3,7},{12,8},{13,9},{14,... | collective-permute-start | bytes 884744 | tf_op jit(solution)/shard_map/ppermute | solution.py:477
  65.3 9.3 %collective-permute-start.10 = (f32[64,8,128]{2,1,0:T(8,128)S(1)}, f32[64,8,128]{2,1,0:T(8,128)S(1)}, u32[]{:S(2)}, u32[]{:S(2)}) collective-permute-start(f32[64,8,128]{2,1,0:T(8,128)S(1)} %get-tuple-element.54), channel_id=1, source_target_pairs={{2,1},{1,2},{6,5},{5,6},{10,9},{9,10},{14,13},{13,14},{18,17},{17,... | collective-permute-start | bytes 786440 | tf_op jit(solution)/shard_map/ppermute | solution.py:477
  67.2 7.3 %collective-permute-start.9 = (f32[64,8,128]{2,1,0:T(8,128)S(1)}, f32[64,8,128]{2,1,0:T(8,128)S(1)}, u32[]{:S(2)}, u32[]{:S(2)}) collective-permute-start(f32[64,8,128]{2,1,0:T(8,128)S(1)} %get-tuple-element.53), channel_id=1, source_target_pairs={{1,0},{0,1},{3,2},{2,3},{5,4},{4,5},{7,6},{6,7},{9,8},{8,9},{11,10... | collective-permute-start | bytes 786440 | tf_op jit(solution)/shard_map/ppermute | solution.py:477
  67.3 5.2 %collective-permute-start.7 = (f32[18,8,128]{2,1,0:T(8,128)S(1)}, f32[18,8,128]{2,1,0:T(8,128)S(1)}, u32[]{:S(2)}, u32[]{:S(2)}) collective-permute-start(f32[18,8,128]{2,1,0:T(8,128)S(1)} %get-tuple-element.51), channel_id=1, source_target_pairs={{5,0},{4,1},{7,2},{6,3},{1,4},{0,5},{3,6},{2,7},{13,8},{12,9},{15,... | collective-permute-start | bytes 221192 | tf_op jit(solution)/shard_map/ppermute | solution.py:477
  68.0 6.6 %collective-permute-start.8 = (f32[18,8,128]{2,1,0:T(8,128)S(1)}, f32[18,8,128]{2,1,0:T(8,128)S(1)}, u32[]{:S(2)}, u32[]{:S(2)}) collective-permute-start(f32[18,8,128]{2,1,0:T(8,128)S(1)} %get-tuple-element.52), channel_id=1, source_target_pairs={{6,1},{5,2},{2,5},{1,6},{14,9},{13,10},{10,13},{9,14},{22,17},{21,... | collective-permute-start | bytes 221192 | tf_op jit(solution)/shard_map/ppermute | solution.py:477
  79.7 5.4 %collective-permute-start.11 = (f32[16,32,128]{2,1,0:T(8,128)S(1)}, f32[16,32,128]{2,1,0:T(8,128)S(1)}, u32[]{:S(2)}, u32[]{:S(2)}) collective-permute-start(f32[16,32,128]{2,1,0:T(8,128)S(1)} %slice_bitcast_fusion.3), channel_id=1, source_target_pairs={{0,8},{1,9},{2,10},{3,11},{4,12},{5,13},{6,14},{7,15}} | collective-permute-start | bytes 786440 | tf_op jit(solution)/shard_map/ppermute | solution.py:557
  80.3 4.7 %collective-permute-start.12 = (f32[6,32,128]{2,1,0:T(8,128)S(1)}, f32[6,32,128]{2,1,0:T(8,128)S(1)}, u32[]{:S(2)}, u32[]{:S(2)}) collective-permute-start(f32[6,32,128]{2,1,0:T(8,128)S(1)} %get-tuple-element.59), channel_id=1, source_target_pairs={{4,8},{5,9},{6,10},{7,11},{0,12},{1,13},{2,14},{3,15}} | collective-permute-start | bytes 294920 | tf_op jit(solution)/shard_map/ppermute | solution.py:477
  81.0 2.0 %collective-permute-start.13 = (f32[6,8,128]{2,1,0:T(8,128)S(1)}, f32[6,8,128]{2,1,0:T(8,128)S(1)}, u32[]{:S(2)}, u32[]{:S(2)}) collective-permute-start(f32[6,8,128]{2,1,0:T(8,128)S(1)} %get-tuple-element.60), channel_id=1, source_target_pairs={{5,8},{4,9},{7,10},{6,11},{1,12},{0,13},{3,14},{2,15}} | collective-permute-start | bytes 73736 | tf_op jit(solution)/shard_map/ppermute | solution.py:477
  81.7 3.3 %collective-permute-start.15 = (f32[16,8,128]{2,1,0:T(8,128)S(1)}, f32[16,8,128]{2,1,0:T(8,128)S(1)}, u32[]{:S(2)}, u32[]{:S(2)}) collective-permute-start(f32[16,8,128]{2,1,0:T(8,128)S(1)} %get-tuple-element.62), channel_id=1, source_target_pairs={{1,8},{0,9},{3,10},{2,11},{5,12},{4,13},{7,14},{6,15}} | collective-permute-start | bytes 196616 | tf_op jit(solution)/shard_map/ppermute | solution.py:477
  82.4 2.7 %collective-permute-start.16 = (f32[16,8,128]{2,1,0:T(8,128)S(1)}, f32[16,8,128]{2,1,0:T(8,128)S(1)}, u32[]{:S(2)}, u32[]{:S(2)}) collective-permute-start(f32[16,8,128]{2,1,0:T(8,128)S(1)} %get-tuple-element.63), channel_id=1, source_target_pairs={{2,9},{1,10},{6,13},{5,14}} | collective-permute-start | bytes 196616 | tf_op jit(solution)/shard_map/ppermute | solution.py:477
  83.0 0.7 collective-permute-start.14
  83.7 98.6 %collective-permute-start.5 = (f32[32,64,128]{2,1,0:T(8,128)S(1)}, f32[32,64,128]{2,1,0:T(8,128)S(1)}, u32[]{:S(2)}, u32[]{:S(2)}) collective-permute-start(f32[32,64,128]{2,1,0:T(8,128)S(1)} %copy-done.5), channel_id=1, source_target_pairs={{0,8},{8,16},{16,24},{1,9},{9,17},{17,25},{2,10},{10,18},{18,26},{... | collective-permute-start | bytes 3145736 | tf_op jit(solution)/shard_map/ppermute | solution.py:518
  86.8 4.1 %collective-permute-start.17 = (f32[16,32,128]{2,1,0:T(8,128)S(1)}, f32[16,32,128]{2,1,0:T(8,128)S(1)}, u32[]{:S(2)}, u32[]{:S(2)}) collective-permute-start(f32[16,32,128]{2,1,0:T(8,128)S(1)} %slice_bitcast_fusion.2), channel_id=1, source_target_pairs={{8,16},{9,17},{10,18},{11,19},{12,20},{13,21},{14,22},{15,23}} | collective-permute-start | bytes 786440 | tf_op jit(solution)/shard_map/ppermute | solution.py:557
  87.5 3.4 %collective-permute-start.18 = (f32[6,32,128]{2,1,0:T(8,128)S(1)}, f32[6,32,128]{2,1,0:T(8,128)S(1)}, u32[]{:S(2)}, u32[]{:S(2)}) collective-permute-start(f32[6,32,128]{2,1,0:T(8,128)S(1)} %get-tuple-element.65), channel_id=1, source_target_pairs={{12,16},{13,17},{14,18},{15,19},{8,20},{9,21},{10,22},{11,23}} | collective-permute-start | bytes 294920 | tf_op jit(solution)/shard_map/ppermute | solution.py:477
  88.1 1.3 collective-permute-start.19
  88.8 1.4 collective-permute-start.20
  89.5 1.4 collective-permute-start.21
  90.2 0.7 collective-permute-start.22
  92.6 63.8 %collective-permute-start.25 = (f32[6,8,128]{2,1,0:T(8,128)S(1)}, f32[6,8,128]{2,1,0:T(8,128)S(1)}, u32[]{:S(2)}, u32[]{:S(2)}) collective-permute-start(f32[6,8,128]{2,1,0:T(8,128)S(1)} %get-tuple-element.72), channel_id=1, source_target_pairs={{21,24},{20,25},{23,26},{22,27},{17,28},{16,29},{19,30},{18,31}} | collective-permute-start | bytes 73736 | tf_op jit(solution)/shard_map/ppermute | solution.py:477
  93.9 66.1 %collective-permute-start.26 = (f32[6,8,128]{2,1,0:T(8,128)S(1)}, f32[6,8,128]{2,1,0:T(8,128)S(1)}, u32[]{:S(2)}, u32[]{:S(2)}) collective-permute-start(f32[6,8,128]{2,1,0:T(8,128)S(1)} %get-tuple-element.73), channel_id=1, source_target_pairs={{22,25},{21,26},{18,29},{17,30}} | collective-permute-start | bytes 73736 | tf_op jit(solution)/shard_map/ppermute | solution.py:477
  95.2 74.5 %collective-permute-start.23 = (f32[16,32,128]{2,1,0:T(8,128)S(1)}, f32[16,32,128]{2,1,0:T(8,128)S(1)}, u32[]{:S(2)}, u32[]{:S(2)}) collective-permute-start(f32[16,32,128]{2,1,0:T(8,128)S(1)} %slice_bitcast_fusion.1), channel_id=1, source_target_pairs={{16,24},{17,25},{18,26},{19,27},{20,28},{21,29},{22,30},{23,31}} | collective-permute-start | bytes 786440 | tf_op jit(solution)/shard_map/ppermute | solution.py:557
  96.5 73.2 %collective-permute-start.24 = (f32[6,32,128]{2,1,0:T(8,128)S(1)}, f32[6,32,128]{2,1,0:T(8,128)S(1)}, u32[]{:S(2)}, u32[]{:S(2)}) collective-permute-start(f32[6,32,128]{2,1,0:T(8,128)S(1)} %get-tuple-element.71), channel_id=1, source_target_pairs={{20,24},{21,25},{22,26},{23,27},{16,28},{17,29},{18,30},{19,31}} | collective-permute-start | bytes 294920 | tf_op jit(solution)/shard_map/ppermute | solution.py:477
  156.3 6.4 %collective-permute-start.27 = (f32[16,8,128]{2,1,0:T(8,128)S(1)}, f32[16,8,128]{2,1,0:T(8,128)S(1)}, u32[]{:S(2)}, u32[]{:S(2)}) collective-permute-start(f32[16,8,128]{2,1,0:T(8,128)S(1)} %get-tuple-element.74), channel_id=1, source_target_pairs={{17,24},{16,25},{19,26},{18,27},{21,28},{20,29},{23,30},{22,31}} | collective-permute-start | bytes 196616 | tf_op jit(solution)/shard_map/ppermute | solution.py:477
  160.0 9.7 %collective-permute-start.28 = (f32[16,8,128]{2,1,0:T(8,128)S(1)}, f32[16,8,128]{2,1,0:T(8,128)S(1)}, u32[]{:S(2)}, u32[]{:S(2)}) collective-permute-start(f32[16,8,128]{2,1,0:T(8,128)S(1)} %get-tuple-element.75), channel_id=1, source_target_pairs={{18,25},{17,26},{22,29},{21,30}} | collective-permute-start | bytes 196616 | tf_op jit(solution)/shard_map/ppermute | solution.py:477
  (4 other events, 10.3 us)

commit v2 on v1

v2 whole, which is shorter than its diff:
```python
import functools
import jax
import jax.numpy as jnp
from jax import lax
from jax.experimental import pallas as pl
from jax.experimental.pallas import tpu as pltpu
from jax.sharding import PartitionSpec as P

TILE = 4
FW = 8
CW = 6
CN = 3
FEW, MANY = 2, 4
YW = 8
STEP_UNIT = 0.05
WEIGHTS = ((5.0 / 24.0, 1.0 / 3.0, -1.0 / 24.0), (-1.0 / 24.0, 1.0 / 3.0, 5.0 / 24.0))
AXES = ("tm", "gx", "gy")
ANY = pl.BlockSpec(memory_space=pl.ANY)
VM = pl.BlockSpec(memory_space=pltpu.VMEM)
SM = pl.BlockSpec(memory_space=pltpu.SMEM)
f32 = jnp.float32


def params(mib):
    return pltpu.CompilerParams(vmem_limit_bytes=mib * 1024 * 1024)


def shape(*dims):
    return jax.ShapeDtypeStruct(dims, f32)


def partner(i, color, size):
    j = i + 1 if (i + color) % 2 == 0 else i - 1
    return j if 0 <= j < size else None


def colors(size):
    return [k for k in (0, 1) if any(partner(i, k, size) is not None for i in range(size))]


def routes(sizes, cx, cy, hop):
    nt, nx, ny = sizes
    out = []
    for t in range(nt):
        if hop is not None and t != hop:
            continue
        for x in range(nx):
            px = x if cx is None else partner(x, cx, nx)
            for y in range(ny):
                py = y if cy is None else partner(y, cy, ny)
                if px is None or py is None:
                    continue
                target = t if hop is None else t + 1
                out.append(((t * nx + px) * ny + py, (target * nx + x) * ny + y))
    return out


def message_keys(nx, ny):
    keys = [(k, None) for k in colors(nx)]
    keys += [(k, l) for k in colors(nx) for l in colors(ny)]
    keys += [(None, l) for l in colors(ny)]
    return keys


def upper(axis, color):
    return lax.rem(lax.axis_index(axis) + color, 2) == 0


def pick(cond, a, b):
    return jnp.where(cond, jnp.int32(a), jnp.int32(b))


def times(steps, sect):
    h = steps[sect].astype(f32) * STEP_UNIT
    return h, 0.5 * h


def reaction(v):
    return v - v * v * v


def run_copies(pairs, sems):
    copies = [pltpu.make_async_copy(a, b, sems.at[i]) for i, (a, b) in enumerate(pairs)]
    for c in copies:
        c.start()
    for c in copies:
        c.wait()


def table_rows(rows, tiles):
    return -(-tiles // rows)


def table_copies(table, msg, base, out):
    tiles, height = table.shape[0], msg.shape[1]
    pairs = []
    for i in range(table_rows(height, tiles)):
        n = min(height, tiles - i * height)
        pair = (table.at[pl.ds(i * height, n)], msg.at[base + i, pl.ds(0, n)])
        pairs.append(pair if out else pair[::-1])
    return pairs


def pack_kernel(keys, u, table, *rest):
    outs, sems = rest[:-1], rest[-1]
    nx, ny = u.shape[1], u.shape[2]
    pairs = []
    for (k, l), o in zip(keys, outs):
        w = nx if k is None else FW
        xs = pl.ds(0 if k is None else pick(upper("gx", k), nx - FW, 0), w)
        ys = pl.ds(0, ny) if l is None else pl.ds(pl.multiple_of(pick(upper("gy", l), ny - YW, 0), 8), YW)
        pairs += [(u.at[j, xs, ys, :], o.at[pl.ds(j * w, w)]) for j in range(3)]
        pairs += table_copies(table, o, 3 * w, True)
    run_copies(pairs, sems)


def permuted(ref, *lead):
    t_count = ref.shape[-2] // 8
    return jnp.concatenate([ref[(*lead, pl.ds(t, 8, stride=t_count))] for t in range(t_count)], axis=-2)


def store_plain(ref, lead, value):
    t_count = value.shape[-2] // 8
    for t in range(t_count):
        ref[(*lead, pl.ds(t, 8, stride=t_count))] = value[..., t * 8 : t * 8 + 8, :]


def expand(tables, tx, ty, row, piece, cells):
    sub = lax.broadcasted_iota(jnp.int32, (8, 128), 0)
    lane = lax.broadcasted_iota(jnp.int32, (8, 128), 1)
    if isinstance(row, int):
        sx = 0 if row < 0 else (2 if row >= tx else 1)
        r = row - (sx - 1) * tx
    else:
        sx = jnp.where(row < 0, 0, jnp.where(row >= tx, 2, 1))
        r = row - (sx - 1) * tx
    runs = ty * cells // 8
    per = 8 // cells
    sy, first = (0, ty - per) if piece < 0 else ((2, 0) if piece >= runs else (1, piece * per))
    hot = lane == first + lax.div(sub, cells)
    return jnp.sum(jnp.where(hot, tables[sx, sy, pl.ds(r, 1), :], 0.0), axis=1, keepdims=True)


def fill_coefficients(tables, local, cells, low, rows, plain, write):
    tx, ty = local
    count = plain.shape[1] // 8
    for i in range(rows):
        slot = i % plain.shape[0]
        for p in range(count):
            k = expand(tables, tx, ty, low + i, p - 1, cells)
            plain[slot, p * 8 : p * 8 + 8, :] = jnp.broadcast_to(k, (8, 128))
        write(i, jnp.concatenate([plain[slot, pl.ds(t, 8, stride=count), :] for t in range(count)], axis=0))


def coarse_coefficient_kernel(local, steps, tables, coarse, plain):
    _, a = times(steps, lax.axis_index("tm"))

    def write(i, k):
        inv = 1.0 / (1.0 + a * k * 3.0)
        coarse[0, i] = a * k * inv
        coarse[1, i] = inv

    rows = local[0] + CW
    fill_coefficients(tables, local, TILE // 2, -(CW // 2), rows, plain, write)
    for i in range(rows, coarse.shape[1]):
        write(i, jnp.zeros(plain.shape[1:], f32))


def neighbours(v, masks):
    c = v[1:-1]
    px = v[2:] + v[:-2]
    before = jnp.concatenate([pltpu.roll(c[:, -8:], 1, 1), c[:, :-8]], axis=1)
    after = jnp.concatenate([c[:, 8:], pltpu.roll(c[:, :8], 7, 1)], axis=1)
    z = pltpu.roll(c, 1, 2) * masks[0] + pltpu.roll(c, 127, 2) * masks[1]
    return c, px + (before + after), z


def z_masks():
    lane = lax.broadcasted_iota(jnp.int32, (1, 8, 128), 2)
    return (jnp.where(lane == 0, 0.0, 1.0), jnp.where(lane == 127, 0.0, 1.0))


def wide_masks(rows, y):
    return tuple(jnp.concatenate([jnp.concatenate([m] * (y // 8), axis=1)] * rows, axis=0) for m in z_masks())


def sweep_rows(own, width, r, step, body):
    gx, ngx = lax.axis_index("gx"), lax.axis_size("gx")
    n = own + r * min(ngx - 1, 2)
    pad = -n % step
    if ngx == 2:
        begin = width - pick(gx > 0, r, pad)
    else:
        begin = width - r * min(ngx - 1, 2) // 2
    lax.fori_loop(0, (n + pad) // step, lambda i, _: (body(begin + i * step), 0)[1], 0)


def clear_walls(width, own, bufs, count=4):
    gx, ngx = lax.axis_index("gx"), lax.axis_size("gx")
    for b in bufs:
        zero = jnp.zeros((count,) + b.shape[1:], f32)

        @pl.when(gx == 0)
        def _():
            b[width - count : width] = zero

        @pl.when(gx == ngx - 1)
        def _():
            b[width + own : width + own + count] = zero


SEAM = 12
FIELDS = 10


class Stages:
    def __init__(self, u, f0, q0, qa, qb, p2, w1, w2, fine, h, a, tile_of):
        self.u, self.f0, self.q0, self.qa, self.qb, self.p2, self.w1, self.w2 = u, f0, q0, qa, qb, p2, w1, w2
        self.fine, self.h, self.a, self.tile_of = fine, h, a, tile_of

    def coef(self, n, x, step):
        return jnp.stack([self.fine[n, self.tile_of(x + i)] for i in range(step)])

    def forces(self, x, step, masks):
        k, h, a = self.coef(0, x, step), self.h, self.a
        c, f = [], []
        for j in range(3):
            cj, pj, zj = neighbours(self.u(j, pl.ds(x - 1, step + 2)), masks)
            c.append(cj)
            f.append(reaction(cj) + k * (pj + zj - 6.0 * cj))
        at = pl.ds(x, step)
        self.f0[at] = f[0]
        h0 = WEIGHTS[0][0] * f[0] + WEIGHTS[0][1] * f[1] + WEIGHTS[0][2] * f[2]
        h1 = WEIGHTS[1][0] * f[0] + WEIGHTS[1][1] * f[1] + WEIGHTS[1][2] * f[2]
        self.q0[at] = (c[0] + h * h0 - c[1]) * self.coef(2, x, step)
        self.p2[at] = h * h1 - c[2] - a * reaction(c[1])

    def jacobi(self, src, start, x, step, masks):
        _, p, z = neighbours(src[pl.ds(x - 1, step + 2)], masks)
        return start[pl.ds(x, step)] + self.coef(1, x, step) * (p + z)

    def into(self, dst, src, start):
        def body(x, step, masks):
            dst[pl.ds(x, step)] = self.jacobi(src, start, x, step, masks)
        return body

    def end1(self, x, step, masks):
        at = pl.ds(x, step)
        w = self.u(1, at) + self.jacobi(self.qb, self.q0, x, step, masks)
        self.w1[at] = w
        self.p2[at] = (w + self.a * reaction(w) + self.p2[at]) * self.coef(2, x, step)

    def end2(self, x, step, masks):
        at = pl.ds(x, step)
        self.w2[at] = self.u(2, at) + self.jacobi(self.qb, self.p2, x, step, masks)

    def bodies(self):
        return [
            (1, self.forces),
            (2, self.into(self.qa, self.q0, self.q0)),
            (3, self.into(self.qb, self.qa, self.q0)),
            (4, self.end1),
            (5, self.into(self.qa, self.p2, self.p2)),
            (6, self.into(self.qb, self.qa, self.p2)),
            (7, self.end2),
        ]

    def coarse_pair(self, x, i, w1o, w2o, co, plain, tmp, ny):
        ye = ny + 2 * YW
        masks = wide_masks(2, ye)
        h, a = self.h, self.a

        def pair_sum(v):
            v = v[0] + v[1]
            return jnp.concatenate([v[t : t + 8] + v[t + 8 : t + 16] for t in range(0, ye, 16)], axis=0)

        at = pl.ds(x, 2)
        k = self.coef(0, x, 2)
        g = [self.f0[at]]
        w = [self.u(0, at)]
        for m, (ref, out) in enumerate(((self.w1, w1o), (self.w2, w2o))):
            c, p, z = neighbours(ref[pl.ds(x - 1, 4)], masks)
            w.append(c)
            g.append(reaction(c) + k * (p + z - 6.0 * c))
            store_plain(tmp, (2 * m + 0,), c[0])
            store_plain(tmp, (2 * m + 1,), c[1])
            out[pl.ds(2 * i, 2)] = tmp[2 * m : 2 * m + 2, YW : YW + ny]
        c0, c1 = [pair_sum(wt[0] * g[0] + wt[1] * g[1] + wt[2] * g[2]) * 0.25 for wt in WEIGHTS]
        u0, u1, u2 = [pair_sum(v) * 0.25 for v in w]
        values = (h * c0 - a * reaction(u0) - u1, u1, h * c1 - a * reaction(u1) - u2, u0, u2)
        for n, v in enumerate(values):
            store_plain(plain, (n,), v)
            co[n, i] = plain[n, YW // 2 : YW // 2 + ny // 2]


def seam_count(size):
    return min(size - 1, 2)


def seam_is_low(seam):
    return lax.axis_index("gx") > 0 if lax.axis_size("gx") == 2 else seam == 0


def target_y(l, ny):
    return pl.ds(YW, ny) if l is None else pl.ds(pl.multiple_of(pick(upper("gy", l), YW + ny, 0), 8), YW)


def inner_kernel(keys, local, seams, steps, u, table, *rest):
    nmsg = len(keys)
    msgs, rest = rest[:nmsg], rest[nmsg:]
    w1o, w2o, co, seam, rest = rest[0], rest[1], rest[2], rest[3], rest[4:]
    ue, f0, q0, qa, qb, p2, w1, w2, fine, tables, plain, tmp, sems = rest
    nx, ny = u.shape[1], u.shape[2]
    ye = ny + 2 * YW
    h, a = times(steps, lax.axis_index("tm"))

    if nmsg < 2:
        def clear(i, _):
            for j in range(3):
                ue[j, i] = jnp.zeros((ye, 128), f32)
            return 0
        lax.fori_loop(0, ue.shape[1], clear, 0)
    clear_walls(FW, nx, [ue.at[0], ue.at[1], ue.at[2], q0, qa, qb, p2, w1, w2])
    for j in (0, 2):
        tables[1, j] = jnp.zeros(tables.shape[2:], f32)
    pairs = [(u, ue.at[:, pl.ds(FW, nx), pl.ds(YW, ny), :])]
    for (_, l), m in zip(keys, msgs):
        pairs += [(m.at[pl.ds(j * nx, nx)], ue.at[j, pl.ds(FW, nx), target_y(l, ny), :]) for j in range(3)]
        pairs += table_copies(tables.at[1, pick(upper("gy", l), 2, 0)], m, 3 * nx, False)
    pairs.append((table, tables.at[1, 1]))
    run_copies(pairs, sems)

    def write(i, k):
        inv = 1.0 / (1.0 + a * k * 6.0)
        fine[0, i] = k
        fine[1, i] = a * k * inv
        fine[2, i] = inv

    ft = FW // TILE
    for i in list(range(ft)) + list(range(ft + local[0], fine.shape[1])):
        write(i, jnp.zeros((ye, 128), f32))
    fill_coefficients(tables, local, TILE, 0, local[0], tmp, lambda i, k: write(ft + i, k))
    st = Stages(
        lambda j, at: permuted(ue, j, at), f0, q0, qa, qb, p2, w1, w2, fine, h, a, lambda x: lax.div(x, TILE)
    )
    for k, body in st.bodies():
        step = FEW if k == 1 else MANY
        if seams == 2 and (nx - 2 * k) % step:
            step = 2
        masks = wide_masks(step, ye)
        sweep_rows(nx, FW, -k, step, functools.partial(lambda body, step, masks, x: body(x, step, masks), body, step, masks))

    def coarse_rows(x):
        st.coarse_pair(x, lax.div(x - FW, 2), w1o, w2o, co, plain, tmp, ny)

    sweep_rows(nx, FW, -8, 2, coarse_rows)
    for n in range(seams):
        low = seam_is_low(n)
        src, dst = pick(low, FW, FW + nx - SEAM), pick(low, FW, 0)

        def keep(i, _):
            x, to = pl.ds(src + 4 * i, 4), pl.ds(dst + 4 * i, 4)
            for j in range(3):
                seam[n, j, to] = permuted(ue, j, x)
            for j, b in enumerate((f0, q0, qa, qb, p2, w1, w2)):
                seam[n, 3 + j, to] = b[x]
            return 0

        lax.fori_loop(0, SEAM // 4, keep, 0)


def seam_kernel(keys, ckeys, local, seams, steps, table, *rest):
    nmsg = len(keys)
    msgs, rest = rest[:nmsg], rest[nmsg + 4 :]
    w1o, w2o, co, seam, tables = rest[:5]
    nc = len(ckeys)
    couts, rest = rest[5 : 5 + nc], rest[5 + nc :]
    halo, fine, plain, tmp, sems = rest
    nx, ny = w1o.shape[0], w1o.shape[1]
    ye = ny + 2 * YW
    h, a = times(steps, lax.axis_index("tm"))
    for i in range(3):
        for j in range(3):
            if (i, j) != (1, 1):
                tables[i, j] = jnp.zeros(tables.shape[2:], f32)
    if len(colors(lax.axis_size("gy"))) < 2 or len(colors(lax.axis_size("gx"))) < min(seams, 2):
        halo[...] = jnp.zeros(halo.shape, f32)
    pairs = []
    for (k, l), m in zip(keys, msgs):
        w = nx if k is None else FW
        if k is not None:
            n = 0 if seams == 1 else pick(upper("gx", k), 1, 0)
            pairs += [(m.at[pl.ds(j * w, w)], halo.at[n, j, :, target_y(l, ny), :]) for j in range(3)]
        sx = 1 if k is None else pick(upper("gx", k), 2, 0)
        sy = 1 if l is None else pick(upper("gy", l), 2, 0)
        pairs += table_copies(tables.at[sx, sy], m, 3 * w, False)
    pairs.append((table, tables.at[1, 1]))
    run_copies(pairs, sems)
    tx = local[0]
    for n in range(seams):
        low = seam_is_low(n)

        def write(i, k):
            inv = 1.0 / (1.0 + a * k * 6.0)
            fine[0, i] = k
            fine[1, i] = a * k * inv
            fine[2, i] = inv

        fill_coefficients(
            tables, local, TILE, pick(low, -(FW // TILE), tx - SEAM // TILE), fine.shape[1], tmp, write
        )
        to = pick(low, 0, SEAM)
        for i in range(0, FW, 4):
            for j in range(3):
                seam[n, j, pl.ds(to + i, 4)] = permuted(halo, n, j, pl.ds(i, 4))
        st = Stages(
            lambda j, at: seam[n, j, at], *[seam.at[n, 3 + j] for j in range(7)], fine, h, a, lambda x: lax.div(x, TILE)
        )
        for k, body in st.bodies():
            step = FEW if k == 1 else MANY
            masks = wide_masks(step, ye)
            first = pick(low, k, SEAM - k)
            lax.fori_loop(0, 8 // step, lambda i, _: (body(first + i * step, step, masks), 0)[1], 0)
        first = pick(low, FW, SEAM - 8)
        row = pick(low, 0, nx // 2 - 4)
        lax.fori_loop(
            0, 4, lambda i, _: (st.coarse_pair(first + 2 * i, row + i, w1o, w2o, co, plain, tmp, ny), 0)[1], 0
        )
    cx, cy = nx // 2, ny // 2
    fields = ((0, CW), (1, CN), (2, CN), (3, CW))
    for (k, l), o in zip(ckeys, couts):
        ys = pl.ds(0, cy) if l is None else pl.ds(pl.multiple_of(pick(upper("gy", l), cy - YW, 0), 8), YW)
        at = 0
        for fld, width in fields:
            if k is None:
                width, first = cx, 0
            else:
                first = pick(upper("gx", k), cx - width, 0)
            o[pl.ds(at, width)] = co[fld, pl.ds(first, width), ys, :]
            at += width


def assemble_kernel(keys, co, *rest):
    nm = len(keys)
    msgs, (gp, ce, ge), sems = rest[:nm], rest[nm : nm + 3], rest[nm + 3]
    cx, cy = co.shape[1], co.shape[2]

    def clear(i, _):
        for f in range(3):
            ge[f, i] = jnp.zeros(ge.shape[2:], f32)
        ce[i] = jnp.zeros(ge.shape[2:], f32)
        return 0

    lax.fori_loop(0, ce.shape[0], clear, 0)
    fields = ((0, CW), (1, CN), (2, CN), (3, CW))
    pairs = []

    def target(f):
        return ce if f == 3 else ge.at[f]

    for f, _ in fields:
        pairs.append((co.at[f], target(f).at[pl.ds(CW, cx), pl.ds(YW, cy), :]))
    for (k, l), m in zip(keys, msgs):
        ys = pl.ds(YW, cy) if l is None else pl.ds(pl.multiple_of(pick(upper("gy", l), YW + cy, 0), 8), YW)
        at = 0
        for f, width in fields:
            if k is None:
                width, first = cx, CW
            else:
                first = pick(upper("gx", k), CW + cx, CW - width)
            pairs.append((m.at[pl.ds(at, width)], target(f).at[pl.ds(first, width), ys, :]))
            at += width
    run_copies(pairs, sems)

    def order(i, _):
        at = pl.ds(2 * i, 2)
        for f in range(3):
            gp[f, at] = permuted(ge, f, at)
        return 0

    lax.fori_loop(0, ce.shape[0] // 2, order, 0)


def chain_kernel(turn, keys, arrive, steps, ge, coef, co, *rest):
    first = turn == 0
    if first:
        ce, rest = rest[0], rest[1:]
    else:
        _, own, rest = rest[0], rest[1], rest[2:]
        nm = len(arrive)
        msgs, rest = rest[:nm], rest[nm:]
        if turn == 1:
            rest = rest[1:]
    state = rest[0]
    rest = rest[1:]
    no = len(keys)
    whole, couts, rest = rest[0], rest[1 : 1 + no], rest[1 + no :]
    cin, q0, qa, qb, plain, sems = rest
    cx, cy = co.shape[1], co.shape[2]
    ye = cy + 2 * YW
    sect = lax.axis_index("tm")
    h, a = times(steps, sect)
    ngx, ngy = lax.axis_size("gx"), lax.axis_size("gy")

    @pl.when(sect == turn)
    def _():
        clear_walls(CW, cx, (q0, qa, qb))
        if first:
            c = ce
        else:
            c = cin
            if len(colors(ngy)) < 2:
                cin[...] = jnp.zeros(cin.shape, f32)
            else:
                clear_walls(CW, cx, (cin,))
            pairs = [(own, cin.at[pl.ds(CW, cx), pl.ds(YW, cy), :])]
            for (k, l), m in zip(arrive, msgs):
                if k is None:
                    xs = pl.ds(CW, cx)
                else:
                    xs = pl.ds(pick(upper("gx", k), CW + cx, 0), CW)
                ys = pl.ds(YW, cy) if l is None else pl.ds(pl.multiple_of(pick(upper("gy", l), YW + cy, 0), 8), YW)
                pairs.append((m, cin.at[xs, ys, :]))
            run_copies(pairs, sems)
        step = 4
        masks = wide_masks(step, ye)

        def rows(r, body):
            sweep_rows(cx, CW, r, step, body)

        def coefs(n, x):
            return jnp.stack([coef[n, lax.div(x + i, 2)] for i in range(step)])

        def jacobi(src, x):
            _, p, z = neighbours(src[pl.ds(x - 1, step + 2)], masks)
            return q0[pl.ds(x, step)] + coefs(0, x) * (0.25 * p + z)

        def into(dst, src):
            def body(x):
                dst[pl.ds(x, step)] = jacobi(src, x)
            return body

        def start(x):
            at = pl.ds(x, step)
            v = permuted(c, at)
            q0[at] = (v + a * reaction(v) + ge[0, at]) * coefs(1, x)

        rows(6, start)
        rows(5, into(qa, q0))
        rows(4, into(qb, qa))

        def middle(x):
            at = pl.ds(x, step)
            w = ge[1, at] + jacobi(qb, x)
            q0[at] = (w + a * reaction(w) + ge[2, at]) * coefs(1, x)
            store_plain(plain, (0, at), w)

        rows(3, middle)
        rows(2, into(qa, q0))
        rows(1, into(qb, qa))

        def end(x):
            store_plain(plain, (1, pl.ds(x, step)), jacobi(qb, x))

        rows(0, end)

        def keep(i, _):
            x, at = pl.ds(CW + 4 * i, 4), pl.ds(4 * i, 4)
            state[0, at] = c[x, YW : YW + cy]
            state[1, at] = plain[0, x, YW : YW + cy]
            state[2, at] = co[4, at] + plain[1, x, YW : YW + cy]
            whole[at] = state[2, at]
            return 0

        lax.fori_loop(0, cx // 4, keep, 0)
        for (k, l), o in zip(keys, couts):
            xs = pl.ds(0, cx) if k is None else pl.ds(pick(upper("gx", k), cx - CW, 0), CW)
            ys = pl.ds(0, cy) if l is None else pl.ds(pl.multiple_of(pick(upper("gy", l), cy - YW, 0), 8), YW)
            o[...] = state[2, xs, ys, :]


def finish_kernel(u0, arrived, w1, w2, state, co, out):
    sect = lax.axis_index("tm")
    ny = u0.shape[1]
    ft, ct = ny // 8, ny // 16

    def row(i, _):
        at = pl.ds(2 * i, 2)

        def fine_tile(ref, t):
            return ref[at, pl.ds(t, 8, stride=ft), :]

        def coarse_tile(ref, n, t):
            return ref[n, i, pl.ds(t, 8, stride=ct), :]

        for t in range(ct):
            base = [jnp.where(sect == 0, fine_tile(u0, 2 * t + d), fine_tile(arrived, 2 * t + d)) for d in range(2)]
            both = base[0] + base[1]
            d0 = coarse_tile(state, 0, t) - (both[0] + both[1]) * 0.25
            d1 = coarse_tile(state, 1, t) - coarse_tile(co, 1, t)
            d2 = coarse_tile(state, 2, t) - coarse_tile(co, 4, t)
            for d in range(2):
                to = pl.ds(2 * t + d, 8, stride=ft)
                out[0, at, to, :] = base[d] + d0
                out[1, at, to, :] = fine_tile(w1, 2 * t + d) + d1
                out[2, at, to, :] = fine_tile(w2, 2 * t + d) + d2
        return 0

    lax.fori_loop(0, u0.shape[0] // 2, row, 0)


def per_device(sizes, fine_nodes, section_steps, diffusivities, tile_kinds):
    nt, ngx, ngy = sizes
    u = fine_nodes[0]
    nodes, nx, ny, cz = u.shape
    cx, cy = nx // 2, ny // 2
    keys = message_keys(ngx, ngy)
    nk = len(keys)

    def dims(k, l, wx, lx, ly):
        return (lx if k is None else wx, ly if l is None else YW, cz)

    def send(some, arrays, hop):
        return [lax.ppermute(v, AXES, routes(sizes, k, l, hop)) for (k, l), v in zip(some, arrays)]

    def edge(v, l):
        first = jnp.where(upper("gy", l), v.shape[-2] - YW, 0)
        return lax.dynamic_slice_in_dim(v, first, YW, axis=v.ndim - 2)

    now = [(k, l) for k, l in keys if k is None or l != 0]
    after = [(k, l) for k, l in keys if k is not None and l == 0]
    straight = [(k, l) for k, l in now if l != 0]

    picks = tile_kinds[:, :, None] == jnp.arange(diffusivities.shape[0], dtype=jnp.int32)
    table = jnp.sum(jnp.where(picks, diffusivities, 0.0), axis=-1)
    local = table.shape
    table = jnp.pad(table, ((0, -local[0] % 8), (0, 128 - local[1])))
    tp = table.shape[0]

    def fine_dims(k, l):
        a, b, c = dims(k, l, FW, nx, ny)
        return shape(nodes * a + table_rows(b, tp), b, c)

    packed = pl.pallas_call(
        functools.partial(pack_kernel, keys),
        out_shape=[fine_dims(k, l) for k, l in keys],
        in_specs=[ANY, ANY],
        out_specs=[ANY] * nk,
        scratch_shapes=[pltpu.SemaphoreType.DMA((nk * (3 + tp),))],
        compiler_params=params(4),
        name="pack",
    )(u, table)
    halos = send(keys, packed, None)

    fye, cye, cxe = ny + 2 * YW, cy + 2 * YW, cx + 2 * CW + 4
    xe = nx + 2 * FW
    buf = pltpu.VMEM((xe, fye, cz), f32)
    depth = 2 * CW + 2 * CN
    seams = seam_count(ngx)
    ykeys = [key for key in keys if key[0] is None]
    yhalos = [m for key, m in zip(keys, halos) if key[0] is None]
    inner = pl.pallas_call(
        functools.partial(inner_kernel, ykeys, local, seams),
        out_shape=[
            shape(nx, ny, cz), shape(nx, ny, cz), shape(5, cx, cy, cz), shape(seams, FIELDS, FW + SEAM, fye, cz)
        ],
        in_specs=[SM, ANY, ANY] + [ANY] * len(ykeys),
        out_specs=[VM] * 4,
        scratch_shapes=[pltpu.VMEM((3, xe, fye, cz), f32)] + [buf] * 7
        + [
            pltpu.VMEM((3, xe // TILE, fye, cz), f32),
            pltpu.VMEM((3, 3, tp, cz), f32),
            pltpu.VMEM((5, fye // 2, cz), f32),
            pltpu.VMEM((4, fye, cz), f32),
            pltpu.SemaphoreType.DMA((nk * (3 + tp) + 2,)),
        ],
        compiler_params=params(38),
        cost_estimate=pl.CostEstimate(flops=200 * nx * ny * cz, bytes_accessed=40_000_000, transcendentals=0),
        name="fine_inner",
    )(section_steps, u, table, *yhalos)
    out = pl.pallas_call(
        functools.partial(seam_kernel, keys, now, local, seams),
        out_shape=[shape(*v.shape) for v in inner] + [shape(3, 3, tp, cz)]
        + [shape(*dims(k, l, depth, 4 * cx, cy)) for k, l in now],
        in_specs=[SM, ANY] + [ANY] * nk + [VM] * 4,
        out_specs=[VM] * (5 + len(now)),
        scratch_shapes=[
            pltpu.VMEM((seams, 3, FW, fye, cz), f32),
            pltpu.VMEM((3, (FW + SEAM) // TILE, fye, cz), f32),
            pltpu.VMEM((5, fye // 2, cz), f32),
            pltpu.VMEM((4, fye, cz), f32),
            pltpu.SemaphoreType.DMA((nk * (3 + tp) + 2,)),
        ],
        input_output_aliases={2 + nk + i: i for i in range(4)},
        compiler_params=params(24),
        name="fine_seam",
    )(section_steps, table, *halos, *inner)
    w1, w2, co, _, tables = out[:5]
    strips = dict(zip(now, lax.optimization_barrier(send(now, out[5:], None))))
    arrived = lax.ppermute(w2, "tm", [(i, i + 1) for i in range(nt - 1)])
    coef = pl.pallas_call(
        functools.partial(coarse_coefficient_kernel, local),
        out_shape=shape(2, cxe // 2, cye, cz),
        in_specs=[SM, VM],
        out_specs=VM,
        scratch_shapes=[pltpu.VMEM((4, cye, cz), f32)],
        compiler_params=params(4),
        name="coarse_coefficients",
    )(section_steps, tables)
    strips.update(zip(after, send([(None, l) for _, l in after], [edge(strips[(k, None)], l) for k, l in after], None)))

    ncopy = 4 + 4 * nk
    ge, ce = pl.pallas_call(
        functools.partial(assemble_kernel, keys),
        out_shape=[shape(3, cxe, cye, cz), shape(cxe, cye, cz)],
        in_specs=[ANY] + [ANY] * nk,
        out_specs=[VM, VM],
        scratch_shapes=[pltpu.VMEM((3, cxe, cye, cz), f32), pltpu.SemaphoreType.DMA((ncopy,))],
        compiler_params=params(10),
        name="assemble",
    )(co, *[strips[k] for k in keys])

    state, handed = None, None
    cbuf = pltpu.VMEM((cxe, cye, cz), f32)
    arrive = straight + [(None, 0)] * (0 in colors(ngy)) + after
    for n in range(nt):
        last = n == nt - 1
        args = [section_steps, ge, coef, co]
        specs = [SM, VM, VM, VM]
        alias = {}
        if n == 0:
            args.append(ce)
            specs.append(VM)
        else:
            alias = {len(args): 0}
            args += [state] + handed
            specs += [VM] + [ANY] * len(handed)
            if n == 1:
                args.append(arrived)
                specs.append(ANY)
        sent = [] if last else straight
        res = pl.pallas_call(
            functools.partial(chain_kernel, n, sent, arrive),
            out_shape=[shape(3, cx, cy, cz), shape(cx, cy, cz)] + [shape(*dims(k, l, CW, cx, cy)) for k, l in sent],
            in_specs=specs,
            out_specs=[VM] * (2 + len(sent)),
            scratch_shapes=[cbuf] * 4 + [pltpu.VMEM((2, cxe, cye, cz), f32), pltpu.SemaphoreType.DMA((nk + 1,))],
            input_output_aliases=alias,
            compiler_params=params(14),
            name=f"chain_{n}",
        )(*args)
        state = res[0]
        if not last:
            own = lax.ppermute(res[1], AXES, routes(sizes, None, None, n))
            own, *got = lax.optimization_barrier([own] + send(straight, res[2:], n))
            rows = [own] + [got[straight.index((k, None))] for k in colors(ngx)]
            side = []
            for l in colors(ngy)[:1]:
                strip = edge(jnp.concatenate(rows, axis=0), l)
                strip = lax.ppermute(strip, AXES, [p for p in routes(sizes, None, l, None) if p[1] // (ngx * ngy) == n + 1])
                side = [strip[:cx]] + [strip[cx + i * CW : cx + i * CW + CW] for i in range(len(after))]
            handed = [own] + got + side

    blk = 8
    fspec = pl.BlockSpec((blk, ny, cz), lambda i: (i, 0, 0))
    result = pl.pallas_call(
        finish_kernel,
        grid=(nx // blk,),
        out_shape=shape(3, nx, ny, cz),
        in_specs=[pl.BlockSpec((None, blk, ny, cz), lambda i: (0, i, 0, 0))] + [fspec] * 3
        + [pl.BlockSpec((3, blk // 2, cy, cz), lambda i: (0, i, 0, 0)), pl.BlockSpec((5, blk // 2, cy, cz), lambda i: (0, i, 0, 0))],
        out_specs=pl.BlockSpec((3, blk, ny, cz), lambda i: (0, i, 0, 0)),
        compiler_params=params(12),
        name="finish",
    )(u, arrived, w1, w2, state, co)
    return result[None]


def solution(mesh):
    sizes = tuple(mesh.shape[a] for a in AXES)
    return jax.shard_map(
        functools.partial(per_device, sizes),
        mesh=mesh,
        in_specs=(P("tm", None, "gx", "gy", None), P(), P(), P("gx", "gy")),
        out_specs=P("tm", None, "gx", "gy", None),
        check_vma=False,
    )
```

time: 188 us -> 128 us (0.68)
  Pallas kernels: 63.9 us -> 38 us
  waiting for transfers between devices: 70.1 us -> 55.5 us
  blocking collectives: 14.1 us -> 0 us
  starting transfers between devices: 32.9 us -> 29.6 us
  local copies, waits for them, and re-layouts: 5.22 us -> 2.83 us
    pallas_call x7 -> x8, Pallas kernels: 57.7 us -> 31.7 us  [the longest x1 16.4 us: per_device(): pl.pallas_call(functools.partial(inner_kernel, ykeys, local, seams), out_...]
    ppermute x25 -> x19, waiting for transfers between devices: 70.1 us -> 50.9 us  [send(): lax.ppermute(v, AXES, routes(sizes, k, l, hop))]
    all_gather x2 -> x0, blocking collectives: 14.1 us -> none  [the longest x1 8.78 us: per_device(): kinds = lax.all_gather(kinds, 'gx', axis=0, tiled=True)]
    ppermute x25 -> x19, starting transfers between devices: 28.9 us -> 22.4 us  [send(): lax.ppermute(v, AXES, routes(sizes, k, l, hop))]
    ppermute x1, waiting for transfers between devices: 0.01 us -> 3.29 us  [per_device(): arrived = lax.ppermute(w2, 'tm', [(i, i + 1) for i in range(nt - 1)])]
    ppermute x3 -> x6, starting transfers between devices: 2.65 us -> 5.9 us  [the longest x3 3.25 us: per_device(): lax.ppermute(strip, AXES, [p for p in routes(sizes, None, l, None) if p[1...]
  transfers between devices with their start and end apart: 29 -> 26, of which waited for: 5 -> 6; matrix products, arithmetic and copies ran while one was open for 1% -> 1% of each run, Pallas kernels for 10% -> 15%
where the time goes in v2:
time: 128 us; the launch traced here: 127 us
  waiting for transfers between devices  55.5 us (43%)
  Pallas kernels  38 us (30%)
  starting transfers between devices  29.6 us (23%)
  local copies, waits for them, and re-layouts  2.83 us (2%)
    ppermute x19, waiting for transfers between devices, send(): lax.ppermute(v, AXES, routes(sizes, k, l, hop))  50.9 us
    ppermute x19, starting transfers between devices, send(): lax.ppermute(v, AXES, routes(sizes, k, l, hop))  22.4 us
    pallas_call x1, Pallas kernels, per_device(): pl.pallas_call(functools.partial(inner_kernel, ykeys, local, seams), out_...  16.4 us
    pallas_call x4, Pallas kernels, per_device(): pl.pallas_call(functools.partial(chain_kernel, n, sent, arrive), out_shap...  7.41 us
    pallas_call x1, Pallas kernels, per_device(): pl.pallas_call(functools.partial(seam_kernel, keys, now, local, seams), o...  6.42 us
    pallas_call x1, Pallas kernels, per_device(): pl.pallas_call(finish_kernel, grid=(nx // blk,), out_shape=shape(3, nx, n...  4.26 us
    ppermute x1, waiting for transfers between devices, per_device(): arrived = lax.ppermute(w2, 'tm', [(i, i + 1) for i in range(nt - 1)])  3.29 us
    ppermute x3, starting transfers between devices, per_device(): lax.ppermute(strip, AXES, [p for p in routes(sizes, None, l, None) if p[1...  3.25 us
  transfers between devices with their start and end apart: 26, of which 6 were waited for; matrix products, arithmetic and copies ran while one was open for 1% of the time, Pallas kernels for 15%

profile of v2, /device:TPU:26, one launch (start us, length us, event | category | flops | bytes accessed | tf_op | source)
XLA Modules:
  0.0 127.3 jit_solution(889175563980583759)
XLA Ops:
  0.0 0.9 select_reduce_fusion
  0.9 1.9 %copy-done = f32[1,3,32,64,128]{4,3,2,1,0:T(8,128)S(1)} copy-done((f32[1,3,32,64,128]{4,3,2,1,0:T(8,128)S(1)}, f32[1,3,32,64,128]{4,3,2,1,0:T(8,128)}, u32[]{:S(2)}) %copy-start) | copy-done | bytes 3145752
  2.8 0.8 pack.1
  3.6 1.6 %collective-permute-start = (f32[25,64,128]{2,1,0:T(8,128)S(1)}, f32[25,64,128]{2,1,0:T(8,128)S(1)}, u32[]{:S(2)}, u32[]{:S(2)}) collective-permute-start(f32[25,64,128]{2,1,0:T(8,128)S(1)} %get-tuple-element.56), channel_id=1, source_target_pairs={{4,0},{5,1},{6,2},{7,3},{0,4},{1,5},{2,6},{3,7},{12,8},{13,9},{14,... | collective-permute-start | bytes 2457608 | tf_op jit(solution)/shard_map/ppermute | solution.py:624
  5.1 2.5 %collective-permute-start.4 = (f32[97,8,128]{2,1,0:T(8,128)S(1)}, f32[97,8,128]{2,1,0:T(8,128)S(1)}, u32[]{:S(2)}, u32[]{:S(2)}) collective-permute-start(f32[97,8,128]{2,1,0:T(8,128)S(1)} %get-tuple-element.60), channel_id=1, source_target_pairs={{2,1},{1,2},{6,5},{5,6},{10,9},{9,10},{14,13},{13,14},{18,17},{17,... | collective-permute-start | bytes 1191944 | tf_op jit(solution)/shard_map/ppermute | solution.py:624
  7.8 3.0 %collective-permute-start.2 = (f32[25,8,128]{2,1,0:T(8,128)S(1)}, f32[25,8,128]{2,1,0:T(8,128)S(1)}, u32[]{:S(2)}, u32[]{:S(2)}) collective-permute-start(f32[25,8,128]{2,1,0:T(8,128)S(1)} %get-tuple-element.58), channel_id=1, source_target_pairs={{6,1},{5,2},{2,5},{1,6},{14,9},{13,10},{10,13},{9,14},{22,17},{21,... | collective-permute-start | bytes 307208 | tf_op jit(solution)/shard_map/ppermute | solution.py:624
  10.7 3.5 %collective-permute-done.4.rest_1_.rest_4_ = f32[97,8,128]{2,1,0:T(8,128)S(1)} collective-permute-done((f32[97,8,128]{2,1,0:T(8,128)S(1)}, f32[97,8,128]{2,1,0:T(8,128)S(1)}, u32[]{:S(2)}, u32[]{:S(2)}) %collective-permute-start.4) | collective-permute-done | bytes 397344 | tf_op jit(solution)/shard_map/ppermute | solution.py:624
  14.3 16.4 %fine_inner.1 = (f32[32,64,128]{2,1,0:T(8,128)S(1)}, f32[32,64,128]{2,1,0:T(8,128)S(1)}, f32[5,16,32,128]{3,2,1,0:T(8,128)S(1)}, f32[1,10,20,80,128]{4,3,2,1,0:T(8,128)S(1)}) custom-call(s32[4]{0:T(128)S(1)} %copy-done.3, f32[3,32,64,128]{3,2,1,0:T(8,128)S(1)} %bitcast.3, f32[8,128]{1,0:T(8,128)S(1)} %pad.4.table, ...), custom_call_target="tpu_custom_call" | custom-call | flops 52428800 | bytes 40000000 | tf_op jit(solution)/shard_map/fine_inner/pallas_call | solution.py:662
  30.7 6.4 %fine_seam.1 = (f32[32,64,128]{2,1,0:T(8,128)S(1)}, f32[32,64,128]{2,1,0:T(8,128)S(1)}, f32[5,16,32,128]{3,2,1,0:T(8,128)S(1)}, f32[1,10,20,80,128]{4,3,2,1,0:T(...) custom-call(s32[4]{0:T(128)S(1)} %copy-done.3, ...), custom_call_target="tpu_custom_call", output_to_operand_aliasing={{0}: (7, {}), {1}: (8, {}), {2}: (9, {}), {3}: (10, {})} | custom-call | tf_op jit(solution)/shard_map/fine_seam/pallas_call | solution.py:681
  37.2 1.3 %collective-permute-start.5 = (f32[32,64,128]{2,1,0:T(8,128)S(1)}, f32[32,64,128]{2,1,0:T(8,128)}, u32[]{:S(2)}, u32[]{:S(2)}) collective-permute-start(f32[32,64,128]{2,1,0:T(8,128)S(1)} %get-tuple-element.65.w2), channel_id=1, source_target_pairs={{0,8},{8,16},{16,24},{1,9},{9,17},{17,25},{2,10},{10,18},{18,26},{... | collective-permute-start | bytes 3145736 | tf_op jit(solution)/shard_map/ppermute | solution.py:700
  39.1 2.6 %collective-permute-start.9 = (f32[64,8,128]{2,1,0:T(8,128)}, f32[64,8,128]{2,1,0:T(8,128)}, u32[]{:S(2)}, u32[]{:S(2)}) collective-permute-start(f32[64,8,128]{2,1,0:T(8,128)} %get-tuple-element.71), channel_id=1, source_target_pairs={{2,1},{1,2},{6,5},{5,6},{10,9},{9,10},{14,13},{13,14},{18,17},{17,... | collective-permute-start | bytes 786440 | tf_op jit(solution)/shard_map/ppermute | solution.py:624
  41.6 3.9 %collective-permute-start.7 = (f32[18,8,128]{2,1,0:T(8,128)}, f32[18,8,128]{2,1,0:T(8,128)S(1)}, u32[]{:S(2)}, u32[]{:S(2)}) collective-permute-start(f32[18,8,128]{2,1,0:T(8,128)} %get-tuple-element.69), channel_id=1, source_target_pairs={{6,1},{5,2},{2,5},{1,6},{14,9},{13,10},{10,13},{9,14},{22,17},{21,... | collective-permute-start | bytes 221192 | tf_op jit(solution)/shard_map/ppermute | solution.py:624
  45.6 3.1 %collective-permute-done.7.rest_2_ = f32[18,8,128]{2,1,0:T(8,128)S(1)} collective-permute-done((f32[18,8,128]{2,1,0:T(8,128)}, f32[18,8,128]{2,1,0:T(8,128)S(1)}, u32[]{:S(2)}, u32[]{:S(2)}) %collective-permute-start.7) | collective-permute-done | bytes 73760 | tf_op jit(solution)/shard_map/ppermute | solution.py:624
  48.7 0.9 constant_dynamic-slice_fusion
  49.6 0.7 coarse_coefficients.1.coef
  50.9 1.9 %assemble.1 = (f32[3,32,48,128]{3,2,1,0:T(8,128)S(1)}, f32[32,48,128]{2,1,0:T(8,128)S(1)}) custom-call(f32[5,16,32,128]{3,2,1,0:T(8,128)S(1)} %get-tuple-element.67.co, f32[18,32,128]{2,1,0:T(8,128)} %collective-permute-done.6.rest_0_, f32[18,8,128]{2,1,0:T(8,128)S(1)} %collective-permute-done.10.rest_1_, f32[18,8,128]{2,1,0:T(8,128)S(1)} %collective-permute-done.7.rest_2_, ...), custom_call_target="tpu_custom_call" | custom-call | tf_op jit(solution)/shard_map/assemble/pallas_call | solution.py:713
  53.4 0.7 collective-permute-start.11
  54.1 0.7 collective-permute-start.12
  56.2 0.7 collective-permute-start.15
  56.9 3.3 %collective-permute-done.5.rest_7_.arrived = f32[32,64,128]{2,1,0:T(8,128)} collective-permute-done((f32[32,64,128]{2,1,0:T(8,128)S(1)}, f32[32,64,128]{2,1,0:T(8,128)}, u32[]{:S(2)}, u32[]{:S(2)}) %collective-permute-start.5) | collective-permute-done | bytes 1048608 | tf_op jit(solution)/shard_map/ppermute | solution.py:700
  60.8 0.7 collective-permute-start.16
  61.5 0.7 collective-permute-start.17
  63.6 0.7 collective-permute-start.20
  64.9 1.3 %collective-permute-start.21 = (f32[16,32,128]{2,1,0:T(8,128)S(1)}, f32[16,32,128]{2,1,0:T(8,128)S(1)}, u32[]{:S(2)}, u32[]{:S(2)}) collective-permute-start(f32[16,32,128]{2,1,0:T(8,128)S(1)} %get-tuple-element.98), channel_id=1, source_target_pairs={{16,24},{17,25},{18,26},{19,27},{20,28},{21,29},{22,30},{23,31}} | collective-permute-start | bytes 786440 | tf_op jit(solution)/shard_map/ppermute | solution.py:754
  66.2 1.3 %collective-permute-start.22 = (f32[6,32,128]{2,1,0:T(8,128)S(1)}, f32[6,32,128]{2,1,0:T(8,128)S(1)}, u32[]{:S(2)}, u32[]{:S(2)}) collective-permute-start(f32[6,32,128]{2,1,0:T(8,128)S(1)} %get-tuple-element.99), channel_id=1, source_target_pairs={{20,24},{21,25},{22,26},{23,27},{16,28},{17,29},{18,30},{19,31}} | collective-permute-start | bytes 294920 | tf_op jit(solution)/shard_map/ppermute | solution.py:624
  67.5 1.3 %collective-permute-start.24 = (f32[16,8,128]{2,1,0:T(8,128)S(1)}, f32[16,8,128]{2,1,0:T(8,128)S(1)}, u32[]{:S(2)}, u32[]{:S(2)}) collective-permute-start(f32[16,8,128]{2,1,0:T(8,128)S(1)} %get-tuple-element.101), channel_id=1, source_target_pairs={{18,25},{17,26},{22,29},{21,30}} | collective-permute-start | bytes 196616 | tf_op jit(solution)/shard_map/ppermute | solution.py:624
  68.8 1.6 %collective-permute-start.23 = (f32[6,8,128]{2,1,0:T(8,128)S(1)}, f32[6,8,128]{2,1,0:T(8,128)S(1)}, u32[]{:S(2)}, u32[]{:S(2)}) collective-permute-start(f32[6,8,128]{2,1,0:T(8,128)S(1)} %get-tuple-element.100), channel_id=1, source_target_pairs={{22,25},{21,26},{18,29},{17,30}} | collective-permute-start | bytes 73736 | tf_op jit(solution)/shard_map/ppermute | solution.py:624
  70.4 43.8 %collective-permute-done.23.rest_3_ = f32[6,8,128]{2,1,0:T(8,128)S(1)} collective-permute-done((f32[6,8,128]{2,1,0:T(8,128)S(1)}, f32[6,8,128]{2,1,0:T(8,128)S(1)}, u32[]{:S(2)}, u32[]{:S(2)}) %collective-permute-start.23) | collective-permute-done | bytes 24608 | tf_op jit(solution)/shard_map/ppermute | solution.py:624
  114.2 1.9 %collective-permute-start.25 = (f32[22,8,128]{2,1,0:T(8,128)S(1)}, f32[22,8,128]{2,1,0:T(8,128)S(1)}, u32[]{:S(2)}, u32[]{:S(2)}) collective-permute-start(f32[22,8,128]{2,1,0:T(8,128)S(1)} %fusion), channel_id=1, source_target_pairs={{25,24},{24,25},{27,26},{26,27},{29,28},{28,29},{31,30},{30,31}} | collective-permute-start | bytes 270344 | tf_op jit(solution)/shard_map/ppermute | solution.py:760
  116.1 1.3 collective-permute-done.25
  117.4 5.6 %chain_3.1 = (f32[3,16,32,128]{3,2,1,0:T(8,128)S(1)}, f32[16,32,128]{2,1,0:T(8,128)}) custom-call(s32[4]{0:T(128)S(1)} %copy-done.3, f32[3,32,48,128]{3,2,1,0:T(8,128)S(1)} %get-tuple-element.76.ge, f32[2,16,48,128]{3,2,1,0:T(8,128)S(1)} %coarse_coefficients.1.coef, f32[5,16,32,128]{3,2,1,0:T(8,128)S(1)} %get-tuple-element.67.co, ...), custom_call_target="tpu_custom_call", output_to_operand_aliasing={{0}: (4, {})} | custom-call | tf_op jit(solution)/shard_map/chain_3/pallas_call | solution.py:742
  123.0 4.3 %finish.1 = f32[3,32,64,128]{3,2,1,0:T(8,128)} custom-call(f32[3,32,64,128]{3,2,1,0:T(8,128)S(1)} %bitcast.4, f32[32,64,128]{2,1,0:T(8,128)} %collective-permute-done.5.rest_7_.arrived, f32[32,64,128]{2,1,0:T(8,128)S(1)} %get-tuple-element.66.w1, f32[32,64,128]{2,1,0:T(8,128)S(1)} %get-tuple-element.65.w2, f32[3,16,32,128]{3,2,1,0:T(8,128)S(1)} %get-tuple-element.106.state, ...), custom_call_target="tpu_custom_call" | custom-call | tf_op jit(solution)/shard_map/finish/pallas_call | solution.py:766
  (50 shorter events, 5.8 us)
Async XLA Ops:
  0.0 14.3 %copy-start.3 = (s32[4]{0:T(128)S(1)}, s32[4]{0:T(128)}, u32[]{:S(2)}) copy-start(s32[4]{0:T(128)} %steps.13) | copy-start | bytes 52
  0.9 1.9 %copy-start = (f32[1,3,32,64,128]{4,3,2,1,0:T(8,128)S(1)}, f32[1,3,32,64,128]{4,3,2,1,0:T(8,128)}, u32[]{:S(2)}) copy-start(f32[1,3,32,64,128]{4,3,2,1,0:T(8,128)} %param.4) | copy-start | bytes 9437188
  2.8 11.5 %copy-start.1 = (f32[1,3,32,64,128]{4,3,2,1,0:T(8,128)S(1)}, f32[1,3,32,64,128]{4,3,2,1,0:T(8,128)}, u32[]{:S(2)}) copy-start(f32[1,3,32,64,128]{4,3,2,1,0:T(8,128)} %param.4) | copy-start | bytes 9437188
  3.6 27.2 %collective-permute-start = (f32[25,64,128]{2,1,0:T(8,128)S(1)}, f32[25,64,128]{2,1,0:T(8,128)S(1)}, u32[]{:S(2)}, u32[]{:S(2)}) collective-permute-start(f32[25,64,128]{2,1,0:T(8,128)S(1)} %get-tuple-element.56), channel_id=1, source_target_pairs={{4,0},{5,1},{6,2},{7,3},{0,4},{1,5},{2,6},{3,7},{12,8},{13,9},{14,... | collective-permute-start | bytes 2457608 | tf_op jit(solution)/shard_map/ppermute | solution.py:624
  5.1 5.6 %collective-permute-start.3 = (f32[97,8,128]{2,1,0:T(8,128)S(1)}, f32[97,8,128]{2,1,0:T(8,128)S(1)}, u32[]{:S(2)}, u32[]{:S(2)}) collective-permute-start(f32[97,8,128]{2,1,0:T(8,128)S(1)} %get-tuple-element.59), channel_id=1, source_target_pairs={{1,0},{0,1},{3,2},{2,3},{5,4},{4,5},{7,6},{6,7},{9,8},{8,9},{11,10... | collective-permute-start | bytes 1191944 | tf_op jit(solution)/shard_map/ppermute | solution.py:624
  5.1 9.1 %collective-permute-start.4 = (f32[97,8,128]{2,1,0:T(8,128)S(1)}, f32[97,8,128]{2,1,0:T(8,128)S(1)}, u32[]{:S(2)}, u32[]{:S(2)}) collective-permute-start(f32[97,8,128]{2,1,0:T(8,128)S(1)} %get-tuple-element.60), channel_id=1, source_target_pairs={{2,1},{1,2},{6,5},{5,6},{10,9},{9,10},{14,13},{13,14},{18,17},{17,... | collective-permute-start | bytes 1191944 | tf_op jit(solution)/shard_map/ppermute | solution.py:624
  7.7 23.0 %collective-permute-start.1 = (f32[25,8,128]{2,1,0:T(8,128)S(1)}, f32[25,8,128]{2,1,0:T(8,128)S(1)}, u32[]{:S(2)}, u32[]{:S(2)}) collective-permute-start(f32[25,8,128]{2,1,0:T(8,128)S(1)} %get-tuple-element.57), channel_id=1, source_target_pairs={{5,0},{4,1},{7,2},{6,3},{1,4},{0,5},{3,6},{2,7},{13,8},{12,9},{15,... | collective-permute-start | bytes 307208 | tf_op jit(solution)/shard_map/ppermute | solution.py:624
  7.8 22.9 %collective-permute-start.2 = (f32[25,8,128]{2,1,0:T(8,128)S(1)}, f32[25,8,128]{2,1,0:T(8,128)S(1)}, u32[]{:S(2)}, u32[]{:S(2)}) collective-permute-start(f32[25,8,128]{2,1,0:T(8,128)S(1)} %get-tuple-element.58), channel_id=1, source_target_pairs={{6,1},{5,2},{2,5},{1,6},{14,9},{13,10},{10,13},{9,14},{22,17},{21,... | collective-permute-start | bytes 307208 | tf_op jit(solution)/shard_map/ppermute | solution.py:624
  37.2 23.0 %collective-permute-start.5 = (f32[32,64,128]{2,1,0:T(8,128)S(1)}, f32[32,64,128]{2,1,0:T(8,128)}, u32[]{:S(2)}, u32[]{:S(2)}) collective-permute-start(f32[32,64,128]{2,1,0:T(8,128)S(1)} %get-tuple-element.65.w2), channel_id=1, source_target_pairs={{0,8},{8,16},{16,24},{1,9},{9,17},{17,25},{2,10},{10,18},{18,26},{... | collective-permute-start | bytes 3145736 | tf_op jit(solution)/shard_map/ppermute | solution.py:700
  38.5 10.2 %collective-permute-start.6 = (f32[18,32,128]{2,1,0:T(8,128)}, f32[18,32,128]{2,1,0:T(8,128)}, u32[]{:S(2)}, u32[]{:S(2)}) collective-permute-start(f32[18,32,128]{2,1,0:T(8,128)} %get-tuple-element.68), channel_id=1, source_target_pairs={{4,0},{5,1},{6,2},{7,3},{0,4},{1,5},{2,6},{3,7},{12,8},{13,9},{14,... | collective-permute-start | bytes 884744 | tf_op jit(solution)/shard_map/ppermute | solution.py:624
  39.0 9.6 %collective-permute-start.8 = (f32[64,8,128]{2,1,0:T(8,128)}, f32[64,8,128]{2,1,0:T(8,128)}, u32[]{:S(2)}, u32[]{:S(2)}) collective-permute-start(f32[64,8,128]{2,1,0:T(8,128)} %get-tuple-element.70), channel_id=1, source_target_pairs={{1,0},{0,1},{3,2},{2,3},{5,4},{4,5},{7,6},{6,7},{9,8},{8,9},{11,10... | collective-permute-start | bytes 786440 | tf_op jit(solution)/shard_map/ppermute | solution.py:624
  39.1 9.6 %collective-permute-start.9 = (f32[64,8,128]{2,1,0:T(8,128)}, f32[64,8,128]{2,1,0:T(8,128)}, u32[]{:S(2)}, u32[]{:S(2)}) collective-permute-start(f32[64,8,128]{2,1,0:T(8,128)} %get-tuple-element.71), channel_id=1, source_target_pairs={{2,1},{1,2},{6,5},{5,6},{10,9},{9,10},{14,13},{13,14},{18,17},{17,... | collective-permute-start | bytes 786440 | tf_op jit(solution)/shard_map/ppermute | solution.py:624
  41.6 7.1 %collective-permute-start.7 = (f32[18,8,128]{2,1,0:T(8,128)}, f32[18,8,128]{2,1,0:T(8,128)S(1)}, u32[]{:S(2)}, u32[]{:S(2)}) collective-permute-start(f32[18,8,128]{2,1,0:T(8,128)} %get-tuple-element.69), channel_id=1, source_target_pairs={{6,1},{5,2},{2,5},{1,6},{14,9},{13,10},{10,13},{9,14},{22,17},{21,... | collective-permute-start | bytes 221192 | tf_op jit(solution)/shard_map/ppermute | solution.py:624
  49.6 1.3 collective-permute-start.10
  53.4 2.7 %collective-permute-start.11 = (f32[16,32,128]{2,1,0:T(8,128)S(1)}, f32[16,32,128]{2,1,0:T(8,128)S(1)}, u32[]{:S(2)}, u32[]{:S(2)}) collective-permute-start(f32[16,32,128]{2,1,0:T(8,128)S(1)} %get-tuple-element.80), channel_id=1, source_target_pairs={{0,8},{1,9},{2,10},{3,11},{4,12},{5,13},{6,14},{7,15}} | collective-permute-start | bytes 786440 | tf_op jit(solution)/shard_map/ppermute | solution.py:754
  54.1 2.0 %collective-permute-start.12 = (f32[6,32,128]{2,1,0:T(8,128)S(1)}, f32[6,32,128]{2,1,0:T(8,128)S(1)}, u32[]{:S(2)}, u32[]{:S(2)}) collective-permute-start(f32[6,32,128]{2,1,0:T(8,128)S(1)} %get-tuple-element.81), channel_id=1, source_target_pairs={{4,8},{5,9},{6,10},{7,11},{0,12},{1,13},{2,14},{3,15}} | collective-permute-start | bytes 294920 | tf_op jit(solution)/shard_map/ppermute | solution.py:624
  54.8 1.4 %collective-permute-start.14 = (f32[16,8,128]{2,1,0:T(8,128)S(1)}, f32[16,8,128]{2,1,0:T(8,128)S(1)}, u32[]{:S(2)}, u32[]{:S(2)}) collective-permute-start(f32[16,8,128]{2,1,0:T(8,128)S(1)} %get-tuple-element.83), channel_id=1, source_target_pairs={{2,9},{1,10},{6,13},{5,14}} | collective-permute-start | bytes 196616 | tf_op jit(solution)/shard_map/ppermute | solution.py:624
  55.5 0.7 collective-permute-start.13
  56.2 0.7 collective-permute-start.15
  60.8 2.7 %collective-permute-start.16 = (f32[16,32,128]{2,1,0:T(8,128)S(1)}, f32[16,32,128]{2,1,0:T(8,128)S(1)}, u32[]{:S(2)}, u32[]{:S(2)}) collective-permute-start(f32[16,32,128]{2,1,0:T(8,128)S(1)} %get-tuple-element.89), channel_id=1, source_target_pairs={{8,16},{9,17},{10,18},{11,19},{12,20},{13,21},{14,22},{15,23}} | collective-permute-start | bytes 786440 | tf_op jit(solution)/shard_map/ppermute | solution.py:754
  61.5 2.0 %collective-permute-start.17 = (f32[6,32,128]{2,1,0:T(8,128)S(1)}, f32[6,32,128]{2,1,0:T(8,128)S(1)}, u32[]{:S(2)}, u32[]{:S(2)}) collective-permute-start(f32[6,32,128]{2,1,0:T(8,128)S(1)} %get-tuple-element.90), channel_id=1, source_target_pairs={{12,16},{13,17},{14,18},{15,19},{8,20},{9,21},{10,22},{11,23}} | collective-permute-start | bytes 294920 | tf_op jit(solution)/shard_map/ppermute | solution.py:624
  62.2 1.4 %collective-permute-start.19 = (f32[16,8,128]{2,1,0:T(8,128)S(1)}, f32[16,8,128]{2,1,0:T(8,128)S(1)}, u32[]{:S(2)}, u32[]{:S(2)}) collective-permute-start(f32[16,8,128]{2,1,0:T(8,128)S(1)} %get-tuple-element.92), channel_id=1, source_target_pairs={{10,17},{9,18},{14,21},{13,22}} | collective-permute-start | bytes 196616 | tf_op jit(solution)/shard_map/ppermute | solution.py:624
  62.9 0.7 collective-permute-start.18
  63.6 0.7 collective-permute-start.20
  64.9 49.2 %collective-permute-start.21 = (f32[16,32,128]{2,1,0:T(8,128)S(1)}, f32[16,32,128]{2,1,0:T(8,128)S(1)}, u32[]{:S(2)}, u32[]{:S(2)}) collective-permute-start(f32[16,32,128]{2,1,0:T(8,128)S(1)} %get-tuple-element.98), channel_id=1, source_target_pairs={{16,24},{17,25},{18,26},{19,27},{20,28},{21,29},{22,30},{23,31}} | collective-permute-start | bytes 786440 | tf_op jit(solution)/shard_map/ppermute | solution.py:754
  66.2 47.9 %collective-permute-start.22 = (f32[6,32,128]{2,1,0:T(8,128)S(1)}, f32[6,32,128]{2,1,0:T(8,128)S(1)}, u32[]{:S(2)}, u32[]{:S(2)}) collective-permute-start(f32[6,32,128]{2,1,0:T(8,128)S(1)} %get-tuple-element.99), channel_id=1, source_target_pairs={{20,24},{21,25},{22,26},{23,27},{16,28},{17,29},{18,30},{19,31}} | collective-permute-start | bytes 294920 | tf_op jit(solution)/shard_map/ppermute | solution.py:624
  67.5 46.6 %collective-permute-start.24 = (f32[16,8,128]{2,1,0:T(8,128)S(1)}, f32[16,8,128]{2,1,0:T(8,128)S(1)}, u32[]{:S(2)}, u32[]{:S(2)}) collective-permute-start(f32[16,8,128]{2,1,0:T(8,128)S(1)} %get-tuple-element.101), channel_id=1, source_target_pairs={{18,25},{17,26},{22,29},{21,30}} | collective-permute-start | bytes 196616 | tf_op jit(solution)/shard_map/ppermute | solution.py:624
  68.8 54.2 %copy-start.2 = (f32[1,3,32,64,128]{4,3,2,1,0:T(8,128)S(1)}, f32[1,3,32,64,128]{4,3,2,1,0:T(8,128)}, u32[]{:S(2)}) copy-start(f32[1,3,32,64,128]{4,3,2,1,0:T(8,128)} %param.4) | copy-start | bytes 9437188
  68.8 45.3 %collective-permute-start.23 = (f32[6,8,128]{2,1,0:T(8,128)S(1)}, f32[6,8,128]{2,1,0:T(8,128)S(1)}, u32[]{:S(2)}, u32[]{:S(2)}) collective-permute-start(f32[6,8,128]{2,1,0:T(8,128)S(1)} %get-tuple-element.100), channel_id=1, source_target_pairs={{22,25},{21,26},{18,29},{17,30}} | collective-permute-start | bytes 73736 | tf_op jit(solution)/shard_map/ppermute | solution.py:624
  114.2 3.2 %collective-permute-start.25 = (f32[22,8,128]{2,1,0:T(8,128)S(1)}, f32[22,8,128]{2,1,0:T(8,128)S(1)}, u32[]{:S(2)}, u32[]{:S(2)}) collective-permute-start(f32[22,8,128]{2,1,0:T(8,128)S(1)} %fusion), channel_id=1, source_target_pairs={{25,24},{24,25},{27,26},{26,27},{29,28},{28,29},{31,30},{30,31}} | collective-permute-start | bytes 270344 | tf_op jit(solution)/shard_map/ppermute | solution.py:760

commit v3 on v2

--- a/solution.py
+++ b/solution.py
@@ -10,7 +10,8 @@
 FW = 8
 CW = 6
 CN = 3
-FEW, MANY = 2, 4
+SUB = 1
+FEW, MANY, LOW = 8, 8, 6
 YW = 8
 STEP_UNIT = 0.05
 WEIGHTS = ((5.0 / 24.0, 1.0 / 3.0, -1.0 / 24.0), (-1.0 / 24.0, 1.0 / 3.0, 5.0 / 24.0))
@@ -195,7 +196,7 @@
     lax.fori_loop(0, (n + pad) // step, lambda i, _: (body(begin + i * step), 0)[1], 0)
 
 
-def clear_walls(width, own, bufs, count=4):
+def clear_walls(width, own, bufs, count=CW):
     gx, ngx = lax.axis_index("gx"), lax.axis_size("gx")
     for b in bufs:
         zero = jnp.zeros((count,) + b.shape[1:], f32)
@@ -287,10 +288,16 @@
             out[pl.ds(2 * i, 2)] = tmp[2 * m : 2 * m + 2, YW : YW + ny]
         c0, c1 = [pair_sum(wt[0] * g[0] + wt[1] * g[1] + wt[2] * g[2]) * 0.25 for wt in WEIGHTS]
         u0, u1, u2 = [pair_sum(v) * 0.25 for v in w]
-        values = (h * c0 - a * reaction(u0) - u1, u1, h * c1 - a * reaction(u1) - u2, u0, u2)
+        start = jnp.where(lax.axis_index("tm") == 0, u0 + a * reaction(u0), 0.0)
+        values = (start + h * c0 - a * reaction(u0) - u1, u1, h * c1 - a * reaction(u1) - u2, u0, u2)
         for n, v in enumerate(values):
             store_plain(plain, (n,), v)
             co[n, i] = plain[n, YW // 2 : YW // 2 + ny // 2]
+
+
+def parts(body, step, masks, x):
+    for i in range(0, step, SUB):
+        body(x + i, SUB, masks)
 
 
 def seam_count(size):
@@ -320,7 +327,7 @@
                 ue[j, i] = jnp.zeros((ye, 128), f32)
             return 0
         lax.fori_loop(0, ue.shape[1], clear, 0)
-    clear_walls(FW, nx, [ue.at[0], ue.at[1], ue.at[2], q0, qa, qb, p2, w1, w2])
+    clear_walls(FW, nx, [ue.at[0], ue.at[1], ue.at[2], q0, qa, qb, p2, w1, w2], FW)
     for j in (0, 2):
         tables[1, j] = jnp.zeros(tables.shape[2:], f32)
     pairs = [(u, ue.at[:, pl.ds(FW, nx), pl.ds(YW, ny), :])]
@@ -347,8 +354,7 @@
         step = FEW if k == 1 else MANY
         if seams == 2 and (nx - 2 * k) % step:
             step = 2
-        masks = wide_masks(step, ye)
-        sweep_rows(nx, FW, -k, step, functools.partial(lambda body, step, masks, x: body(x, step, masks), body, step, masks))
+        sweep_rows(nx, FW, -k, step, functools.partial(parts, body, step, wide_masks(SUB, ye)))
 
     def coarse_rows(x):
         st.coarse_pair(x, lax.div(x - FW, 2), w1o, w2o, co, plain, tmp, ny)
@@ -418,16 +424,16 @@
         )
         for k, body in st.bodies():
             step = FEW if k == 1 else MANY
-            masks = wide_masks(step, ye)
+            masks = wide_masks(SUB, ye)
             first = pick(low, k, SEAM - k)
-            lax.fori_loop(0, 8 // step, lambda i, _: (body(first + i * step, step, masks), 0)[1], 0)
+            lax.fori_loop(0, 8 // step, lambda i, _: (parts(body, step, masks, first + i * step), 0)[1], 0)
         first = pick(low, FW, SEAM - 8)
         row = pick(low, 0, nx // 2 - 4)
         lax.fori_loop(
             0, 4, lambda i, _: (st.coarse_pair(first + 2 * i, row + i, w1o, w2o, co, plain, tmp, ny), 0)[1], 0
         )
     cx, cy = nx // 2, ny // 2
-    fields = ((0, CW), (1, CN), (2, CN), (3, CW))
+    fields = ((0, CW), (1, CN), (2, CN))
     for (k, l), o in zip(ckeys, couts):
         ys = pl.ds(0, cy) if l is None else pl.ds(pl.multiple_of(pick(upper("gy", l), cy - YW, 0), 8), YW)
         at = 0
@@ -442,24 +448,20 @@
 
 def assemble_kernel(keys, co, *rest):
     nm = len(keys)
-    msgs, (gp, ce, ge), sems = rest[:nm], rest[nm : nm + 3], rest[nm + 3]
+    msgs, (gp, ge), sems = rest[:nm], rest[nm : nm + 2], rest[nm + 2]
     cx, cy = co.shape[1], co.shape[2]
 
     def clear(i, _):
         for f in range(3):
             ge[f, i] = jnp.zeros(ge.shape[2:], f32)
-        ce[i] = jnp.zeros(ge.shape[2:], f32)
         return 0
 
-    lax.fori_loop(0, ce.shape[0], clear, 0)
-    fields = ((0, CW), (1, CN), (2, CN), (3, CW))
+    lax.fori_loop(0, ge.shape[1], clear, 0)
+    fields = ((0, CW), (1, CN), (2, CN))
     pairs = []
 
-    def target(f):
-        return ce if f == 3 else ge.at[f]
-
     for f, _ in fields:
-        pairs.append((co.at[f], target(f).at[pl.ds(CW, cx), pl.ds(YW, cy), :]))
+        pairs.append((co.at[f], ge.at[f].at[pl.ds(CW, cx), pl.ds(YW, cy), :]))
     for (k, l), m in zip(keys, msgs):
         ys = pl.ds(YW, cy) if l is None else pl.ds(pl.multiple_of(pick(upper("gy", l), YW + cy, 0), 8), YW)
         at = 0
@@ -468,7 +470,7 @@
                 width, first = cx, CW
             else:
                 first = pick(upper("gx", k), CW + cx, CW - width)
-            pairs.append((m.at[pl.ds(at, width)], target(f).at[pl.ds(first, width), ys, :]))
+            pairs.append((m.at[pl.ds(at, width)], ge.at[f].at[pl.ds(first, width), ys, :]))
             at += width
     run_copies(pairs, sems)
 
@@ -478,23 +480,26 @@
             gp[f, at] = permuted(ge, f, at)
         return 0
 
-    lax.fori_loop(0, ce.shape[0] // 2, order, 0)
-
-
-def chain_kernel(turn, keys, arrive, steps, ge, coef, co, *rest):
+    lax.fori_loop(0, ge.shape[1] // 2, order, 0)
+
+
+def chain_kernel(turn, keys, arrive, last, steps, ge, coef, co, *rest):
     first = turn == 0
-    if first:
-        ce, rest = rest[0], rest[1:]
-    else:
+    if not first:
         _, own, rest = rest[0], rest[1], rest[2:]
         nm = len(arrive)
         msgs, rest = rest[:nm], rest[nm:]
         if turn == 1:
             rest = rest[1:]
+        if last:
+            ready, rest = rest[0], rest[1:]
     state = rest[0]
     rest = rest[1:]
     no = len(keys)
     whole, couts, rest = rest[0], rest[1 : 1 + no], rest[1 + no :]
+    if last:
+        final, stage, finals = rest[0], rest[-2], rest[-1]
+        rest = rest[1:-2]
     cin, q0, qa, qb, plain, sems = rest
     cx, cy = co.shape[1], co.shape[2]
     ye = cy + 2 * YW
@@ -505,10 +510,7 @@
     @pl.when(sect == turn)
     def _():
         clear_walls(CW, cx, (q0, qa, qb))
-        if first:
-            c = ce
-        else:
-            c = cin
+        if not first:
             if len(colors(ngy)) < 2:
                 cin[...] = jnp.zeros(cin.shape, f32)
             else:
@@ -522,11 +524,11 @@
                 ys = pl.ds(YW, cy) if l is None else pl.ds(pl.multiple_of(pick(upper("gy", l), YW + cy, 0), 8), YW)
                 pairs.append((m, cin.at[xs, ys, :]))
             run_copies(pairs, sems)
-        step = 4
+        step = 1
         masks = wide_masks(step, ye)
 
         def rows(r, body):
-            sweep_rows(cx, CW, r, step, body)
+            sweep_rows(cx, CW, r, LOW, lambda x: [body(x + i) for i in range(0, LOW, step)])
 
         def coefs(n, x):
             return jnp.stack([coef[n, lax.div(x + i, 2)] for i in range(step)])
@@ -542,8 +544,11 @@
 
         def start(x):
             at = pl.ds(x, step)
-            v = permuted(c, at)
-            q0[at] = (v + a * reaction(v) + ge[0, at]) * coefs(1, x)
+            r = ge[0, at]
+            if not first:
+                v = permuted(cin, at)
+                r = v + a * reaction(v) + r
+            q0[at] = r * coefs(1, x)
 
         rows(6, start)
         rows(5, into(qa, q0))
@@ -566,7 +571,7 @@
 
         def keep(i, _):
             x, at = pl.ds(CW + 4 * i, 4), pl.ds(4 * i, 4)
-            state[0, at] = c[x, YW : YW + cy]
+            state[0, at] = co[3, at] if first else cin[x, YW : YW + cy]
             state[1, at] = plain[0, x, YW : YW + cy]
             state[2, at] = co[4, at] + plain[1, x, YW : YW + cy]
             whole[at] = state[2, at]
@@ -578,8 +583,15 @@
             ys = pl.ds(0, cy) if l is None else pl.ds(pl.multiple_of(pick(upper("gy", l), cy - YW, 0), 8), YW)
             o[...] = state[2, xs, ys, :]
 
-
-def finish_kernel(u0, arrived, w1, w2, state, co, out):
+    if last:
+        correct(ready, state, final, stage, finals)
+
+
+PIECES = 4
+
+
+def prepare_kernel(u, arrived, early, w1, w2, co, _, ready, u0, sems):
+    run_copies([(u.at[0], u0)], sems)
     sect = lax.axis_index("tm")
     ny = u0.shape[1]
     ft, ct = ny // 8, ny // 16
@@ -590,23 +602,46 @@
         def fine_tile(ref, t):
             return ref[at, pl.ds(t, 8, stride=ft), :]
 
-        def coarse_tile(ref, n, t):
-            return ref[n, i, pl.ds(t, 8, stride=ct), :]
-
         for t in range(ct):
-            base = [jnp.where(sect == 0, fine_tile(u0, 2 * t + d), fine_tile(arrived, 2 * t + d)) for d in range(2)]
+            base = []
+            for d in range(2):
+                came = jnp.where(sect == 1, fine_tile(early, 2 * t + d), fine_tile(arrived, 2 * t + d))
+                base.append(jnp.where(sect == 0, fine_tile(u0, 2 * t + d), came))
             both = base[0] + base[1]
-            d0 = coarse_tile(state, 0, t) - (both[0] + both[1]) * 0.25
-            d1 = coarse_tile(state, 1, t) - coarse_tile(co, 1, t)
-            d2 = coarse_tile(state, 2, t) - coarse_tile(co, 4, t)
+            less = ((both[0] + both[1]) * 0.25,) + tuple(co[n, i, pl.ds(t, 8, stride=ct), :] for n in (1, 4))
             for d in range(2):
                 to = pl.ds(2 * t + d, 8, stride=ft)
-                out[0, at, to, :] = base[d] + d0
-                out[1, at, to, :] = fine_tile(w1, 2 * t + d) + d1
-                out[2, at, to, :] = fine_tile(w2, 2 * t + d) + d2
+                ready[0, at, to, :] = base[d] - less[0]
+                ready[1, at, to, :] = fine_tile(w1, 2 * t + d) - less[1]
+                ready[2, at, to, :] = fine_tile(w2, 2 * t + d) - less[2]
         return 0
 
     lax.fori_loop(0, u0.shape[0] // 2, row, 0)
+
+
+def correct(ready, state, out, stage, sems):
+    nx, ny = ready.shape[1], ready.shape[2]
+    ft, ct = ny // 8, ny // 16
+    rows = nx // PIECES
+    copies = []
+    for m in range(3):
+        for p in range(PIECES):
+
+            def row(i, _):
+                at = pl.ds(2 * i, 2)
+                for t in range(ct):
+                    c = state[m, i, pl.ds(t, 8, stride=ct), :]
+                    for d in range(2):
+                        to = pl.ds(2 * t + d, 8, stride=ft)
+                        stage[m, at, to, :] = ready[m, at, to, :] + c
+                return 0
+
+            lax.fori_loop(p * rows // 2, (p + 1) * rows // 2, row, 0)
+            part = pl.ds(p * rows, rows)
+            copies.append(pltpu.make_async_copy(stage.at[m, part], out.at[m, part], sems.at[m * PIECES + p]))
+            copies[-1].start()
+    for c in copies:
+        c.wait()
 
 
 def per_device(sizes, fine_nodes, section_steps, diffusivities, tile_kinds):
@@ -655,7 +690,7 @@
     fye, cye, cxe = ny + 2 * YW, cy + 2 * YW, cx + 2 * CW + 4
     xe = nx + 2 * FW
     buf = pltpu.VMEM((xe, fye, cz), f32)
-    depth = 2 * CW + 2 * CN
+    depth = CW + 2 * CN
     seams = seam_count(ngx)
     ykeys = [key for key in keys if key[0] is None]
     yhalos = [m for key, m in zip(keys, halos) if key[0] is None]
@@ -681,7 +716,7 @@
     out = pl.pallas_call(
         functools.partial(seam_kernel, keys, now, local, seams),
         out_shape=[shape(*v.shape) for v in inner] + [shape(3, 3, tp, cz)]
-        + [shape(*dims(k, l, depth, 4 * cx, cy)) for k, l in now],
+        + [shape(*dims(k, l, depth, 3 * cx, cy)) for k, l in now],
         in_specs=[SM, ANY] + [ANY] * nk + [VM] * 4,
         out_specs=[VM] * (5 + len(now)),
         scratch_shapes=[
@@ -697,7 +732,7 @@
     )(section_steps, table, *halos, *inner)
     w1, w2, co, _, tables = out[:5]
     strips = dict(zip(now, lax.optimization_barrier(send(now, out[5:], None))))
-    arrived = lax.ppermute(w2, "tm", [(i, i + 1) for i in range(nt - 1)])
+    arrived = lax.ppermute(w2, "tm", [(i, i + 1) for i in range(1, nt - 1)])
     coef = pl.pallas_call(
         functools.partial(coarse_coefficient_kernel, local),
         out_shape=shape(2, cxe // 2, cye, cz),
@@ -709,12 +744,12 @@
     )(section_steps, tables)
     strips.update(zip(after, send([(None, l) for _, l in after], [edge(strips[(k, None)], l) for k, l in after], None)))
 
-    ncopy = 4 + 4 * nk
-    ge, ce = pl.pallas_call(
+    ncopy = 3 + 3 * nk
+    ge = pl.pallas_call(
         functools.partial(assemble_kernel, keys),
-        out_shape=[shape(3, cxe, cye, cz), shape(cxe, cye, cz)],
+        out_shape=shape(3, cxe, cye, cz),
         in_specs=[ANY] + [ANY] * nk,
-        out_specs=[VM, VM],
+        out_specs=VM,
         scratch_shapes=[pltpu.VMEM((3, cxe, cye, cz), f32), pltpu.SemaphoreType.DMA((ncopy,))],
         compiler_params=params(10),
         name="assemble",
@@ -728,10 +763,7 @@
         args = [section_steps, ge, coef, co]
         specs = [SM, VM, VM, VM]
         alias = {}
-        if n == 0:
-            args.append(ce)
-            specs.append(VM)
-        else:
+        if n > 0:
             alias = {len(args): 0}
             args += [state] + handed
             specs += [VM] + [ANY] * len(handed)
@@ -739,41 +771,56 @@
                 args.append(arrived)
                 specs.append(ANY)
         sent = [] if last else straight
+        outs = [shape(3, cx, cy, cz), shape(cx, cy, cz)] + [shape(*dims(k, l, CW, cx, cy)) for k, l in sent]
+        ospecs = [VM] * len(outs)
+        scratch = [cbuf] * 4 + [pltpu.VMEM((2, cxe, cye, cz), f32), pltpu.SemaphoreType.DMA((nk + 1,))]
+        if last:
+            args.append(ready)
+            specs.append(VM)
+            outs.append(shape(3, nx, ny, cz))
+            ospecs.append(ANY)
+            scratch += [pltpu.VMEM((3, nx, ny, cz), f32), pltpu.SemaphoreType.DMA((PIECES * 3,))]
         res = pl.pallas_call(
-            functools.partial(chain_kernel, n, sent, arrive),
-            out_shape=[shape(3, cx, cy, cz), shape(cx, cy, cz)] + [shape(*dims(k, l, CW, cx, cy)) for k, l in sent],
+            functools.partial(chain_kernel, n, sent, arrive if n else [], last),
+            out_shape=outs,
             in_specs=specs,
-            out_specs=[VM] * (2 + len(sent)),
-            scratch_shapes=[cbuf] * 4 + [pltpu.VMEM((2, cxe, cye, cz), f32), pltpu.SemaphoreType.DMA((nk + 1,))],
+            out_specs=ospecs,
+            scratch_shapes=scratch,
             input_output_aliases=alias,
-            compiler_params=params(14),
+            compiler_params=params(20 if last else 14),
             name=f"chain_{n}",
         )(*args)
         state = res[0]
         if not last:
-            own = lax.ppermute(res[1], AXES, routes(sizes, None, None, n))
-            own, *got = lax.optimization_barrier([own] + send(straight, res[2:], n))
+            whole = res[1]
+            own = lax.ppermute(whole, AXES, routes(sizes, None, None, n))
+            moving = [own] + send(straight, res[2:], n)
+            if n == nt - 2:
+                ready = pl.pallas_call(
+                    prepare_kernel,
+                    out_shape=shape(3, nx, ny, cz),
+                    in_specs=[ANY] + [VM] * 5 + [ANY],
+                    out_specs=VM,
+                    scratch_shapes=[pltpu.VMEM((nx, ny, cz), f32), pltpu.SemaphoreType.DMA((1,))],
+                    compiler_params=params(16),
+                    name="prepare",
+                )(u, arrived, early, w1, w2, co, whole)
+                moving.append(ready)
+            moving = lax.optimization_barrier(moving)
+            if n == min(1, nt - 2):
+                late, moving[0] = lax.optimization_barrier((w2, moving[0]))
+                early = lax.ppermute(late, "tm", [(0, 1)])
+            own, got = moving[0], moving[1 : 1 + len(straight)]
+            ready = moving[-1]
             rows = [own] + [got[straight.index((k, None))] for k in colors(ngx)]
             side = []
             for l in colors(ngy)[:1]:
                 strip = edge(jnp.concatenate(rows, axis=0), l)
-                strip = lax.ppermute(strip, AXES, [p for p in routes(sizes, None, l, None) if p[1] // (ngx * ngy) == n + 1])
+                pairs = [p for p in routes(sizes, None, l, None) if p[1] // (ngx * ngy) == n + 1]
+                strip = lax.ppermute(strip, AXES, pairs)
                 side = [strip[:cx]] + [strip[cx + i * CW : cx + i * CW + CW] for i in range(len(after))]
             handed = [own] + got + side
-
-    blk = 8
-    fspec = pl.BlockSpec((blk, ny, cz), lambda i: (i, 0, 0))
-    result = pl.pallas_call(
-        finish_kernel,
-        grid=(nx // blk,),
-        out_shape=shape(3, nx, ny, cz),
-        in_specs=[pl.BlockSpec((None, blk, ny, cz), lambda i: (0, i, 0, 0))] + [fspec] * 3
-        + [pl.BlockSpec((3, blk // 2, cy, cz), lambda i: (0, i, 0, 0)), pl.BlockSpec((5, blk // 2, cy, cz), lambda i: (0, i, 0, 0))],
-        out_specs=pl.BlockSpec((3, blk, ny, cz), lambda i: (0, i, 0, 0)),
-        compiler_params=params(12),
-        name="finish",
-    )(u, arrived, w1, w2, state, co)
-    return result[None]
+    return res[2][None]
 
 
 def solution(mesh):

time: 128 us -> 119 us (0.930)
  waiting for transfers between devices: 55.5 us -> 48.9 us
  Pallas kernels: 38 us -> 33.8 us
    ppermute x19, waiting for transfers between devices: 50.9 us -> 40.7 us  [send(): lax.ppermute(v, AXES, routes(sizes, k, l, hop))]
    ppermute x7 -> x8, waiting for transfers between devices: 4.56 us -> 8.18 us  [the longest x1 6.91 us: per_device(): arrived = lax.ppermute(w2, 'tm', [(i, i + 1) for i in range(1, nt - 1)])]
    pallas_call x1, Pallas kernels: 16.4 us -> 13.9 us  [per_device(): pl.pallas_call(functools.partial(inner_kernel, ykeys, local, seams), out_...]
    ppermute x7 -> x8, starting transfers between devices: 7.19 us -> 8.05 us  [the longest x3 3.25 us: per_device(): strip = lax.ppermute(strip, AXES, pairs)]
  transfers between devices with their start and end apart: 26 -> 27, of which waited for: 6 -> 6; matrix products, arithmetic and copies ran while one was open for 1% -> 1% of each run, Pallas kernels for 15% -> 17%
where the time goes in v3:
time: 119 us; the launch traced here: 117 us
  waiting for transfers between devices  48.9 us (41%)
  Pallas kernels  33.8 us (28%)
  starting transfers between devices  30.3 us (25%)
  local copies, waits for them, and re-layouts  2.74 us (2%)
    ppermute x19, waiting for transfers between devices, send(): lax.ppermute(v, AXES, routes(sizes, k, l, hop))  40.7 us
    ppermute x19, starting transfers between devices, send(): lax.ppermute(v, AXES, routes(sizes, k, l, hop))  22.2 us
    pallas_call x1, Pallas kernels, per_device(): pl.pallas_call(functools.partial(inner_kernel, ykeys, local, seams), out_...  13.9 us
    pallas_call x4, Pallas kernels, per_device(): pl.pallas_call(functools.partial(chain_kernel, n, sent, arrive if n else...  8.61 us
    ppermute x1, waiting for transfers between devices, per_device(): arrived = lax.ppermute(w2, 'tm', [(i, i + 1) for i in range(1, nt - 1)])  6.91 us
    pallas_call x1, Pallas kernels, per_device(): pl.pallas_call(functools.partial(seam_kernel, keys, now, local, seams), o...  5.48 us
    ppermute x3, starting transfers between devices, per_device(): strip = lax.ppermute(strip, AXES, pairs)  3.25 us
    ppermute x3, starting transfers between devices, per_device(): own = lax.ppermute(whole, AXES, routes(sizes, None, None, n))  2.65 us
  transfers between devices with their start and end apart: 27, of which 6 were waited for; matrix products, arithmetic and copies ran while one was open for 1% of the time, Pallas kernels for 17%

profile of v3, /device:TPU:26, one launch (start us, length us, event | category | flops | bytes accessed | tf_op | source)
XLA Modules:
  0.0 117.1 jit_solution(6859691559426140871)
XLA Ops:
  0.0 0.9 select_reduce_fusion
  0.9 1.9 %copy-done = f32[1,3,32,64,128]{4,3,2,1,0:T(8,128)S(1)} copy-done((f32[1,3,32,64,128]{4,3,2,1,0:T(8,128)S(1)}, f32[1,3,32,64,128]{4,3,2,1,0:T(8,128)}, u32[]{:S(2)}) %copy-start) | copy-done | bytes 3145752
  2.8 0.8 pack.1
  3.6 1.6 %collective-permute-start = (f32[25,64,128]{2,1,0:T(8,128)S(1)}, f32[25,64,128]{2,1,0:T(8,128)S(1)}, u32[]{:S(2)}, u32[]{:S(2)}) collective-permute-start(f32[25,64,128]{2,1,0:T(8,128)S(1)} %get-tuple-element.57), channel_id=1, source_target_pairs={{4,0},{5,1},{6,2},{7,3},{0,4},{1,5},{2,6},{3,7},{12,8},{13,9},{14,... | collective-permute-start | bytes 2457608 | tf_op jit(solution)/shard_map/ppermute | solution.py:659
  5.1 2.5 %collective-permute-start.4 = (f32[97,8,128]{2,1,0:T(8,128)S(1)}, f32[97,8,128]{2,1,0:T(8,128)S(1)}, u32[]{:S(2)}, u32[]{:S(2)}) collective-permute-start(f32[97,8,128]{2,1,0:T(8,128)S(1)} %get-tuple-element.61), channel_id=1, source_target_pairs={{2,1},{1,2},{6,5},{5,6},{10,9},{9,10},{14,13},{13,14},{18,17},{17,... | collective-permute-start | bytes 1191944 | tf_op jit(solution)/shard_map/ppermute | solution.py:659
  7.8 3.0 %collective-permute-start.2 = (f32[25,8,128]{2,1,0:T(8,128)S(1)}, f32[25,8,128]{2,1,0:T(8,128)S(1)}, u32[]{:S(2)}, u32[]{:S(2)}) collective-permute-start(f32[25,8,128]{2,1,0:T(8,128)S(1)} %get-tuple-element.59), channel_id=1, source_target_pairs={{6,1},{5,2},{2,5},{1,6},{14,9},{13,10},{10,13},{9,14},{22,17},{21,... | collective-permute-start | bytes 307208 | tf_op jit(solution)/shard_map/ppermute | solution.py:659
  10.7 3.5 %collective-permute-done.4.rest_1_.rest_4_ = f32[97,8,128]{2,1,0:T(8,128)S(1)} collective-permute-done((f32[97,8,128]{2,1,0:T(8,128)S(1)}, f32[97,8,128]{2,1,0:T(8,128)S(1)}, u32[]{:S(2)}, u32[]{:S(2)}) %collective-permute-start.4) | collective-permute-done | bytes 397344 | tf_op jit(solution)/shard_map/ppermute | solution.py:659
  14.3 13.9 %fine_inner.1 = (f32[32,64,128]{2,1,0:T(8,128)S(1)}, f32[32,64,128]{2,1,0:T(8,128)S(1)}, f32[5,16,32,128]{3,2,1,0:T(8,128)S(1)}, f32[1,10,20,80,128]{4,3,2,1,0:T(8,128)S(1)}) custom-call(s32[4]{0:T(128)S(1)} %copy-done.3, f32[3,32,64,128]{3,2,1,0:T(8,128)S(1)} %bitcast.3, f32[8,128]{1,0:T(8,128)S(1)} %pad.4.table, ...), custom_call_target="tpu_custom_call" | custom-call | flops 52428800 | bytes 40000000 | tf_op jit(solution)/shard_map/fine_inner/pallas_call | solution.py:697
  28.2 5.5 %fine_seam.1 = (f32[32,64,128]{2,1,0:T(8,128)S(1)}, f32[32,64,128]{2,1,0:T(8,128)S(1)}, f32[5,16,32,128]{3,2,1,0:T(8,128)S(1)}, f32[1,10,20,80,128]{4,3,2,1,0:T(...) custom-call(s32[4]{0:T(128)S(1)} %copy-done.3, ...), custom_call_target="tpu_custom_call", output_to_operand_aliasing={{0}: (7, {}), {1}: (8, {}), {2}: (9, {}), {3}: (10, {})} | custom-call | tf_op jit(solution)/shard_map/fine_seam/pallas_call | solution.py:716
  33.7 1.3 %collective-permute-start.15 = (f32[32,64,128]{2,1,0:T(8,128)S(1)}, f32[32,64,128]{2,1,0:T(8,128)}, u32[]{:S(2)}, u32[]{:S(2)}) collective-permute-start(f32[32,64,128]{2,1,0:T(8,128)S(1)} %get-tuple-element.101.w2), channel_id=1, source_target_pairs={{8,16},{16,24},{9,17},{17,25},{10,18},{18,26},{11,19},{19,27},{12,... | collective-permute-start | bytes 3145736 | tf_op jit(solution)/shard_map/ppermute | solution.py:735
  35.5 2.6 %collective-permute-start.8 = (f32[48,8,128]{2,1,0:T(8,128)}, f32[48,8,128]{2,1,0:T(8,128)}, u32[]{:S(2)}, u32[]{:S(2)}) collective-permute-start(f32[48,8,128]{2,1,0:T(8,128)} %get-tuple-element.70), channel_id=1, source_target_pairs={{2,1},{1,2},{6,5},{5,6},{10,9},{9,10},{14,13},{13,14},{18,17},{17,... | collective-permute-start | bytes 589832 | tf_op jit(solution)/shard_map/ppermute | solution.py:659
  38.1 4.0 %collective-permute-start.6 = (f32[12,8,128]{2,1,0:T(8,128)S(1)}, f32[12,8,128]{2,1,0:T(8,128)S(1)}, u32[]{:S(2)}, u32[]{:S(2)}) collective-permute-start(f32[12,8,128]{2,1,0:T(8,128)S(1)} %get-tuple-element.68), channel_id=1, source_target_pairs={{6,1},{5,2},{2,5},{1,6},{14,9},{13,10},{10,13},{9,14},{22,17},{21,... | collective-permute-start | bytes 147464 | tf_op jit(solution)/shard_map/ppermute | solution.py:659
  42.1 2.3 %collective-permute-done.6.rest_2_ = f32[12,8,128]{2,1,0:T(8,128)S(1)} collective-permute-done((f32[12,8,128]{2,1,0:T(8,128)S(1)}, f32[12,8,128]{2,1,0:T(8,128)S(1)}, u32[]{:S(2)}, u32[]{:S(2)}) %collective-permute-start.6) | collective-permute-done | bytes 49184 | tf_op jit(solution)/shard_map/ppermute | solution.py:659
  44.4 0.8 constant_dynamic-slice_fusion
  45.2 0.7 coarse_coefficients.1.coef
  46.5 1.8 %assemble.1.ge = f32[3,32,48,128]{3,2,1,0:T(8,128)S(1)} custom-call(f32[5,16,32,128]{3,2,1,0:T(8,128)S(1)} %get-tuple-element.66.co, f32[12,32,128]{2,1,0:T(8,128)} %collective-permute-done.5.rest_0_, f32[12,8,128]{2,1,0:T(8,128)S(1)} %collective-permute-done.9.rest_1_, f32[12,8,128]{2,1,0:T(8,128)S(1)} %collective-permute-done.6.rest_2_, ...), custom_call_target="tpu_custom_call" | custom-call | tf_op jit(solution)/shard_map/assemble/pallas_call | solution.py:748
  48.9 0.7 collective-permute-start.10
  49.5 0.7 collective-permute-start.11
  52.3 6.9 %collective-permute-done.15.rest_7_.arrived = f32[32,64,128]{2,1,0:T(8,128)} collective-permute-done((f32[32,64,128]{2,1,0:T(8,128)S(1)}, f32[32,64,128]{2,1,0:T(8,128)}, u32[]{:S(2)}, u32[]{:S(2)}) %collective-permute-start.15) | collective-permute-done | bytes 1048608 | tf_op jit(solution)/shard_map/ppermute | solution.py:735
  59.9 0.7 collective-permute-start.16
  60.6 0.7 collective-permute-start.17
  61.9 0.8 collective-permute-start.18
  62.8 0.9 collective-permute-start.25
  65.0 1.3 %collective-permute-start.21 = (f32[16,32,128]{2,1,0:T(8,128)S(1)}, f32[16,32,128]{2,1,0:T(8,128)S(1)}, u32[]{:S(2)}, u32[]{:S(2)}) collective-permute-start(f32[16,32,128]{2,1,0:T(8,128)S(1)} %get-tuple-element.97._), channel_id=1, source_target_pairs={{16,24},{17,25},{18,26},{19,27},{20,28},{21,29},{22,30},{23,31}} | collective-permute-start | bytes 786440 | tf_op jit(solution)/shard_map/ppermute | solution.py:796
  66.3 1.3 %collective-permute-start.22 = (f32[6,32,128]{2,1,0:T(8,128)S(1)}, f32[6,32,128]{2,1,0:T(8,128)S(1)}, u32[]{:S(2)}, u32[]{:S(2)}) collective-permute-start(f32[6,32,128]{2,1,0:T(8,128)S(1)} %get-tuple-element.98), channel_id=1, source_target_pairs={{20,24},{21,25},{22,26},{23,27},{16,28},{17,29},{18,30},{19,31}} | collective-permute-start | bytes 294920 | tf_op jit(solution)/shard_map/ppermute | solution.py:659
  67.6 1.3 %collective-permute-start.24 = (f32[16,8,128]{2,1,0:T(8,128)S(1)}, f32[16,8,128]{2,1,0:T(8,128)S(1)}, u32[]{:S(2)}, u32[]{:S(2)}) collective-permute-start(f32[16,8,128]{2,1,0:T(8,128)S(1)} %get-tuple-element.100), channel_id=1, source_target_pairs={{18,25},{17,26},{22,29},{21,30}} | collective-permute-start | bytes 196616 | tf_op jit(solution)/shard_map/ppermute | solution.py:659
  68.9 1.3 %collective-permute-start.23 = (f32[6,8,128]{2,1,0:T(8,128)S(1)}, f32[6,8,128]{2,1,0:T(8,128)S(1)}, u32[]{:S(2)}, u32[]{:S(2)}) collective-permute-start(f32[6,8,128]{2,1,0:T(8,128)S(1)} %get-tuple-element.99), channel_id=1, source_target_pairs={{22,25},{21,26},{18,29},{17,30}} | collective-permute-start | bytes 73736 | tf_op jit(solution)/shard_map/ppermute | solution.py:659
  70.2 2.5 %prepare.1.rest_7_ = f32[3,32,64,128]{3,2,1,0:T(8,128)S(1)} custom-call(f32[3,32,64,128]{3,2,1,0:T(8,128)S(1)} %bitcast.4, f32[32,64,128]{2,1,0:T(8,128)} %collective-permute-done.15.rest_7_.arrived, f32[32,64,128]{2,1,0:T(8,128)S(1)} %collective-permute-done.25.early, f32[32,64,128]{2,1,0:T(8,128)S(1)} %get-tuple-element.102.w1, ...), custom_call_target="tpu_custom_call" | custom-call | tf_op jit(solution)/shard_map/prepare/pallas_call | solution.py:799
  72.7 34.4 %collective-permute-done.23.rest_3_ = f32[6,8,128]{2,1,0:T(8,128)S(1)} collective-permute-done((f32[6,8,128]{2,1,0:T(8,128)S(1)}, f32[6,8,128]{2,1,0:T(8,128)S(1)}, u32[]{:S(2)}, u32[]{:S(2)}) %collective-permute-start.23) | collective-permute-done | bytes 24608 | tf_op jit(solution)/shard_map/ppermute | solution.py:659
  107.1 1.9 %collective-permute-start.26 = (f32[22,8,128]{2,1,0:T(8,128)S(1)}, f32[22,8,128]{2,1,0:T(8,128)S(1)}, u32[]{:S(2)}, u32[]{:S(2)}) collective-permute-start(f32[22,8,128]{2,1,0:T(8,128)S(1)} %fusion), channel_id=1, source_target_pairs={{25,24},{24,25},{27,26},{26,27},{29,28},{28,29},{31,30},{30,31}} | collective-permute-start | bytes 270344 | tf_op jit(solution)/shard_map/ppermute | solution.py:820
  109.1 1.3 %collective-permute-done.26 = f32[22,8,128]{2,1,0:T(8,128)S(1)} collective-permute-done((f32[22,8,128]{2,1,0:T(8,128)S(1)}, f32[22,8,128]{2,1,0:T(8,128)S(1)}, u32[]{:S(2)}, u32[]{:S(2)}) %collective-permute-start.26) | collective-permute-done | bytes 90144 | tf_op jit(solution)/shard_map/ppermute | solution.py:820
  110.3 6.8 %chain_3.1 = (f32[3,16,32,128]{3,2,1,0:T(8,128)S(1)}, f32[16,32,128]{2,1,0:T(8,128)}, f32[3,32,64,128]{3,2,1,0:T(8,128)}) custom-call(s32[4]{0:T(128)S(1)} %copy-done.3, f32[3,32,48,128]{3,2,1,0:T(8,128)S(1)} %assemble.1.ge, f32[2,16,48,128]{3,2,1,0:T(8,128)S(1)} %coarse_coefficients.1.coef, ...), custom_call_target="tpu_custom_call", output_to_operand_aliasing={{0}: (4, {})} | custom-call | tf_op jit(solution)/shard_map/chain_3/pallas_call | solution.py:783
  (52 shorter events, 6.4 us)
Async XLA Ops:
  0.0 14.3 %copy-start.3 = (s32[4]{0:T(128)S(1)}, s32[4]{0:T(128)}, u32[]{:S(2)}) copy-start(s32[4]{0:T(128)} %steps.13) | copy-start | bytes 52
  0.9 1.9 %copy-start = (f32[1,3,32,64,128]{4,3,2,1,0:T(8,128)S(1)}, f32[1,3,32,64,128]{4,3,2,1,0:T(8,128)}, u32[]{:S(2)}) copy-start(f32[1,3,32,64,128]{4,3,2,1,0:T(8,128)} %param.4) | copy-start | bytes 9437188
  2.8 11.5 %copy-start.1 = (f32[1,3,32,64,128]{4,3,2,1,0:T(8,128)S(1)}, f32[1,3,32,64,128]{4,3,2,1,0:T(8,128)}, u32[]{:S(2)}) copy-start(f32[1,3,32,64,128]{4,3,2,1,0:T(8,128)} %param.4) | copy-start | bytes 9437188
  3.6 24.6 %collective-permute-start = (f32[25,64,128]{2,1,0:T(8,128)S(1)}, f32[25,64,128]{2,1,0:T(8,128)S(1)}, u32[]{:S(2)}, u32[]{:S(2)}) collective-permute-start(f32[25,64,128]{2,1,0:T(8,128)S(1)} %get-tuple-element.57), channel_id=1, source_target_pairs={{4,0},{5,1},{6,2},{7,3},{0,4},{1,5},{2,6},{3,7},{12,8},{13,9},{14,... | collective-permute-start | bytes 2457608 | tf_op jit(solution)/shard_map/ppermute | solution.py:659
  5.1 5.6 %collective-permute-start.3 = (f32[97,8,128]{2,1,0:T(8,128)S(1)}, f32[97,8,128]{2,1,0:T(8,128)S(1)}, u32[]{:S(2)}, u32[]{:S(2)}) collective-permute-start(f32[97,8,128]{2,1,0:T(8,128)S(1)} %get-tuple-element.60), channel_id=1, source_target_pairs={{1,0},{0,1},{3,2},{2,3},{5,4},{4,5},{7,6},{6,7},{9,8},{8,9},{11,10... | collective-permute-start | bytes 1191944 | tf_op jit(solution)/shard_map/ppermute | solution.py:659
  5.1 9.1 %collective-permute-start.4 = (f32[97,8,128]{2,1,0:T(8,128)S(1)}, f32[97,8,128]{2,1,0:T(8,128)S(1)}, u32[]{:S(2)}, u32[]{:S(2)}) collective-permute-start(f32[97,8,128]{2,1,0:T(8,128)S(1)} %get-tuple-element.61), channel_id=1, source_target_pairs={{2,1},{1,2},{6,5},{5,6},{10,9},{9,10},{14,13},{13,14},{18,17},{17,... | collective-permute-start | bytes 1191944 | tf_op jit(solution)/shard_map/ppermute | solution.py:659
  7.7 20.5 %collective-permute-start.1 = (f32[25,8,128]{2,1,0:T(8,128)S(1)}, f32[25,8,128]{2,1,0:T(8,128)S(1)}, u32[]{:S(2)}, u32[]{:S(2)}) collective-permute-start(f32[25,8,128]{2,1,0:T(8,128)S(1)} %get-tuple-element.58), channel_id=1, source_target_pairs={{5,0},{4,1},{7,2},{6,3},{1,4},{0,5},{3,6},{2,7},{13,8},{12,9},{15,... | collective-permute-start | bytes 307208 | tf_op jit(solution)/shard_map/ppermute | solution.py:659
  7.8 20.4 %collective-permute-start.2 = (f32[25,8,128]{2,1,0:T(8,128)S(1)}, f32[25,8,128]{2,1,0:T(8,128)S(1)}, u32[]{:S(2)}, u32[]{:S(2)}) collective-permute-start(f32[25,8,128]{2,1,0:T(8,128)S(1)} %get-tuple-element.59), channel_id=1, source_target_pairs={{6,1},{5,2},{2,5},{1,6},{14,9},{13,10},{10,13},{9,14},{22,17},{21,... | collective-permute-start | bytes 307208 | tf_op jit(solution)/shard_map/ppermute | solution.py:659
  33.7 25.6 %collective-permute-start.15 = (f32[32,64,128]{2,1,0:T(8,128)S(1)}, f32[32,64,128]{2,1,0:T(8,128)}, u32[]{:S(2)}, u32[]{:S(2)}) collective-permute-start(f32[32,64,128]{2,1,0:T(8,128)S(1)} %get-tuple-element.101.w2), channel_id=1, source_target_pairs={{8,16},{16,24},{9,17},{17,25},{10,18},{18,26},{11,19},{19,27},{12,... | collective-permute-start | bytes 3145736 | tf_op jit(solution)/shard_map/ppermute | solution.py:735
  35.0 9.4 %collective-permute-start.5 = (f32[12,32,128]{2,1,0:T(8,128)}, f32[12,32,128]{2,1,0:T(8,128)}, u32[]{:S(2)}, u32[]{:S(2)}) collective-permute-start(f32[12,32,128]{2,1,0:T(8,128)} %get-tuple-element.67), channel_id=1, source_target_pairs={{4,0},{5,1},{6,2},{7,3},{0,4},{1,5},{2,6},{3,7},{12,8},{13,9},{14,... | collective-permute-start | bytes 589832 | tf_op jit(solution)/shard_map/ppermute | solution.py:659
  35.5 8.9 %collective-permute-start.7 = (f32[48,8,128]{2,1,0:T(8,128)}, f32[48,8,128]{2,1,0:T(8,128)}, u32[]{:S(2)}, u32[]{:S(2)}) collective-permute-start(f32[48,8,128]{2,1,0:T(8,128)} %get-tuple-element.69), channel_id=1, source_target_pairs={{1,0},{0,1},{3,2},{2,3},{5,4},{4,5},{7,6},{6,7},{9,8},{8,9},{11,10... | collective-permute-start | bytes 589832 | tf_op jit(solution)/shard_map/ppermute | solution.py:659
  35.5 8.9 %collective-permute-start.8 = (f32[48,8,128]{2,1,0:T(8,128)}, f32[48,8,128]{2,1,0:T(8,128)}, u32[]{:S(2)}, u32[]{:S(2)}) collective-permute-start(f32[48,8,128]{2,1,0:T(8,128)} %get-tuple-element.70), channel_id=1, source_target_pairs={{2,1},{1,2},{6,5},{5,6},{10,9},{9,10},{14,13},{13,14},{18,17},{17,... | collective-permute-start | bytes 589832 | tf_op jit(solution)/shard_map/ppermute | solution.py:659
  38.1 6.3 %collective-permute-start.6 = (f32[12,8,128]{2,1,0:T(8,128)S(1)}, f32[12,8,128]{2,1,0:T(8,128)S(1)}, u32[]{:S(2)}, u32[]{:S(2)}) collective-permute-start(f32[12,8,128]{2,1,0:T(8,128)S(1)} %get-tuple-element.68), channel_id=1, source_target_pairs={{6,1},{5,2},{2,5},{1,6},{14,9},{13,10},{10,13},{9,14},{22,17},{21,... | collective-permute-start | bytes 147464 | tf_op jit(solution)/shard_map/ppermute | solution.py:659
  45.2 1.2 %collective-permute-start.9 = (f32[12,8,128]{2,1,0:T(8,128)S(1)}, f32[12,8,128]{2,1,0:T(8,128)S(1)}, u32[]{:S(2)}, u32[]{:S(2)}) collective-permute-start(f32[12,8,128]{2,1,0:T(8,128)S(1)} %constant_dynamic-slice_fusion), channel_id=1, source_target_pairs={{1,0},{0,1},{3,2},{2,3},{5,4},{4,5},{7,6},{6,7},{9,8},{8,9},{11,10... | collective-permute-start | bytes 147464 | tf_op jit(solution)/shard_map/ppermute | solution.py:659
  48.9 2.7 %collective-permute-start.10 = (f32[16,32,128]{2,1,0:T(8,128)S(1)}, f32[16,32,128]{2,1,0:T(8,128)S(1)}, u32[]{:S(2)}, u32[]{:S(2)}) collective-permute-start(f32[16,32,128]{2,1,0:T(8,128)S(1)} %get-tuple-element.77), channel_id=1, source_target_pairs={{0,8},{1,9},{2,10},{3,11},{4,12},{5,13},{6,14},{7,15}} | collective-permute-start | bytes 786440 | tf_op jit(solution)/shard_map/ppermute | solution.py:796
  49.5 2.0 %collective-permute-start.11 = (f32[6,32,128]{2,1,0:T(8,128)S(1)}, f32[6,32,128]{2,1,0:T(8,128)S(1)}, u32[]{:S(2)}, u32[]{:S(2)}) collective-permute-start(f32[6,32,128]{2,1,0:T(8,128)S(1)} %get-tuple-element.78), channel_id=1, source_target_pairs={{4,8},{5,9},{6,10},{7,11},{0,12},{1,13},{2,14},{3,15}} | collective-permute-start | bytes 294920 | tf_op jit(solution)/shard_map/ppermute | solution.py:659
  50.2 1.4 %collective-permute-start.13 = (f32[16,8,128]{2,1,0:T(8,128)S(1)}, f32[16,8,128]{2,1,0:T(8,128)S(1)}, u32[]{:S(2)}, u32[]{:S(2)}) collective-permute-start(f32[16,8,128]{2,1,0:T(8,128)S(1)} %get-tuple-element.80), channel_id=1, source_target_pairs={{2,9},{1,10},{6,13},{5,14}} | collective-permute-start | bytes 196616 | tf_op jit(solution)/shard_map/ppermute | solution.py:659
  50.9 0.7 collective-permute-start.12
  51.6 0.7 collective-permute-start.14
  59.9 2.9 %collective-permute-start.16 = (f32[16,32,128]{2,1,0:T(8,128)S(1)}, f32[16,32,128]{2,1,0:T(8,128)S(1)}, u32[]{:S(2)}, u32[]{:S(2)}) collective-permute-start(f32[16,32,128]{2,1,0:T(8,128)S(1)} %get-tuple-element.87), channel_id=1, source_target_pairs={{8,16},{9,17},{10,18},{11,19},{12,20},{13,21},{14,22},{15,23}} | collective-permute-start | bytes 786440 | tf_op jit(solution)/shard_map/ppermute | solution.py:796
  60.6 2.2 %collective-permute-start.17 = (f32[6,32,128]{2,1,0:T(8,128)S(1)}, f32[6,32,128]{2,1,0:T(8,128)S(1)}, u32[]{:S(2)}, u32[]{:S(2)}) collective-permute-start(f32[6,32,128]{2,1,0:T(8,128)S(1)} %get-tuple-element.88), channel_id=1, source_target_pairs={{12,16},{13,17},{14,18},{15,19},{8,20},{9,21},{10,22},{11,23}} | collective-permute-start | bytes 294920 | tf_op jit(solution)/shard_map/ppermute | solution.py:659
  61.2 1.5 %collective-permute-start.19 = (f32[16,8,128]{2,1,0:T(8,128)S(1)}, f32[16,8,128]{2,1,0:T(8,128)S(1)}, u32[]{:S(2)}, u32[]{:S(2)}) collective-permute-start(f32[16,8,128]{2,1,0:T(8,128)S(1)} %get-tuple-element.90), channel_id=1, source_target_pairs={{10,17},{9,18},{14,21},{13,22}} | collective-permute-start | bytes 196616 | tf_op jit(solution)/shard_map/ppermute | solution.py:659
  61.9 8.3 %copy-start.2 = (f32[1,3,32,64,128]{4,3,2,1,0:T(8,128)S(1)}, f32[1,3,32,64,128]{4,3,2,1,0:T(8,128)}, u32[]{:S(2)}) copy-start(f32[1,3,32,64,128]{4,3,2,1,0:T(8,128)} %param.4) | copy-start | bytes 9437188
  61.9 0.8 collective-permute-start.18
  62.8 7.4 %collective-permute-start.25 = (f32[32,64,128]{2,1,0:T(8,128)S(1)}, f32[32,64,128]{2,1,0:T(8,128)S(1)}, u32[]{:S(2)}, u32[]{:S(2)}) collective-permute-start(f32[32,64,128]{2,1,0:T(8,128)S(1)} %get-tuple-element.101.w2), channel_id=1, source_target_pairs={{0,8},{1,9},{2,10},{3,11},{4,12},{5,13},{6,14},{7,15}} | collective-permute-start | bytes 3145736 | tf_op jit(solution)/shard_map/ppermute | solution.py:812
  63.7 0.7 collective-permute-start.20
  65.0 42.1 %collective-permute-start.21 = (f32[16,32,128]{2,1,0:T(8,128)S(1)}, f32[16,32,128]{2,1,0:T(8,128)S(1)}, u32[]{:S(2)}, u32[]{:S(2)}) collective-permute-start(f32[16,32,128]{2,1,0:T(8,128)S(1)} %get-tuple-element.97._), channel_id=1, source_target_pairs={{16,24},{17,25},{18,26},{19,27},{20,28},{21,29},{22,30},{23,31}} | collective-permute-start | bytes 786440 | tf_op jit(solution)/shard_map/ppermute | solution.py:796
  66.3 40.8 %collective-permute-start.22 = (f32[6,32,128]{2,1,0:T(8,128)S(1)}, f32[6,32,128]{2,1,0:T(8,128)S(1)}, u32[]{:S(2)}, u32[]{:S(2)}) collective-permute-start(f32[6,32,128]{2,1,0:T(8,128)S(1)} %get-tuple-element.98), channel_id=1, source_target_pairs={{20,24},{21,25},{22,26},{23,27},{16,28},{17,29},{18,30},{19,31}} | collective-permute-start | bytes 294920 | tf_op jit(solution)/shard_map/ppermute | solution.py:659
  67.6 39.5 %collective-permute-start.24 = (f32[16,8,128]{2,1,0:T(8,128)S(1)}, f32[16,8,128]{2,1,0:T(8,128)S(1)}, u32[]{:S(2)}, u32[]{:S(2)}) collective-permute-start(f32[16,8,128]{2,1,0:T(8,128)S(1)} %get-tuple-element.100), channel_id=1, source_target_pairs={{18,25},{17,26},{22,29},{21,30}} | collective-permute-start | bytes 196616 | tf_op jit(solution)/shard_map/ppermute | solution.py:659
  68.9 38.2 %collective-permute-start.23 = (f32[6,8,128]{2,1,0:T(8,128)S(1)}, f32[6,8,128]{2,1,0:T(8,128)S(1)}, u32[]{:S(2)}, u32[]{:S(2)}) collective-permute-start(f32[6,8,128]{2,1,0:T(8,128)S(1)} %get-tuple-element.99), channel_id=1, source_target_pairs={{22,25},{21,26},{18,29},{17,30}} | collective-permute-start | bytes 73736 | tf_op jit(solution)/shard_map/ppermute | solution.py:659
  107.1 3.2 %collective-permute-start.26 = (f32[22,8,128]{2,1,0:T(8,128)S(1)}, f32[22,8,128]{2,1,0:T(8,128)S(1)}, u32[]{:S(2)}, u32[]{:S(2)}) collective-permute-start(f32[22,8,128]{2,1,0:T(8,128)S(1)} %fusion), channel_id=1, source_target_pairs={{25,24},{24,25},{27,26},{26,27},{29,28},{28,29},{31,30},{30,31}} | collective-permute-start | bytes 270344 | tf_op jit(solution)/shard_map/ppermute | solution.py:820

commit v4 on v3

--- a/solution.py
+++ b/solution.py
@@ -266,7 +266,7 @@
             (7, self.end2),
         ]
 
-    def coarse_pair(self, x, i, w1o, w2o, co, plain, tmp, ny):
+    def coarse_pair(self, x, i, w1o, w2o, co, plain, tmp, ny, turn=0):
         ye = ny + 2 * YW
         masks = wide_masks(2, ye)
         h, a = self.h, self.a
@@ -283,16 +283,17 @@
             c, p, z = neighbours(ref[pl.ds(x - 1, 4)], masks)
             w.append(c)
             g.append(reaction(c) + k * (p + z - 6.0 * c))
-            store_plain(tmp, (2 * m + 0,), c[0])
-            store_plain(tmp, (2 * m + 1,), c[1])
-            out[pl.ds(2 * i, 2)] = tmp[2 * m : 2 * m + 2, YW : YW + ny]
+            slot = 4 * turn + 2 * m
+            store_plain(tmp, (slot,), c[0])
+            store_plain(tmp, (slot + 1,), c[1])
+            out[pl.ds(2 * i, 2)] = tmp[slot : slot + 2, YW : YW + ny]
         c0, c1 = [pair_sum(wt[0] * g[0] + wt[1] * g[1] + wt[2] * g[2]) * 0.25 for wt in WEIGHTS]
         u0, u1, u2 = [pair_sum(v) * 0.25 for v in w]
         start = jnp.where(lax.axis_index("tm") == 0, u0 + a * reaction(u0), 0.0)
         values = (start + h * c0 - a * reaction(u0) - u1, u1, h * c1 - a * reaction(u1) - u2, u0, u2)
         for n, v in enumerate(values):
-            store_plain(plain, (n,), v)
-            co[n, i] = plain[n, YW // 2 : YW // 2 + ny // 2]
+            store_plain(plain, (5 * turn + n,), v)
+            co[n, i] = plain[5 * turn + n, YW // 2 : YW // 2 + ny // 2]
 
 
 def parts(body, step, masks, x):
@@ -351,15 +352,16 @@
         lambda j, at: permuted(ue, j, at), f0, q0, qa, qb, p2, w1, w2, fine, h, a, lambda x: lax.div(x, TILE)
     )
     for k, body in st.bodies():
-        step = FEW if k == 1 else MANY
-        if seams == 2 and (nx - 2 * k) % step:
-            step = 2
+        n = nx - k * seams
+        step = min((s for s in range(7, 33) if seams < 2 or n % s == 0), key=lambda s: (-n % s, -s), default=2)
         sweep_rows(nx, FW, -k, step, functools.partial(parts, body, step, wide_masks(SUB, ye)))
 
     def coarse_rows(x):
-        st.coarse_pair(x, lax.div(x - FW, 2), w1o, w2o, co, plain, tmp, ny)
-
-    sweep_rows(nx, FW, -8, 2, coarse_rows)
+        for turn in range(2):
+            y = x + 2 * turn
+            st.coarse_pair(y, lax.div(y - FW, 2), w1o, w2o, co, plain, tmp, ny, turn)
+
+    sweep_rows(nx, FW, -8, 4, coarse_rows)
     for n in range(seams):
         low = seam_is_low(n)
         src, dst = pick(low, FW, FW + nx - SEAM), pick(low, FW, 0)
@@ -429,9 +431,8 @@
             lax.fori_loop(0, 8 // step, lambda i, _: (parts(body, step, masks, first + i * step), 0)[1], 0)
         first = pick(low, FW, SEAM - 8)
         row = pick(low, 0, nx // 2 - 4)
-        lax.fori_loop(
-            0, 4, lambda i, _: (st.coarse_pair(first + 2 * i, row + i, w1o, w2o, co, plain, tmp, ny), 0)[1], 0
-        )
+        for i in range(4):
+            st.coarse_pair(first + 2 * i, row + i, w1o, w2o, co, plain, tmp, ny, i % 2)
     cx, cy = nx // 2, ny // 2
     fields = ((0, CW), (1, CN), (2, CN))
     for (k, l), o in zip(ckeys, couts):
@@ -528,7 +529,8 @@
         masks = wide_masks(step, ye)
 
         def rows(r, body):
-            sweep_rows(cx, CW, r, LOW, lambda x: [body(x + i) for i in range(0, LOW, step)])
+            n = cx + r * min(ngx - 1, 2)
+            sweep_rows(cx, CW, r, n, lambda x: [body(x + i) for i in range(0, n, step)])
 
         def coefs(n, x):
             return jnp.stack([coef[n, lax.div(x + i, 2)] for i in range(step)])
@@ -705,8 +707,8 @@
         + [
             pltpu.VMEM((3, xe // TILE, fye, cz), f32),
             pltpu.VMEM((3, 3, tp, cz), f32),
-            pltpu.VMEM((5, fye // 2, cz), f32),
-            pltpu.VMEM((4, fye, cz), f32),
+            pltpu.VMEM((10, fye // 2, cz), f32),
+            pltpu.VMEM((8, fye, cz), f32),
             pltpu.SemaphoreType.DMA((nk * (3 + tp) + 2,)),
         ],
         compiler_params=params(38),
@@ -722,8 +724,8 @@
         scratch_shapes=[
             pltpu.VMEM((seams, 3, FW, fye, cz), f32),
             pltpu.VMEM((3, (FW + SEAM) // TILE, fye, cz), f32),
-            pltpu.VMEM((5, fye // 2, cz), f32),
-            pltpu.VMEM((4, fye, cz), f32),
+            pltpu.VMEM((10, fye // 2, cz), f32),
+            pltpu.VMEM((8, fye, cz), f32),
             pltpu.SemaphoreType.DMA((nk * (3 + tp) + 2,)),
         ],
         input_output_aliases={2 + nk + i: i for i in range(4)},
@@ -807,7 +809,7 @@
                 )(u, arrived, early, w1, w2, co, whole)
                 moving.append(ready)
             moving = lax.optimization_barrier(moving)
-            if n == min(1, nt - 2):
+            if n == 0:
                 late, moving[0] = lax.optimization_barrier((w2, moving[0]))
                 early = lax.ppermute(late, "tm", [(0, 1)])
             own, got = moving[0], moving[1 : 1 + len(straight)]

time: 119 us -> 113 us (0.950)
  Pallas kernels: 33.8 us -> 30.3 us
  waiting for transfers between devices: 48.9 us -> 46.7 us
    ppermute x19, waiting for transfers between devices: 40.7 us -> 38.2 us  [send(): lax.ppermute(v, AXES, routes(sizes, k, l, hop))]
    pallas_call x1, Pallas kernels: 13.9 us -> 11.5 us  [per_device(): pl.pallas_call(functools.partial(inner_kernel, ykeys, local, seams), out_...]
  transfers between devices with their start and end apart: 27 -> 27, of which waited for: 6 -> 7; matrix products, arithmetic and copies ran while one was open for 1% -> 1% of each run, Pallas kernels for 17% -> 17%
where the time goes in v4:
time: 113 us; the launch traced here: 112 us
  waiting for transfers between devices  46.7 us (41%)
  starting transfers between devices  30.8 us (27%)
  Pallas kernels  30.3 us (27%)
  local copies, waits for them, and re-layouts  2.74 us (2%)
    ppermute x19, waiting for transfers between devices, send(): lax.ppermute(v, AXES, routes(sizes, k, l, hop))  38.2 us
    ppermute x19, starting transfers between devices, send(): lax.ppermute(v, AXES, routes(sizes, k, l, hop))  22.7 us
    pallas_call x1, Pallas kernels, per_device(): pl.pallas_call(functools.partial(inner_kernel, ykeys, local, seams), out_...  11.5 us
    pallas_call x4, Pallas kernels, per_device(): pl.pallas_call(functools.partial(chain_kernel, n, sent, arrive if n else...  7.65 us
    ppermute x1, waiting for transfers between devices, per_device(): arrived = lax.ppermute(w2, 'tm', [(i, i + 1) for i in range(1, nt - 1)])  7.25 us
    pallas_call x1, Pallas kernels, per_device(): pl.pallas_call(functools.partial(seam_kernel, keys, now, local, seams), o...  5.31 us
    ppermute x3, starting transfers between devices, per_device(): strip = lax.ppermute(strip, AXES, pairs)  3.38 us
    ppermute x3, starting transfers between devices, per_device(): own = lax.ppermute(whole, AXES, routes(sizes, None, None, n))  2.65 us
  transfers between devices with their start and end apart: 27, of which 7 were waited for; matrix products, arithmetic and copies ran while one was open for 1% of the time, Pallas kernels for 17%

profile of v4, /device:TPU:26, one launch (start us, length us, event | category | flops | bytes accessed | tf_op | source)
XLA Modules:
  0.0 112.1 jit_solution(18319576303130248199)
XLA Ops:
  0.0 0.9 select_reduce_fusion
  0.9 1.9 %copy-done = f32[1,3,32,64,128]{4,3,2,1,0:T(8,128)S(1)} copy-done((f32[1,3,32,64,128]{4,3,2,1,0:T(8,128)S(1)}, f32[1,3,32,64,128]{4,3,2,1,0:T(8,128)}, u32[]{:S(2)}) %copy-start) | copy-done | bytes 3145752
  2.8 0.8 pack.1
  3.6 1.6 %collective-permute-start = (f32[25,64,128]{2,1,0:T(8,128)S(1)}, f32[25,64,128]{2,1,0:T(8,128)S(1)}, u32[]{:S(2)}, u32[]{:S(2)}) collective-permute-start(f32[25,64,128]{2,1,0:T(8,128)S(1)} %get-tuple-element.57), channel_id=1, source_target_pairs={{4,0},{5,1},{6,2},{7,3},{0,4},{1,5},{2,6},{3,7},{12,8},{13,9},{14,... | collective-permute-start | bytes 2457608 | tf_op jit(solution)/shard_map/ppermute | solution.py:661
  5.1 2.5 %collective-permute-start.4 = (f32[97,8,128]{2,1,0:T(8,128)S(1)}, f32[97,8,128]{2,1,0:T(8,128)S(1)}, u32[]{:S(2)}, u32[]{:S(2)}) collective-permute-start(f32[97,8,128]{2,1,0:T(8,128)S(1)} %get-tuple-element.61), channel_id=1, source_target_pairs={{2,1},{1,2},{6,5},{5,6},{10,9},{9,10},{14,13},{13,14},{18,17},{17,... | collective-permute-start | bytes 1191944 | tf_op jit(solution)/shard_map/ppermute | solution.py:661
  7.8 3.0 %collective-permute-start.2 = (f32[25,8,128]{2,1,0:T(8,128)S(1)}, f32[25,8,128]{2,1,0:T(8,128)S(1)}, u32[]{:S(2)}, u32[]{:S(2)}) collective-permute-start(f32[25,8,128]{2,1,0:T(8,128)S(1)} %get-tuple-element.59), channel_id=1, source_target_pairs={{6,1},{5,2},{2,5},{1,6},{14,9},{13,10},{10,13},{9,14},{22,17},{21,... | collective-permute-start | bytes 307208 | tf_op jit(solution)/shard_map/ppermute | solution.py:661
  10.7 3.5 %collective-permute-done.4.rest_1_.rest_4_ = f32[97,8,128]{2,1,0:T(8,128)S(1)} collective-permute-done((f32[97,8,128]{2,1,0:T(8,128)S(1)}, f32[97,8,128]{2,1,0:T(8,128)S(1)}, u32[]{:S(2)}, u32[]{:S(2)}) %collective-permute-start.4) | collective-permute-done | bytes 397344 | tf_op jit(solution)/shard_map/ppermute | solution.py:661
  14.3 11.5 %fine_inner.1 = (f32[32,64,128]{2,1,0:T(8,128)S(1)}, f32[32,64,128]{2,1,0:T(8,128)S(1)}, f32[5,16,32,128]{3,2,1,0:T(8,128)S(1)}, f32[1,10,20,80,128]{4,3,2,1,0:T(8,128)S(1)}) custom-call(s32[4]{0:T(128)S(1)} %copy-done.3, f32[3,32,64,128]{3,2,1,0:T(8,128)S(1)} %bitcast.3, f32[8,128]{1,0:T(8,128)S(1)} %pad.4.table, ...), custom_call_target="tpu_custom_call" | custom-call | flops 52428800 | bytes 40000000 | tf_op jit(solution)/shard_map/fine_inner/pallas_call | solution.py:699
  25.9 5.3 %fine_seam.1 = (f32[32,64,128]{2,1,0:T(8,128)S(1)}, f32[32,64,128]{2,1,0:T(8,128)S(1)}, f32[5,16,32,128]{3,2,1,0:T(8,128)S(1)}, f32[1,10,20,80,128]{4,3,2,1,0:T(...) custom-call(s32[4]{0:T(128)S(1)} %copy-done.3, ...), custom_call_target="tpu_custom_call", output_to_operand_aliasing={{0}: (7, {}), {1}: (8, {}), {2}: (9, {}), {3}: (10, {})} | custom-call | tf_op jit(solution)/shard_map/fine_seam/pallas_call | solution.py:718
  31.3 1.3 %collective-permute-start.15 = (f32[32,64,128]{2,1,0:T(8,128)S(1)}, f32[32,64,128]{2,1,0:T(8,128)}, u32[]{:S(2)}, u32[]{:S(2)}) collective-permute-start(f32[32,64,128]{2,1,0:T(8,128)S(1)} %get-tuple-element.101.w2), channel_id=1, source_target_pairs={{8,16},{16,24},{9,17},{17,25},{10,18},{18,26},{11,19},{19,27},{12,... | collective-permute-start | bytes 3145736 | tf_op jit(solution)/shard_map/ppermute | solution.py:737
  32.6 1.4 %collective-permute-start.5 = (f32[12,32,128]{2,1,0:T(8,128)}, f32[12,32,128]{2,1,0:T(8,128)}, u32[]{:S(2)}, u32[]{:S(2)}) collective-permute-start(f32[12,32,128]{2,1,0:T(8,128)} %get-tuple-element.67), channel_id=1, source_target_pairs={{4,0},{5,1},{6,2},{7,3},{0,4},{1,5},{2,6},{3,7},{12,8},{13,9},{14,... | collective-permute-start | bytes 589832 | tf_op jit(solution)/shard_map/ppermute | solution.py:661
  34.7 2.0 %collective-permute-start.8 = (f32[48,8,128]{2,1,0:T(8,128)}, f32[48,8,128]{2,1,0:T(8,128)}, u32[]{:S(2)}, u32[]{:S(2)}) collective-permute-start(f32[48,8,128]{2,1,0:T(8,128)} %get-tuple-element.70), channel_id=1, source_target_pairs={{2,1},{1,2},{6,5},{5,6},{10,9},{9,10},{14,13},{13,14},{18,17},{17,... | collective-permute-start | bytes 589832 | tf_op jit(solution)/shard_map/ppermute | solution.py:661
  36.7 3.5 %collective-permute-start.6 = (f32[12,8,128]{2,1,0:T(8,128)S(1)}, f32[12,8,128]{2,1,0:T(8,128)S(1)}, u32[]{:S(2)}, u32[]{:S(2)}) collective-permute-start(f32[12,8,128]{2,1,0:T(8,128)S(1)} %get-tuple-element.68), channel_id=1, source_target_pairs={{6,1},{5,2},{2,5},{1,6},{14,9},{13,10},{10,13},{9,14},{22,17},{21,... | collective-permute-start | bytes 147464 | tf_op jit(solution)/shard_map/ppermute | solution.py:661
  40.2 2.8 %collective-permute-done.6.rest_2_ = f32[12,8,128]{2,1,0:T(8,128)S(1)} collective-permute-done((f32[12,8,128]{2,1,0:T(8,128)S(1)}, f32[12,8,128]{2,1,0:T(8,128)S(1)}, u32[]{:S(2)}, u32[]{:S(2)}) %collective-permute-start.6) | collective-permute-done | bytes 49184 | tf_op jit(solution)/shard_map/ppermute | solution.py:661
  43.0 0.8 constant_dynamic-slice_fusion
  43.8 0.7 coarse_coefficients.1.coef
  45.1 1.8 %assemble.1.ge = f32[3,32,48,128]{3,2,1,0:T(8,128)S(1)} custom-call(f32[5,16,32,128]{3,2,1,0:T(8,128)S(1)} %get-tuple-element.66.co, f32[12,32,128]{2,1,0:T(8,128)} %collective-permute-done.5.rest_0_, f32[12,8,128]{2,1,0:T(8,128)S(1)} %collective-permute-done.9.rest_1_, f32[12,8,128]{2,1,0:T(8,128)S(1)} %collective-permute-done.6.rest_2_, ...), custom_call_target="tpu_custom_call" | custom-call | tf_op jit(solution)/shard_map/assemble/pallas_call | solution.py:750
  46.8 0.8 chain_0.1
  47.6 0.7 collective-permute-start.10
  50.4 0.7 collective-permute-start.25
  51.9 7.3 %collective-permute-done.15.rest_7_.arrived = f32[32,64,128]{2,1,0:T(8,128)} collective-permute-done((f32[32,64,128]{2,1,0:T(8,128)S(1)}, f32[32,64,128]{2,1,0:T(8,128)}, u32[]{:S(2)}, u32[]{:S(2)}) %collective-permute-start.15) | collective-permute-done | bytes 1048608 | tf_op jit(solution)/shard_map/ppermute | solution.py:737
  61.8 0.8 collective-permute-start.18
  62.6 0.8 collective-permute-start.20
  64.1 1.3 %collective-permute-start.21 = (f32[16,32,128]{2,1,0:T(8,128)S(1)}, f32[16,32,128]{2,1,0:T(8,128)S(1)}, u32[]{:S(2)}, u32[]{:S(2)}) collective-permute-start(f32[16,32,128]{2,1,0:T(8,128)S(1)} %get-tuple-element.97._), channel_id=1, source_target_pairs={{16,24},{17,25},{18,26},{19,27},{20,28},{21,29},{22,30},{23,31}} | collective-permute-start | bytes 786440 | tf_op jit(solution)/shard_map/ppermute | solution.py:798
  65.4 1.3 %collective-permute-start.22 = (f32[6,32,128]{2,1,0:T(8,128)S(1)}, f32[6,32,128]{2,1,0:T(8,128)S(1)}, u32[]{:S(2)}, u32[]{:S(2)}) collective-permute-start(f32[6,32,128]{2,1,0:T(8,128)S(1)} %get-tuple-element.98), channel_id=1, source_target_pairs={{20,24},{21,25},{22,26},{23,27},{16,28},{17,29},{18,30},{19,31}} | collective-permute-start | bytes 294920 | tf_op jit(solution)/shard_map/ppermute | solution.py:661
  66.7 1.3 %collective-permute-start.24 = (f32[16,8,128]{2,1,0:T(8,128)S(1)}, f32[16,8,128]{2,1,0:T(8,128)S(1)}, u32[]{:S(2)}, u32[]{:S(2)}) collective-permute-start(f32[16,8,128]{2,1,0:T(8,128)S(1)} %get-tuple-element.100), channel_id=1, source_target_pairs={{18,25},{17,26},{22,29},{21,30}} | collective-permute-start | bytes 196616 | tf_op jit(solution)/shard_map/ppermute | solution.py:661
  68.0 1.3 %collective-permute-start.23 = (f32[6,8,128]{2,1,0:T(8,128)S(1)}, f32[6,8,128]{2,1,0:T(8,128)S(1)}, u32[]{:S(2)}, u32[]{:S(2)}) collective-permute-start(f32[6,8,128]{2,1,0:T(8,128)S(1)} %get-tuple-element.99), channel_id=1, source_target_pairs={{22,25},{21,26},{18,29},{17,30}} | collective-permute-start | bytes 73736 | tf_op jit(solution)/shard_map/ppermute | solution.py:661
  69.3 2.5 %prepare.1.rest_7_ = f32[3,32,64,128]{3,2,1,0:T(8,128)S(1)} custom-call(f32[3,32,64,128]{3,2,1,0:T(8,128)S(1)} %bitcast.4, f32[32,64,128]{2,1,0:T(8,128)} %collective-permute-done.15.rest_7_.arrived, f32[32,64,128]{2,1,0:T(8,128)S(1)} %collective-permute-done.25.early, f32[32,64,128]{2,1,0:T(8,128)S(1)} %get-tuple-element.102.w1, ...), custom_call_target="tpu_custom_call" | custom-call | tf_op jit(solution)/shard_map/prepare/pallas_call | solution.py:801
  71.9 31.2 %collective-permute-done.23.rest_3_ = f32[6,8,128]{2,1,0:T(8,128)S(1)} collective-permute-done((f32[6,8,128]{2,1,0:T(8,128)S(1)}, f32[6,8,128]{2,1,0:T(8,128)S(1)}, u32[]{:S(2)}, u32[]{:S(2)}) %collective-permute-start.23) | collective-permute-done | bytes 24608 | tf_op jit(solution)/shard_map/ppermute | solution.py:661
  103.1 1.9 %collective-permute-start.26 = (f32[22,8,128]{2,1,0:T(8,128)S(1)}, f32[22,8,128]{2,1,0:T(8,128)S(1)}, u32[]{:S(2)}, u32[]{:S(2)}) collective-permute-start(f32[22,8,128]{2,1,0:T(8,128)S(1)} %fusion), channel_id=1, source_target_pairs={{25,24},{24,25},{27,26},{26,27},{29,28},{28,29},{31,30},{30,31}} | collective-permute-start | bytes 270344 | tf_op jit(solution)/shard_map/ppermute | solution.py:822
  105.1 1.3 %collective-permute-done.26 = f32[22,8,128]{2,1,0:T(8,128)S(1)} collective-permute-done((f32[22,8,128]{2,1,0:T(8,128)S(1)}, f32[22,8,128]{2,1,0:T(8,128)S(1)}, u32[]{:S(2)}, u32[]{:S(2)}) %collective-permute-start.26) | collective-permute-done | bytes 90144 | tf_op jit(solution)/shard_map/ppermute | solution.py:822
  106.3 5.6 %chain_3.1 = (f32[3,16,32,128]{3,2,1,0:T(8,128)S(1)}, f32[16,32,128]{2,1,0:T(8,128)}, f32[3,32,64,128]{3,2,1,0:T(8,128)}) custom-call(s32[4]{0:T(128)S(1)} %copy-done.3, f32[3,32,48,128]{3,2,1,0:T(8,128)S(1)} %assemble.1.ge, f32[2,16,48,128]{3,2,1,0:T(8,128)S(1)} %coarse_coefficients.1.coef, ...), custom_call_target="tpu_custom_call", output_to_operand_aliasing={{0}: (4, {})} | custom-call | tf_op jit(solution)/shard_map/chain_3/pallas_call | solution.py:785
  (52 shorter events, 7.4 us)
Async XLA Ops:
  0.0 14.3 %copy-start.3 = (s32[4]{0:T(128)S(1)}, s32[4]{0:T(128)}, u32[]{:S(2)}) copy-start(s32[4]{0:T(128)} %steps.13) | copy-start | bytes 52
  0.9 1.9 %copy-start = (f32[1,3,32,64,128]{4,3,2,1,0:T(8,128)S(1)}, f32[1,3,32,64,128]{4,3,2,1,0:T(8,128)}, u32[]{:S(2)}) copy-start(f32[1,3,32,64,128]{4,3,2,1,0:T(8,128)} %param.4) | copy-start | bytes 9437188
  2.8 11.5 %copy-start.1 = (f32[1,3,32,64,128]{4,3,2,1,0:T(8,128)S(1)}, f32[1,3,32,64,128]{4,3,2,1,0:T(8,128)}, u32[]{:S(2)}) copy-start(f32[1,3,32,64,128]{4,3,2,1,0:T(8,128)} %param.4) | copy-start | bytes 9437188
  3.6 22.4 %collective-permute-start = (f32[25,64,128]{2,1,0:T(8,128)S(1)}, f32[25,64,128]{2,1,0:T(8,128)S(1)}, u32[]{:S(2)}, u32[]{:S(2)}) collective-permute-start(f32[25,64,128]{2,1,0:T(8,128)S(1)} %get-tuple-element.57), channel_id=1, source_target_pairs={{4,0},{5,1},{6,2},{7,3},{0,4},{1,5},{2,6},{3,7},{12,8},{13,9},{14,... | collective-permute-start | bytes 2457608 | tf_op jit(solution)/shard_map/ppermute | solution.py:661
  5.1 5.6 %collective-permute-start.3 = (f32[97,8,128]{2,1,0:T(8,128)S(1)}, f32[97,8,128]{2,1,0:T(8,128)S(1)}, u32[]{:S(2)}, u32[]{:S(2)}) collective-permute-start(f32[97,8,128]{2,1,0:T(8,128)S(1)} %get-tuple-element.60), channel_id=1, source_target_pairs={{1,0},{0,1},{3,2},{2,3},{5,4},{4,5},{7,6},{6,7},{9,8},{8,9},{11,10... | collective-permute-start | bytes 1191944 | tf_op jit(solution)/shard_map/ppermute | solution.py:661
  5.1 9.1 %collective-permute-start.4 = (f32[97,8,128]{2,1,0:T(8,128)S(1)}, f32[97,8,128]{2,1,0:T(8,128)S(1)}, u32[]{:S(2)}, u32[]{:S(2)}) collective-permute-start(f32[97,8,128]{2,1,0:T(8,128)S(1)} %get-tuple-element.61), channel_id=1, source_target_pairs={{2,1},{1,2},{6,5},{5,6},{10,9},{9,10},{14,13},{13,14},{18,17},{17,... | collective-permute-start | bytes 1191944 | tf_op jit(solution)/shard_map/ppermute | solution.py:661
  7.7 18.2 %collective-permute-start.1 = (f32[25,8,128]{2,1,0:T(8,128)S(1)}, f32[25,8,128]{2,1,0:T(8,128)S(1)}, u32[]{:S(2)}, u32[]{:S(2)}) collective-permute-start(f32[25,8,128]{2,1,0:T(8,128)S(1)} %get-tuple-element.58), channel_id=1, source_target_pairs={{5,0},{4,1},{7,2},{6,3},{1,4},{0,5},{3,6},{2,7},{13,8},{12,9},{15,... | collective-permute-start | bytes 307208 | tf_op jit(solution)/shard_map/ppermute | solution.py:661
  7.8 18.2 %collective-permute-start.2 = (f32[25,8,128]{2,1,0:T(8,128)S(1)}, f32[25,8,128]{2,1,0:T(8,128)S(1)}, u32[]{:S(2)}, u32[]{:S(2)}) collective-permute-start(f32[25,8,128]{2,1,0:T(8,128)S(1)} %get-tuple-element.59), channel_id=1, source_target_pairs={{6,1},{5,2},{2,5},{1,6},{14,9},{13,10},{10,13},{9,14},{22,17},{21,... | collective-permute-start | bytes 307208 | tf_op jit(solution)/shard_map/ppermute | solution.py:661
  31.3 27.8 %collective-permute-start.15 = (f32[32,64,128]{2,1,0:T(8,128)S(1)}, f32[32,64,128]{2,1,0:T(8,128)}, u32[]{:S(2)}, u32[]{:S(2)}) collective-permute-start(f32[32,64,128]{2,1,0:T(8,128)S(1)} %get-tuple-element.101.w2), channel_id=1, source_target_pairs={{8,16},{16,24},{9,17},{17,25},{10,18},{18,26},{11,19},{19,27},{12,... | collective-permute-start | bytes 3145736 | tf_op jit(solution)/shard_map/ppermute | solution.py:737
  32.6 10.5 %collective-permute-start.5 = (f32[12,32,128]{2,1,0:T(8,128)}, f32[12,32,128]{2,1,0:T(8,128)}, u32[]{:S(2)}, u32[]{:S(2)}) collective-permute-start(f32[12,32,128]{2,1,0:T(8,128)} %get-tuple-element.67), channel_id=1, source_target_pairs={{4,0},{5,1},{6,2},{7,3},{0,4},{1,5},{2,6},{3,7},{12,8},{13,9},{14,... | collective-permute-start | bytes 589832 | tf_op jit(solution)/shard_map/ppermute | solution.py:661
  34.0 9.0 %collective-permute-start.7 = (f32[48,8,128]{2,1,0:T(8,128)}, f32[48,8,128]{2,1,0:T(8,128)}, u32[]{:S(2)}, u32[]{:S(2)}) collective-permute-start(f32[48,8,128]{2,1,0:T(8,128)} %get-tuple-element.69), channel_id=1, source_target_pairs={{1,0},{0,1},{3,2},{2,3},{5,4},{4,5},{7,6},{6,7},{9,8},{8,9},{11,10... | collective-permute-start | bytes 589832 | tf_op jit(solution)/shard_map/ppermute | solution.py:661
  34.7 8.4 %collective-permute-start.8 = (f32[48,8,128]{2,1,0:T(8,128)}, f32[48,8,128]{2,1,0:T(8,128)}, u32[]{:S(2)}, u32[]{:S(2)}) collective-permute-start(f32[48,8,128]{2,1,0:T(8,128)} %get-tuple-element.70), channel_id=1, source_target_pairs={{2,1},{1,2},{6,5},{5,6},{10,9},{9,10},{14,13},{13,14},{18,17},{17,... | collective-permute-start | bytes 589832 | tf_op jit(solution)/shard_map/ppermute | solution.py:661
  36.7 6.3 %collective-permute-start.6 = (f32[12,8,128]{2,1,0:T(8,128)S(1)}, f32[12,8,128]{2,1,0:T(8,128)S(1)}, u32[]{:S(2)}, u32[]{:S(2)}) collective-permute-start(f32[12,8,128]{2,1,0:T(8,128)S(1)} %get-tuple-element.68), channel_id=1, source_target_pairs={{6,1},{5,2},{2,5},{1,6},{14,9},{13,10},{10,13},{9,14},{22,17},{21,... | collective-permute-start | bytes 147464 | tf_op jit(solution)/shard_map/ppermute | solution.py:661
  43.8 1.2 %collective-permute-start.9 = (f32[12,8,128]{2,1,0:T(8,128)S(1)}, f32[12,8,128]{2,1,0:T(8,128)S(1)}, u32[]{:S(2)}, u32[]{:S(2)}) collective-permute-start(f32[12,8,128]{2,1,0:T(8,128)S(1)} %constant_dynamic-slice_fusion), channel_id=1, source_target_pairs={{1,0},{0,1},{3,2},{2,3},{5,4},{4,5},{7,6},{6,7},{9,8},{8,9},{11,10... | collective-permute-start | bytes 147464 | tf_op jit(solution)/shard_map/ppermute | solution.py:661
  47.6 2.7 %collective-permute-start.10 = (f32[16,32,128]{2,1,0:T(8,128)S(1)}, f32[16,32,128]{2,1,0:T(8,128)S(1)}, u32[]{:S(2)}, u32[]{:S(2)}) collective-permute-start(f32[16,32,128]{2,1,0:T(8,128)S(1)} %get-tuple-element.78), channel_id=1, source_target_pairs={{0,8},{1,9},{2,10},{3,11},{4,12},{5,13},{6,14},{7,15}} | collective-permute-start | bytes 786440 | tf_op jit(solution)/shard_map/ppermute | solution.py:798
  48.3 2.0 %collective-permute-start.11 = (f32[6,32,128]{2,1,0:T(8,128)S(1)}, f32[6,32,128]{2,1,0:T(8,128)S(1)}, u32[]{:S(2)}, u32[]{:S(2)}) collective-permute-start(f32[6,32,128]{2,1,0:T(8,128)S(1)} %get-tuple-element.79), channel_id=1, source_target_pairs={{4,8},{5,9},{6,10},{7,11},{0,12},{1,13},{2,14},{3,15}} | collective-permute-start | bytes 294920 | tf_op jit(solution)/shard_map/ppermute | solution.py:661
  49.0 1.4 %collective-permute-start.13 = (f32[16,8,128]{2,1,0:T(8,128)S(1)}, f32[16,8,128]{2,1,0:T(8,128)S(1)}, u32[]{:S(2)}, u32[]{:S(2)}) collective-permute-start(f32[16,8,128]{2,1,0:T(8,128)S(1)} %get-tuple-element.81), channel_id=1, source_target_pairs={{2,9},{1,10},{6,13},{5,14}} | collective-permute-start | bytes 196616 | tf_op jit(solution)/shard_map/ppermute | solution.py:661
  49.7 0.7 collective-permute-start.12
  50.4 18.9 %collective-permute-start.25 = (f32[32,64,128]{2,1,0:T(8,128)S(1)}, f32[32,64,128]{2,1,0:T(8,128)S(1)}, u32[]{:S(2)}, u32[]{:S(2)}) collective-permute-start(f32[32,64,128]{2,1,0:T(8,128)S(1)} %get-tuple-element.101.w2), channel_id=1, source_target_pairs={{0,8},{1,9},{2,10},{3,11},{4,12},{5,13},{6,14},{7,15}} | collective-permute-start | bytes 3145736 | tf_op jit(solution)/shard_map/ppermute | solution.py:814
  51.1 0.7 collective-permute-start.14
  59.7 2.9 %collective-permute-start.16 = (f32[16,32,128]{2,1,0:T(8,128)S(1)}, f32[16,32,128]{2,1,0:T(8,128)S(1)}, u32[]{:S(2)}, u32[]{:S(2)}) collective-permute-start(f32[16,32,128]{2,1,0:T(8,128)S(1)} %get-tuple-element.88), channel_id=1, source_target_pairs={{8,16},{9,17},{10,18},{11,19},{12,20},{13,21},{14,22},{15,23}} | collective-permute-start | bytes 786440 | tf_op jit(solution)/shard_map/ppermute | solution.py:798
  60.4 2.2 %collective-permute-start.17 = (f32[6,32,128]{2,1,0:T(8,128)S(1)}, f32[6,32,128]{2,1,0:T(8,128)S(1)}, u32[]{:S(2)}, u32[]{:S(2)}) collective-permute-start(f32[6,32,128]{2,1,0:T(8,128)S(1)} %get-tuple-element.89), channel_id=1, source_target_pairs={{12,16},{13,17},{14,18},{15,19},{8,20},{9,21},{10,22},{11,23}} | collective-permute-start | bytes 294920 | tf_op jit(solution)/shard_map/ppermute | solution.py:661
  61.1 1.5 %collective-permute-start.19 = (f32[16,8,128]{2,1,0:T(8,128)S(1)}, f32[16,8,128]{2,1,0:T(8,128)S(1)}, u32[]{:S(2)}, u32[]{:S(2)}) collective-permute-start(f32[16,8,128]{2,1,0:T(8,128)S(1)} %get-tuple-element.91), channel_id=1, source_target_pairs={{10,17},{9,18},{14,21},{13,22}} | collective-permute-start | bytes 196616 | tf_op jit(solution)/shard_map/ppermute | solution.py:661
  61.8 7.6 %copy-start.2 = (f32[1,3,32,64,128]{4,3,2,1,0:T(8,128)S(1)}, f32[1,3,32,64,128]{4,3,2,1,0:T(8,128)}, u32[]{:S(2)}) copy-start(f32[1,3,32,64,128]{4,3,2,1,0:T(8,128)} %param.4) | copy-start | bytes 9437188
  61.8 0.8 collective-permute-start.18
  62.6 0.8 collective-permute-start.20
  64.1 39.0 %collective-permute-start.21 = (f32[16,32,128]{2,1,0:T(8,128)S(1)}, f32[16,32,128]{2,1,0:T(8,128)S(1)}, u32[]{:S(2)}, u32[]{:S(2)}) collective-permute-start(f32[16,32,128]{2,1,0:T(8,128)S(1)} %get-tuple-element.97._), channel_id=1, source_target_pairs={{16,24},{17,25},{18,26},{19,27},{20,28},{21,29},{22,30},{23,31}} | collective-permute-start | bytes 786440 | tf_op jit(solution)/shard_map/ppermute | solution.py:798
  65.4 37.7 %collective-permute-start.22 = (f32[6,32,128]{2,1,0:T(8,128)S(1)}, f32[6,32,128]{2,1,0:T(8,128)S(1)}, u32[]{:S(2)}, u32[]{:S(2)}) collective-permute-start(f32[6,32,128]{2,1,0:T(8,128)S(1)} %get-tuple-element.98), channel_id=1, source_target_pairs={{20,24},{21,25},{22,26},{23,27},{16,28},{17,29},{18,30},{19,31}} | collective-permute-start | bytes 294920 | tf_op jit(solution)/shard_map/ppermute | solution.py:661
  66.7 36.4 %collective-permute-start.24 = (f32[16,8,128]{2,1,0:T(8,128)S(1)}, f32[16,8,128]{2,1,0:T(8,128)S(1)}, u32[]{:S(2)}, u32[]{:S(2)}) collective-permute-start(f32[16,8,128]{2,1,0:T(8,128)S(1)} %get-tuple-element.100), channel_id=1, source_target_pairs={{18,25},{17,26},{22,29},{21,30}} | collective-permute-start | bytes 196616 | tf_op jit(solution)/shard_map/ppermute | solution.py:661
  68.0 35.1 %collective-permute-start.23 = (f32[6,8,128]{2,1,0:T(8,128)S(1)}, f32[6,8,128]{2,1,0:T(8,128)S(1)}, u32[]{:S(2)}, u32[]{:S(2)}) collective-permute-start(f32[6,8,128]{2,1,0:T(8,128)S(1)} %get-tuple-element.99), channel_id=1, source_target_pairs={{22,25},{21,26},{18,29},{17,30}} | collective-permute-start | bytes 73736 | tf_op jit(solution)/shard_map/ppermute | solution.py:661
  103.1 3.2 %collective-permute-start.26 = (f32[22,8,128]{2,1,0:T(8,128)S(1)}, f32[22,8,128]{2,1,0:T(8,128)S(1)}, u32[]{:S(2)}, u32[]{:S(2)}) collective-permute-start(f32[22,8,128]{2,1,0:T(8,128)S(1)} %fusion), channel_id=1, source_target_pairs={{25,24},{24,25},{27,26},{26,27},{29,28},{28,29},{31,30},{30,31}} | collective-permute-start | bytes 270344 | tf_op jit(solution)/shard_map/ppermute | solution.py:822

commit v5 on v4

--- a/solution.py
+++ b/solution.py
@@ -452,12 +452,15 @@
     msgs, (gp, ge), sems = rest[:nm], rest[nm : nm + 2], rest[nm + 2]
     cx, cy = co.shape[1], co.shape[2]
 
-    def clear(i, _):
+    def clear(i):
         for f in range(3):
             ge[f, i] = jnp.zeros(ge.shape[2:], f32)
-        return 0
-
-    lax.fori_loop(0, ge.shape[1], clear, 0)
+
+    for i in (*range(CW), *range(CW + cx, ge.shape[1])):
+        clear(i)
+    if len(colors(lax.axis_size("gy"))) < 2:
+        for i in range(CW, CW + cx):
+            clear(i)
     fields = ((0, CW), (1, CN), (2, CN))
     pairs = []
 
@@ -476,12 +479,15 @@
     run_copies(pairs, sems)
 
     def order(i, _):
-        at = pl.ds(2 * i, 2)
+        at = pl.ds(8 * i, 8)
         for f in range(3):
             gp[f, at] = permuted(ge, f, at)
         return 0
 
-    lax.fori_loop(0, ge.shape[1] // 2, order, 0)
+    lax.fori_loop(0, ge.shape[1] // 8, order, 0)
+    for x in range(ge.shape[1] // 8 * 8, ge.shape[1]):
+        for f in range(3):
+            gp[f, pl.ds(x, 1)] = permuted(ge, f, pl.ds(x, 1))
 
 
 def chain_kernel(turn, keys, arrive, last, steps, ge, coef, co, *rest):
@@ -508,6 +514,37 @@
     h, a = times(steps, sect)
     ngx, ngy = lax.axis_size("gx"), lax.axis_size("gy")
 
+    step = 1
+    masks = wide_masks(step, ye)
+
+    def rows(r, body):
+        n = cx + r * min(ngx - 1, 2)
+        sweep_rows(cx, CW, r, n, lambda x: [body(x + i) for i in range(0, n, step)])
+
+    def coefs(n, x):
+        return jnp.stack([coef[n, lax.div(x + i, 2)] for i in range(step)])
+
+    def jacobi(src, x):
+        _, p, z = neighbours(src[pl.ds(x - 1, step + 2)], masks)
+        return q0[pl.ds(x, step)] + coefs(0, x) * (0.25 * p + z)
+
+    def into(dst, src):
+        def body(x):
+            dst[pl.ds(x, step)] = jacobi(src, x)
+        return body
+
+    def start(x):
+        at = pl.ds(x, step)
+        r = ge[0, at]
+        if not first:
+            v = permuted(cin, at)
+            r = v + a * reaction(v) + r
+        q0[at] = r * coefs(1, x)
+
+    def keep(m, value):
+        for i in range(0, cx, 4):
+            state[m, i : i + 4] = value(slice(CW + i, CW + i + 4), slice(i, i + 4))
+
     @pl.when(sect == turn)
     def _():
         clear_walls(CW, cx, (q0, qa, qb))
@@ -525,33 +562,6 @@
                 ys = pl.ds(YW, cy) if l is None else pl.ds(pl.multiple_of(pick(upper("gy", l), YW + cy, 0), 8), YW)
                 pairs.append((m, cin.at[xs, ys, :]))
             run_copies(pairs, sems)
-        step = 1
-        masks = wide_masks(step, ye)
-
-        def rows(r, body):
-            n = cx + r * min(ngx - 1, 2)
-            sweep_rows(cx, CW, r, n, lambda x: [body(x + i) for i in range(0, n, step)])
-
-        def coefs(n, x):
-            return jnp.stack([coef[n, lax.div(x + i, 2)] for i in range(step)])
-
-        def jacobi(src, x):
-            _, p, z = neighbours(src[pl.ds(x - 1, step + 2)], masks)
-            return q0[pl.ds(x, step)] + coefs(0, x) * (0.25 * p + z)
-
-        def into(dst, src):
-            def body(x):
-                dst[pl.ds(x, step)] = jacobi(src, x)
-            return body
-
-        def start(x):
-            at = pl.ds(x, step)
-            r = ge[0, at]
-            if not first:
-                v = permuted(cin, at)
-                r = v + a * reaction(v) + r
-            q0[at] = r * coefs(1, x)
-
         rows(6, start)
         rows(5, into(qa, q0))
         rows(4, into(qb, qa))
@@ -563,6 +573,13 @@
             store_plain(plain, (0, at), w)
 
         rows(3, middle)
+        keep(0, lambda x, at: co[3, at] if first else cin[x, YW : YW + cy])
+        keep(1, lambda x, at: plain[0, x, YW : YW + cy])
+
+    copies = correct((0, 1), ready, state, final, stage, finals) if last else []
+
+    @pl.when(sect == turn)
+    def _():
         rows(2, into(qa, q0))
         rows(1, into(qb, qa))
 
@@ -571,22 +588,20 @@
 
         rows(0, end)
 
-        def keep(i, _):
-            x, at = pl.ds(CW + 4 * i, 4), pl.ds(4 * i, 4)
-            state[0, at] = co[3, at] if first else cin[x, YW : YW + cy]
-            state[1, at] = plain[0, x, YW : YW + cy]
-            state[2, at] = co[4, at] + plain[1, x, YW : YW + cy]
-            whole[at] = state[2, at]
-            return 0
-
-        lax.fori_loop(0, cx // 4, keep, 0)
+        def value(x, at):
+            v = co[4, at] + plain[1, x, YW : YW + cy]
+            whole[at] = v
+            return v
+
+        keep(2, value)
         for (k, l), o in zip(keys, couts):
             xs = pl.ds(0, cx) if k is None else pl.ds(pick(upper("gx", k), cx - CW, 0), CW)
             ys = pl.ds(0, cy) if l is None else pl.ds(pl.multiple_of(pick(upper("gy", l), cy - YW, 0), 8), YW)
             o[...] = state[2, xs, ys, :]
 
     if last:
-        correct(ready, state, final, stage, finals)
+        for c in copies + correct((2,), ready, state, final, stage, finals):
+            c.wait()
 
 
 PIECES = 4
@@ -621,29 +636,25 @@
     lax.fori_loop(0, u0.shape[0] // 2, row, 0)
 
 
-def correct(ready, state, out, stage, sems):
+def correct(nodes, ready, state, out, stage, sems):
     nx, ny = ready.shape[1], ready.shape[2]
-    ft, ct = ny // 8, ny // 16
     rows = nx // PIECES
     copies = []
-    for m in range(3):
+    for m in nodes:
         for p in range(PIECES):
-
-            def row(i, _):
-                at = pl.ds(2 * i, 2)
-                for t in range(ct):
-                    c = state[m, i, pl.ds(t, 8, stride=ct), :]
-                    for d in range(2):
-                        to = pl.ds(2 * t + d, 8, stride=ft)
-                        stage[m, at, to, :] = ready[m, at, to, :] + c
-                return 0
-
-            lax.fori_loop(p * rows // 2, (p + 1) * rows // 2, row, 0)
+            mine = range(p * rows // 2, (p + 1) * rows // 2)
+            for i in mine:
+                c = state[m, i]
+                for d in range(2):
+                    stage[m, 2 * i, pl.ds(d, ny // 2, stride=2), :] = c
+            for i in mine:
+                c = stage[m, 2 * i]
+                for d in range(2):
+                    stage[m, 2 * i + d] = ready[m, 2 * i + d] + c
             part = pl.ds(p * rows, rows)
             copies.append(pltpu.make_async_copy(stage.at[m, part], out.at[m, part], sems.at[m * PIECES + p]))
             copies[-1].start()
-    for c in copies:
-        c.wait()
+    return copies
 
 
 def per_device(sizes, fine_nodes, section_steps, diffusivities, tile_kinds):

time: 113 us -> 112 us (level)
  no operation moved by 1% of the time
where the time goes in v5:
time: 112 us; the launch traced here: 111 us
  waiting for transfers between devices  46.8 us (42%)
  starting transfers between devices  30.8 us (28%)
  Pallas kernels  29.4 us (26%)
  local copies, waits for them, and re-layouts  2.74 us (2%)
    ppermute x19, waiting for transfers between devices, send(): lax.ppermute(v, AXES, routes(sizes, k, l, hop))  38.1 us
    ppermute x19, starting transfers between devices, send(): lax.ppermute(v, AXES, routes(sizes, k, l, hop))  22.7 us
    pallas_call x1, Pallas kernels, per_device(): pl.pallas_call(functools.partial(inner_kernel, ykeys, local, seams), out_...  11.5 us
    ppermute x1, waiting for transfers between devices, per_device(): arrived = lax.ppermute(w2, 'tm', [(i, i + 1) for i in range(1, nt - 1)])  7.46 us
    pallas_call x4, Pallas kernels, per_device(): pl.pallas_call(functools.partial(chain_kernel, n, sent, arrive if n else...  6.99 us
    pallas_call x1, Pallas kernels, per_device(): pl.pallas_call(functools.partial(seam_kernel, keys, now, local, seams), o...  5.31 us
    ppermute x3, starting transfers between devices, per_device(): strip = lax.ppermute(strip, AXES, pairs)  3.38 us
    ppermute x3, starting transfers between devices, per_device(): own = lax.ppermute(whole, AXES, routes(sizes, None, None, n))  2.65 us
  transfers between devices with their start and end apart: 27, of which 7 were waited for; matrix products, arithmetic and copies ran while one was open for 1% of the time, Pallas kernels for 17%

profile of v5, /device:TPU:26, one launch (start us, length us, event | category | flops | bytes accessed | tf_op | source)
XLA Modules:
  0.0 111.3 jit_solution(5201284214664446583)
XLA Ops:
  0.0 0.9 select_reduce_fusion
  0.9 1.9 %copy-done = f32[1,3,32,64,128]{4,3,2,1,0:T(8,128)S(1)} copy-done((f32[1,3,32,64,128]{4,3,2,1,0:T(8,128)S(1)}, f32[1,3,32,64,128]{4,3,2,1,0:T(8,128)}, u32[]{:S(2)}) %copy-start) | copy-done | bytes 3145752
  2.8 0.8 pack.1
  3.6 1.6 %collective-permute-start = (f32[25,64,128]{2,1,0:T(8,128)S(1)}, f32[25,64,128]{2,1,0:T(8,128)S(1)}, u32[]{:S(2)}, u32[]{:S(2)}) collective-permute-start(f32[25,64,128]{2,1,0:T(8,128)S(1)} %get-tuple-element.57), channel_id=1, source_target_pairs={{4,0},{5,1},{6,2},{7,3},{0,4},{1,5},{2,6},{3,7},{12,8},{13,9},{14,... | collective-permute-start | bytes 2457608 | tf_op jit(solution)/shard_map/ppermute | solution.py:672
  5.1 2.5 %collective-permute-start.4 = (f32[97,8,128]{2,1,0:T(8,128)S(1)}, f32[97,8,128]{2,1,0:T(8,128)S(1)}, u32[]{:S(2)}, u32[]{:S(2)}) collective-permute-start(f32[97,8,128]{2,1,0:T(8,128)S(1)} %get-tuple-element.61), channel_id=1, source_target_pairs={{2,1},{1,2},{6,5},{5,6},{10,9},{9,10},{14,13},{13,14},{18,17},{17,... | collective-permute-start | bytes 1191944 | tf_op jit(solution)/shard_map/ppermute | solution.py:672
  7.8 3.0 %collective-permute-start.2 = (f32[25,8,128]{2,1,0:T(8,128)S(1)}, f32[25,8,128]{2,1,0:T(8,128)S(1)}, u32[]{:S(2)}, u32[]{:S(2)}) collective-permute-start(f32[25,8,128]{2,1,0:T(8,128)S(1)} %get-tuple-element.59), channel_id=1, source_target_pairs={{6,1},{5,2},{2,5},{1,6},{14,9},{13,10},{10,13},{9,14},{22,17},{21,... | collective-permute-start | bytes 307208 | tf_op jit(solution)/shard_map/ppermute | solution.py:672
  10.7 3.5 %collective-permute-done.4.rest_1_.rest_4_ = f32[97,8,128]{2,1,0:T(8,128)S(1)} collective-permute-done((f32[97,8,128]{2,1,0:T(8,128)S(1)}, f32[97,8,128]{2,1,0:T(8,128)S(1)}, u32[]{:S(2)}, u32[]{:S(2)}) %collective-permute-start.4) | collective-permute-done | bytes 397344 | tf_op jit(solution)/shard_map/ppermute | solution.py:672
  14.3 11.5 %fine_inner.1 = (f32[32,64,128]{2,1,0:T(8,128)S(1)}, f32[32,64,128]{2,1,0:T(8,128)S(1)}, f32[5,16,32,128]{3,2,1,0:T(8,128)S(1)}, f32[1,10,20,80,128]{4,3,2,1,0:T(8,128)S(1)}) custom-call(s32[4]{0:T(128)S(1)} %copy-done.3, f32[3,32,64,128]{3,2,1,0:T(8,128)S(1)} %bitcast.3, f32[8,128]{1,0:T(8,128)S(1)} %pad.4.table, ...), custom_call_target="tpu_custom_call" | custom-call | flops 52428800 | bytes 40000000 | tf_op jit(solution)/shard_map/fine_inner/pallas_call | solution.py:710
  25.9 5.3 %fine_seam.1 = (f32[32,64,128]{2,1,0:T(8,128)S(1)}, f32[32,64,128]{2,1,0:T(8,128)S(1)}, f32[5,16,32,128]{3,2,1,0:T(8,128)S(1)}, f32[1,10,20,80,128]{4,3,2,1,0:T(...) custom-call(s32[4]{0:T(128)S(1)} %copy-done.3, ...), custom_call_target="tpu_custom_call", output_to_operand_aliasing={{0}: (7, {}), {1}: (8, {}), {2}: (9, {}), {3}: (10, {})} | custom-call | tf_op jit(solution)/shard_map/fine_seam/pallas_call | solution.py:729
  31.3 1.3 %collective-permute-start.15 = (f32[32,64,128]{2,1,0:T(8,128)S(1)}, f32[32,64,128]{2,1,0:T(8,128)}, u32[]{:S(2)}, u32[]{:S(2)}) collective-permute-start(f32[32,64,128]{2,1,0:T(8,128)S(1)} %get-tuple-element.101.w2), channel_id=1, source_target_pairs={{8,16},{16,24},{9,17},{17,25},{10,18},{18,26},{11,19},{19,27},{12,... | collective-permute-start | bytes 3145736 | tf_op jit(solution)/shard_map/ppermute | solution.py:748
  32.6 1.4 %collective-permute-start.5 = (f32[12,32,128]{2,1,0:T(8,128)}, f32[12,32,128]{2,1,0:T(8,128)}, u32[]{:S(2)}, u32[]{:S(2)}) collective-permute-start(f32[12,32,128]{2,1,0:T(8,128)} %get-tuple-element.67), channel_id=1, source_target_pairs={{4,0},{5,1},{6,2},{7,3},{0,4},{1,5},{2,6},{3,7},{12,8},{13,9},{14,... | collective-permute-start | bytes 589832 | tf_op jit(solution)/shard_map/ppermute | solution.py:672
  34.7 2.0 %collective-permute-start.8 = (f32[48,8,128]{2,1,0:T(8,128)}, f32[48,8,128]{2,1,0:T(8,128)}, u32[]{:S(2)}, u32[]{:S(2)}) collective-permute-start(f32[48,8,128]{2,1,0:T(8,128)} %get-tuple-element.70), channel_id=1, source_target_pairs={{2,1},{1,2},{6,5},{5,6},{10,9},{9,10},{14,13},{13,14},{18,17},{17,... | collective-permute-start | bytes 589832 | tf_op jit(solution)/shard_map/ppermute | solution.py:672
  36.7 3.5 %collective-permute-start.6 = (f32[12,8,128]{2,1,0:T(8,128)S(1)}, f32[12,8,128]{2,1,0:T(8,128)S(1)}, u32[]{:S(2)}, u32[]{:S(2)}) collective-permute-start(f32[12,8,128]{2,1,0:T(8,128)S(1)} %get-tuple-element.68), channel_id=1, source_target_pairs={{6,1},{5,2},{2,5},{1,6},{14,9},{13,10},{10,13},{9,14},{22,17},{21,... | collective-permute-start | bytes 147464 | tf_op jit(solution)/shard_map/ppermute | solution.py:672
  40.2 2.8 %collective-permute-done.6.rest_2_ = f32[12,8,128]{2,1,0:T(8,128)S(1)} collective-permute-done((f32[12,8,128]{2,1,0:T(8,128)S(1)}, f32[12,8,128]{2,1,0:T(8,128)S(1)}, u32[]{:S(2)}, u32[]{:S(2)}) %collective-permute-start.6) | collective-permute-done | bytes 49184 | tf_op jit(solution)/shard_map/ppermute | solution.py:672
  43.0 0.8 constant_dynamic-slice_fusion
  43.8 0.7 coarse_coefficients.1.coef
  45.1 1.6 %assemble.1.ge = f32[3,32,48,128]{3,2,1,0:T(8,128)S(1)} custom-call(f32[5,16,32,128]{3,2,1,0:T(8,128)S(1)} %get-tuple-element.66.co, f32[12,32,128]{2,1,0:T(8,128)} %collective-permute-done.5.rest_0_, f32[12,8,128]{2,1,0:T(8,128)S(1)} %collective-permute-done.9.rest_1_, f32[12,8,128]{2,1,0:T(8,128)S(1)} %collective-permute-done.6.rest_2_, ...), custom_call_target="tpu_custom_call" | custom-call | tf_op jit(solution)/shard_map/assemble/pallas_call | solution.py:761
  46.6 0.8 chain_0.1
  47.4 0.7 collective-permute-start.10
  50.2 0.7 collective-permute-start.25
  51.7 7.5 %collective-permute-done.15.rest_7_.arrived = f32[32,64,128]{2,1,0:T(8,128)} collective-permute-done((f32[32,64,128]{2,1,0:T(8,128)S(1)}, f32[32,64,128]{2,1,0:T(8,128)}, u32[]{:S(2)}, u32[]{:S(2)}) %collective-permute-start.15) | collective-permute-done | bytes 1048608 | tf_op jit(solution)/shard_map/ppermute | solution.py:748
  61.8 0.8 collective-permute-start.18
  62.6 0.8 collective-permute-start.20
  64.1 1.3 %collective-permute-start.21 = (f32[16,32,128]{2,1,0:T(8,128)S(1)}, f32[16,32,128]{2,1,0:T(8,128)S(1)}, u32[]{:S(2)}, u32[]{:S(2)}) collective-permute-start(f32[16,32,128]{2,1,0:T(8,128)S(1)} %get-tuple-element.97._), channel_id=1, source_target_pairs={{16,24},{17,25},{18,26},{19,27},{20,28},{21,29},{22,30},{23,31}} | collective-permute-start | bytes 786440 | tf_op jit(solution)/shard_map/ppermute | solution.py:809
  65.4 1.3 %collective-permute-start.22 = (f32[6,32,128]{2,1,0:T(8,128)S(1)}, f32[6,32,128]{2,1,0:T(8,128)S(1)}, u32[]{:S(2)}, u32[]{:S(2)}) collective-permute-start(f32[6,32,128]{2,1,0:T(8,128)S(1)} %get-tuple-element.98), channel_id=1, source_target_pairs={{20,24},{21,25},{22,26},{23,27},{16,28},{17,29},{18,30},{19,31}} | collective-permute-start | bytes 294920 | tf_op jit(solution)/shard_map/ppermute | solution.py:672
  66.7 1.3 %collective-permute-start.24 = (f32[16,8,128]{2,1,0:T(8,128)S(1)}, f32[16,8,128]{2,1,0:T(8,128)S(1)}, u32[]{:S(2)}, u32[]{:S(2)}) collective-permute-start(f32[16,8,128]{2,1,0:T(8,128)S(1)} %get-tuple-element.100), channel_id=1, source_target_pairs={{18,25},{17,26},{22,29},{21,30}} | collective-permute-start | bytes 196616 | tf_op jit(solution)/shard_map/ppermute | solution.py:672
  68.0 1.3 %collective-permute-start.23 = (f32[6,8,128]{2,1,0:T(8,128)S(1)}, f32[6,8,128]{2,1,0:T(8,128)S(1)}, u32[]{:S(2)}, u32[]{:S(2)}) collective-permute-start(f32[6,8,128]{2,1,0:T(8,128)S(1)} %get-tuple-element.99), channel_id=1, source_target_pairs={{22,25},{21,26},{18,29},{17,30}} | collective-permute-start | bytes 73736 | tf_op jit(solution)/shard_map/ppermute | solution.py:672
  69.3 2.5 %prepare.1.rest_7_ = f32[3,32,64,128]{3,2,1,0:T(8,128)S(1)} custom-call(f32[3,32,64,128]{3,2,1,0:T(8,128)S(1)} %bitcast.4, f32[32,64,128]{2,1,0:T(8,128)} %collective-permute-done.15.rest_7_.arrived, f32[32,64,128]{2,1,0:T(8,128)S(1)} %collective-permute-done.25.early, f32[32,64,128]{2,1,0:T(8,128)S(1)} %get-tuple-element.102.w1, ...), custom_call_target="tpu_custom_call" | custom-call | tf_op jit(solution)/shard_map/prepare/pallas_call | solution.py:812
  71.9 31.1 %collective-permute-done.23.rest_3_ = f32[6,8,128]{2,1,0:T(8,128)S(1)} collective-permute-done((f32[6,8,128]{2,1,0:T(8,128)S(1)}, f32[6,8,128]{2,1,0:T(8,128)S(1)}, u32[]{:S(2)}, u32[]{:S(2)}) %collective-permute-start.23) | collective-permute-done | bytes 24608 | tf_op jit(solution)/shard_map/ppermute | solution.py:672
  103.0 1.9 %collective-permute-start.26 = (f32[22,8,128]{2,1,0:T(8,128)S(1)}, f32[22,8,128]{2,1,0:T(8,128)S(1)}, u32[]{:S(2)}, u32[]{:S(2)}) collective-permute-start(f32[22,8,128]{2,1,0:T(8,128)S(1)} %fusion), channel_id=1, source_target_pairs={{25,24},{24,25},{27,26},{26,27},{29,28},{28,29},{31,30},{30,31}} | collective-permute-start | bytes 270344 | tf_op jit(solution)/shard_map/ppermute | solution.py:833
  104.9 1.3 %collective-permute-done.26 = f32[22,8,128]{2,1,0:T(8,128)S(1)} collective-permute-done((f32[22,8,128]{2,1,0:T(8,128)S(1)}, f32[22,8,128]{2,1,0:T(8,128)S(1)}, u32[]{:S(2)}, u32[]{:S(2)}) %collective-permute-start.26) | collective-permute-done | bytes 90144 | tf_op jit(solution)/shard_map/ppermute | solution.py:833
  106.2 5.0 %chain_3.1 = (f32[3,16,32,128]{3,2,1,0:T(8,128)S(1)}, f32[16,32,128]{2,1,0:T(8,128)}, f32[3,32,64,128]{3,2,1,0:T(8,128)}) custom-call(s32[4]{0:T(128)S(1)} %copy-done.3, f32[3,32,48,128]{3,2,1,0:T(8,128)S(1)} %assemble.1.ge, f32[2,16,48,128]{3,2,1,0:T(8,128)S(1)} %coarse_coefficients.1.coef, ...), custom_call_target="tpu_custom_call", output_to_operand_aliasing={{0}: (4, {})} | custom-call | tf_op jit(solution)/shard_map/chain_3/pallas_call | solution.py:796
  (52 shorter events, 7.4 us)
Async XLA Ops:
  0.0 14.3 %copy-start.3 = (s32[4]{0:T(128)S(1)}, s32[4]{0:T(128)}, u32[]{:S(2)}) copy-start(s32[4]{0:T(128)} %steps.13) | copy-start | bytes 52
  0.9 1.9 %copy-start = (f32[1,3,32,64,128]{4,3,2,1,0:T(8,128)S(1)}, f32[1,3,32,64,128]{4,3,2,1,0:T(8,128)}, u32[]{:S(2)}) copy-start(f32[1,3,32,64,128]{4,3,2,1,0:T(8,128)} %param.4) | copy-start | bytes 9437188
  2.8 11.5 %copy-start.1 = (f32[1,3,32,64,128]{4,3,2,1,0:T(8,128)S(1)}, f32[1,3,32,64,128]{4,3,2,1,0:T(8,128)}, u32[]{:S(2)}) copy-start(f32[1,3,32,64,128]{4,3,2,1,0:T(8,128)} %param.4) | copy-start | bytes 9437188
  3.6 22.4 %collective-permute-start = (f32[25,64,128]{2,1,0:T(8,128)S(1)}, f32[25,64,128]{2,1,0:T(8,128)S(1)}, u32[]{:S(2)}, u32[]{:S(2)}) collective-permute-start(f32[25,64,128]{2,1,0:T(8,128)S(1)} %get-tuple-element.57), channel_id=1, source_target_pairs={{4,0},{5,1},{6,2},{7,3},{0,4},{1,5},{2,6},{3,7},{12,8},{13,9},{14,... | collective-permute-start | bytes 2457608 | tf_op jit(solution)/shard_map/ppermute | solution.py:672
  5.1 5.6 %collective-permute-start.3 = (f32[97,8,128]{2,1,0:T(8,128)S(1)}, f32[97,8,128]{2,1,0:T(8,128)S(1)}, u32[]{:S(2)}, u32[]{:S(2)}) collective-permute-start(f32[97,8,128]{2,1,0:T(8,128)S(1)} %get-tuple-element.60), channel_id=1, source_target_pairs={{1,0},{0,1},{3,2},{2,3},{5,4},{4,5},{7,6},{6,7},{9,8},{8,9},{11,10... | collective-permute-start | bytes 1191944 | tf_op jit(solution)/shard_map/ppermute | solution.py:672
  5.1 9.1 %collective-permute-start.4 = (f32[97,8,128]{2,1,0:T(8,128)S(1)}, f32[97,8,128]{2,1,0:T(8,128)S(1)}, u32[]{:S(2)}, u32[]{:S(2)}) collective-permute-start(f32[97,8,128]{2,1,0:T(8,128)S(1)} %get-tuple-element.61), channel_id=1, source_target_pairs={{2,1},{1,2},{6,5},{5,6},{10,9},{9,10},{14,13},{13,14},{18,17},{17,... | collective-permute-start | bytes 1191944 | tf_op jit(solution)/shard_map/ppermute | solution.py:672
  7.7 18.2 %collective-permute-start.1 = (f32[25,8,128]{2,1,0:T(8,128)S(1)}, f32[25,8,128]{2,1,0:T(8,128)S(1)}, u32[]{:S(2)}, u32[]{:S(2)}) collective-permute-start(f32[25,8,128]{2,1,0:T(8,128)S(1)} %get-tuple-element.58), channel_id=1, source_target_pairs={{5,0},{4,1},{7,2},{6,3},{1,4},{0,5},{3,6},{2,7},{13,8},{12,9},{15,... | collective-permute-start | bytes 307208 | tf_op jit(solution)/shard_map/ppermute | solution.py:672
  7.8 18.2 %collective-permute-start.2 = (f32[25,8,128]{2,1,0:T(8,128)S(1)}, f32[25,8,128]{2,1,0:T(8,128)S(1)}, u32[]{:S(2)}, u32[]{:S(2)}) collective-permute-start(f32[25,8,128]{2,1,0:T(8,128)S(1)} %get-tuple-element.59), channel_id=1, source_target_pairs={{6,1},{5,2},{2,5},{1,6},{14,9},{13,10},{10,13},{9,14},{22,17},{21,... | collective-permute-start | bytes 307208 | tf_op jit(solution)/shard_map/ppermute | solution.py:672
  31.3 27.8 %collective-permute-start.15 = (f32[32,64,128]{2,1,0:T(8,128)S(1)}, f32[32,64,128]{2,1,0:T(8,128)}, u32[]{:S(2)}, u32[]{:S(2)}) collective-permute-start(f32[32,64,128]{2,1,0:T(8,128)S(1)} %get-tuple-element.101.w2), channel_id=1, source_target_pairs={{8,16},{16,24},{9,17},{17,25},{10,18},{18,26},{11,19},{19,27},{12,... | collective-permute-start | bytes 3145736 | tf_op jit(solution)/shard_map/ppermute | solution.py:748
  32.6 10.5 %collective-permute-start.5 = (f32[12,32,128]{2,1,0:T(8,128)}, f32[12,32,128]{2,1,0:T(8,128)}, u32[]{:S(2)}, u32[]{:S(2)}) collective-permute-start(f32[12,32,128]{2,1,0:T(8,128)} %get-tuple-element.67), channel_id=1, source_target_pairs={{4,0},{5,1},{6,2},{7,3},{0,4},{1,5},{2,6},{3,7},{12,8},{13,9},{14,... | collective-permute-start | bytes 589832 | tf_op jit(solution)/shard_map/ppermute | solution.py:672
  34.0 9.0 %collective-permute-start.7 = (f32[48,8,128]{2,1,0:T(8,128)}, f32[48,8,128]{2,1,0:T(8,128)}, u32[]{:S(2)}, u32[]{:S(2)}) collective-permute-start(f32[48,8,128]{2,1,0:T(8,128)} %get-tuple-element.69), channel_id=1, source_target_pairs={{1,0},{0,1},{3,2},{2,3},{5,4},{4,5},{7,6},{6,7},{9,8},{8,9},{11,10... | collective-permute-start | bytes 589832 | tf_op jit(solution)/shard_map/ppermute | solution.py:672
  34.7 8.4 %collective-permute-start.8 = (f32[48,8,128]{2,1,0:T(8,128)}, f32[48,8,128]{2,1,0:T(8,128)}, u32[]{:S(2)}, u32[]{:S(2)}) collective-permute-start(f32[48,8,128]{2,1,0:T(8,128)} %get-tuple-element.70), channel_id=1, source_target_pairs={{2,1},{1,2},{6,5},{5,6},{10,9},{9,10},{14,13},{13,14},{18,17},{17,... | collective-permute-start | bytes 589832 | tf_op jit(solution)/shard_map/ppermute | solution.py:672
  36.7 6.3 %collective-permute-start.6 = (f32[12,8,128]{2,1,0:T(8,128)S(1)}, f32[12,8,128]{2,1,0:T(8,128)S(1)}, u32[]{:S(2)}, u32[]{:S(2)}) collective-permute-start(f32[12,8,128]{2,1,0:T(8,128)S(1)} %get-tuple-element.68), channel_id=1, source_target_pairs={{6,1},{5,2},{2,5},{1,6},{14,9},{13,10},{10,13},{9,14},{22,17},{21,... | collective-permute-start | bytes 147464 | tf_op jit(solution)/shard_map/ppermute | solution.py:672
  43.8 1.2 %collective-permute-start.9 = (f32[12,8,128]{2,1,0:T(8,128)S(1)}, f32[12,8,128]{2,1,0:T(8,128)S(1)}, u32[]{:S(2)}, u32[]{:S(2)}) collective-permute-start(f32[12,8,128]{2,1,0:T(8,128)S(1)} %constant_dynamic-slice_fusion), channel_id=1, source_target_pairs={{1,0},{0,1},{3,2},{2,3},{5,4},{4,5},{7,6},{6,7},{9,8},{8,9},{11,10... | collective-permute-start | bytes 147464 | tf_op jit(solution)/shard_map/ppermute | solution.py:672
  47.4 2.7 %collective-permute-start.10 = (f32[16,32,128]{2,1,0:T(8,128)S(1)}, f32[16,32,128]{2,1,0:T(8,128)S(1)}, u32[]{:S(2)}, u32[]{:S(2)}) collective-permute-start(f32[16,32,128]{2,1,0:T(8,128)S(1)} %get-tuple-element.78), channel_id=1, source_target_pairs={{0,8},{1,9},{2,10},{3,11},{4,12},{5,13},{6,14},{7,15}} | collective-permute-start | bytes 786440 | tf_op jit(solution)/shard_map/ppermute | solution.py:809
  48.1 2.0 %collective-permute-start.11 = (f32[6,32,128]{2,1,0:T(8,128)S(1)}, f32[6,32,128]{2,1,0:T(8,128)S(1)}, u32[]{:S(2)}, u32[]{:S(2)}) collective-permute-start(f32[6,32,128]{2,1,0:T(8,128)S(1)} %get-tuple-element.79), channel_id=1, source_target_pairs={{4,8},{5,9},{6,10},{7,11},{0,12},{1,13},{2,14},{3,15}} | collective-permute-start | bytes 294920 | tf_op jit(solution)/shard_map/ppermute | solution.py:672
  48.8 1.4 %collective-permute-start.13 = (f32[16,8,128]{2,1,0:T(8,128)S(1)}, f32[16,8,128]{2,1,0:T(8,128)S(1)}, u32[]{:S(2)}, u32[]{:S(2)}) collective-permute-start(f32[16,8,128]{2,1,0:T(8,128)S(1)} %get-tuple-element.81), channel_id=1, source_target_pairs={{2,9},{1,10},{6,13},{5,14}} | collective-permute-start | bytes 196616 | tf_op jit(solution)/shard_map/ppermute | solution.py:672
  49.5 0.7 collective-permute-start.12
  50.2 19.1 %collective-permute-start.25 = (f32[32,64,128]{2,1,0:T(8,128)S(1)}, f32[32,64,128]{2,1,0:T(8,128)S(1)}, u32[]{:S(2)}, u32[]{:S(2)}) collective-permute-start(f32[32,64,128]{2,1,0:T(8,128)S(1)} %get-tuple-element.101.w2), channel_id=1, source_target_pairs={{0,8},{1,9},{2,10},{3,11},{4,12},{5,13},{6,14},{7,15}} | collective-permute-start | bytes 3145736 | tf_op jit(solution)/shard_map/ppermute | solution.py:825
  50.9 0.7 collective-permute-start.14
  59.7 2.9 %collective-permute-start.16 = (f32[16,32,128]{2,1,0:T(8,128)S(1)}, f32[16,32,128]{2,1,0:T(8,128)S(1)}, u32[]{:S(2)}, u32[]{:S(2)}) collective-permute-start(f32[16,32,128]{2,1,0:T(8,128)S(1)} %get-tuple-element.88), channel_id=1, source_target_pairs={{8,16},{9,17},{10,18},{11,19},{12,20},{13,21},{14,22},{15,23}} | collective-permute-start | bytes 786440 | tf_op jit(solution)/shard_map/ppermute | solution.py:809
  60.4 2.2 %collective-permute-start.17 = (f32[6,32,128]{2,1,0:T(8,128)S(1)}, f32[6,32,128]{2,1,0:T(8,128)S(1)}, u32[]{:S(2)}, u32[]{:S(2)}) collective-permute-start(f32[6,32,128]{2,1,0:T(8,128)S(1)} %get-tuple-element.89), channel_id=1, source_target_pairs={{12,16},{13,17},{14,18},{15,19},{8,20},{9,21},{10,22},{11,23}} | collective-permute-start | bytes 294920 | tf_op jit(solution)/shard_map/ppermute | solution.py:672
  61.1 1.5 %collective-permute-start.19 = (f32[16,8,128]{2,1,0:T(8,128)S(1)}, f32[16,8,128]{2,1,0:T(8,128)S(1)}, u32[]{:S(2)}, u32[]{:S(2)}) collective-permute-start(f32[16,8,128]{2,1,0:T(8,128)S(1)} %get-tuple-element.91), channel_id=1, source_target_pairs={{10,17},{9,18},{14,21},{13,22}} | collective-permute-start | bytes 196616 | tf_op jit(solution)/shard_map/ppermute | solution.py:672
  61.8 7.6 %copy-start.2 = (f32[1,3,32,64,128]{4,3,2,1,0:T(8,128)S(1)}, f32[1,3,32,64,128]{4,3,2,1,0:T(8,128)}, u32[]{:S(2)}) copy-start(f32[1,3,32,64,128]{4,3,2,1,0:T(8,128)} %param.4) | copy-start | bytes 9437188
  61.8 0.8 collective-permute-start.18
  62.6 0.8 collective-permute-start.20
  64.1 38.8 %collective-permute-start.21 = (f32[16,32,128]{2,1,0:T(8,128)S(1)}, f32[16,32,128]{2,1,0:T(8,128)S(1)}, u32[]{:S(2)}, u32[]{:S(2)}) collective-permute-start(f32[16,32,128]{2,1,0:T(8,128)S(1)} %get-tuple-element.97._), channel_id=1, source_target_pairs={{16,24},{17,25},{18,26},{19,27},{20,28},{21,29},{22,30},{23,31}} | collective-permute-start | bytes 786440 | tf_op jit(solution)/shard_map/ppermute | solution.py:809
  65.4 37.5 %collective-permute-start.22 = (f32[6,32,128]{2,1,0:T(8,128)S(1)}, f32[6,32,128]{2,1,0:T(8,128)S(1)}, u32[]{:S(2)}, u32[]{:S(2)}) collective-permute-start(f32[6,32,128]{2,1,0:T(8,128)S(1)} %get-tuple-element.98), channel_id=1, source_target_pairs={{20,24},{21,25},{22,26},{23,27},{16,28},{17,29},{18,30},{19,31}} | collective-permute-start | bytes 294920 | tf_op jit(solution)/shard_map/ppermute | solution.py:672
  66.7 36.2 %collective-permute-start.24 = (f32[16,8,128]{2,1,0:T(8,128)S(1)}, f32[16,8,128]{2,1,0:T(8,128)S(1)}, u32[]{:S(2)}, u32[]{:S(2)}) collective-permute-start(f32[16,8,128]{2,1,0:T(8,128)S(1)} %get-tuple-element.100), channel_id=1, source_target_pairs={{18,25},{17,26},{22,29},{21,30}} | collective-permute-start | bytes 196616 | tf_op jit(solution)/shard_map/ppermute | solution.py:672
  68.0 34.9 %collective-permute-start.23 = (f32[6,8,128]{2,1,0:T(8,128)S(1)}, f32[6,8,128]{2,1,0:T(8,128)S(1)}, u32[]{:S(2)}, u32[]{:S(2)}) collective-permute-start(f32[6,8,128]{2,1,0:T(8,128)S(1)} %get-tuple-element.99), channel_id=1, source_target_pairs={{22,25},{21,26},{18,29},{17,30}} | collective-permute-start | bytes 73736 | tf_op jit(solution)/shard_map/ppermute | solution.py:672
  103.0 3.2 %collective-permute-start.26 = (f32[22,8,128]{2,1,0:T(8,128)S(1)}, f32[22,8,128]{2,1,0:T(8,128)S(1)}, u32[]{:S(2)}, u32[]{:S(2)}) collective-permute-start(f32[22,8,128]{2,1,0:T(8,128)S(1)} %fusion), channel_id=1, source_target_pairs={{25,24},{24,25},{27,26},{26,27},{29,28},{28,29},{31,30},{30,31}} | collective-permute-start | bytes 270344 | tf_op jit(solution)/shard_map/ppermute | solution.py:833
